TPU v7x, 128 devices: a whole 4x4x4 slice. The times are simulated.
128 devices in a mesh: blk: 32 (over z, y, core), sub: 4 (over x).
Axes of the slice: x: 4, y: 4, z: 4, core: 2. Of those that a mesh axis runs over, the one named last changes fastest.
Arguments:
- gcm_state: float32 [6, 32, 64, 512], P(None, None, 'blk', 'sub'), may hold values from -6 to 6
- crm_state: bfloat16 [2, 32, 64, 32768], P(None, None, None, ('blk', 'sub')), may hold values from -6 to 6
- owner: int32 [64, 512], P('blk', 'sub'), may hold values from 0 to 127, as said below
- branch: int32 [64, 512], P('blk', 'sub'), may hold values 0 or 1
- diffusion: float32 [6, 32], replicated, may hold values from 0.03 to 0.24
Outputs:
- gcm_next: float32 [6, 32, 64, 512], P(None, None, 'blk', 'sub')
- crm_stats: float32 [2, 32, 64, 512], P(None, None, 'blk', 'sub')
Inputs may be any that keep to these rules, and one draw needn't show every extreme that they name: Every device sends exactly 2 of its columns to each device (itself included); every owner receives exactly 256 columns.
All inputs are finite; a program needn't handle non-finite values. No bound on the sum of `branch` on one device may be relied on, other than what follows from the above.
Results may differ from a plain program's by a relative error of at most 0.0003.
Values sent between devices are 32-bit elements; how exact they have to be, the bound alone decides.
No kernel may reach another device: no remote copies, remote signals or barrier semaphores. Data moves between devices by JAX's collectives and lax.ppermute only.
A program may use at most 64 MiB of HBM per device.

v0:
```python
import math

import jax
import jax.numpy as jnp
from jax import lax
from jax.experimental import pallas as pl
from jax.experimental.pallas import tpu as pltpu
from jax.sharding import PartitionSpec as P

SUBSTEPS = 4
LEV = 32
NXC = 64
LANES = 128
DEVICES = 128
COLS = 256
FIELDS = 6
SUB = 8
INNER = NXC // SUB
GCM_ROWS = FIELDS * LEV * 2
ALPHA = 0.3 * math.log2(math.e)
BETA = 1.5 * ALPHA
SHIFT = math.log2(0.5 * BETA)
MIB = 1 << 20


def pieces(x):
    first = x.astype(jnp.bfloat16)
    rest = x - first.astype(jnp.float32)
    second = rest.astype(jnp.bfloat16)
    third = (rest - second.astype(jnp.float32)).astype(jnp.bfloat16)
    return first, second, third


def select_dot(x, chosen, dims, x_first):
    total = None
    for part in pieces(x):
        pair = (part, chosen) if x_first else (chosen, part)
        term = lax.dot_general(*pair, (dims, ((), ())), preferred_element_type=jnp.float32)
        total = term if total is None else total + term
    return total


def prepare_kernel(
    gcm, above, below, left, right, owner, branch, diffusion, advanced, outgoing, routes
):
    number = diffusion[...]
    lane = lax.broadcasted_iota(jnp.int32, (FIELDS * LEV, LANES), 1)
    level = lax.broadcasted_iota(jnp.int32, (LEV, LANES), 0)

    def rows(ref, y):
        return ref[pl.ds(y, FIELDS * LEV, stride=2), :]

    own = [rows(gcm, 0), rows(gcm, 1)]
    vertical = [rows(above, 1) + own[1], own[0] + rows(below, 0)]
    values = []
    for y in range(2):
        before = pltpu.roll(jnp.where(lane == LANES - 1, rows(left, y), own[y]), 1, axis=1)
        after = pltpu.roll(jnp.where(lane == 0, rows(right, y), own[y]), LANES - 1, axis=1)
        around = vertical[y] + after + before
        state = own[y] + number * (around - 4.0 * own[y])
        advanced[pl.ds(2 * 2 * LEV + y, 4 * LEV, stride=2), :] = state[2 * LEV :]
        field = [state[f * LEV : (f + 1) * LEV] for f in range(FIELDS)]
        warm = ALPHA * (0.25 * field[0] + 0.2 * field[4])
        wet = BETA * (0.25 * field[1] + 0.2 * field[5])
        drift = 0.45 * jnp.tanh(field[2])
        tilt = jnp.tanh(field[3])
        rise = 0.15 * (tilt + pltpu.roll(tilt, LEV - 1, axis=0))
        rate = jnp.where(branch[y : y + 1, :] == 1, 0.6, 0.2)
        rise = jnp.where(level == LEV - 1, rate, rise)
        values.append(jnp.concatenate([warm, wet, drift, rise], axis=0))
    values = jnp.concatenate(values, axis=1)

    device = lax.broadcasted_iota(jnp.int32, (DEVICES, LANES), 0)
    target = jnp.concatenate(
        [(device == owner[y : y + 1, :]).astype(jnp.float32) for y in range(2)], axis=1
    )
    earlier = (
        lax.broadcasted_iota(jnp.int32, (COLS, COLS), 0)
        < lax.broadcasted_iota(jnp.int32, (COLS, COLS), 1)
    ).astype(jnp.bfloat16)
    count = jnp.dot(target.astype(jnp.bfloat16), earlier, preferred_element_type=jnp.float32)
    for slot in range(2):
        here = jnp.where(count < 0.5, 1.0 - slot, 0.0 + slot)
        route = (target * here).astype(jnp.bfloat16)
        routes[slot] = route
        outgoing[pl.ds(slot, DEVICES, stride=2), :] = select_dot(
            values, route, ((1,), (1,)), False
        )


def spread_kernel(crm, state, sums):
    levels = crm.shape[1]
    moist = pl.program_id(0)
    scale = jnp.where(moist == 1, BETA, ALPHA)
    shift = jnp.where(moist == 1, 0.0, SHIFT)

    def level(k, carry):
        for half in range(2):
            x = crm[0, k, :, half * LANES : (half + 1) * LANES].astype(jnp.float32)
            x = x * scale + shift
            total = None
            for part in range(SUB):
                block = x[part * INNER : (part + 1) * INNER]
                state[0, half, pl.ds(k * NXC + part, INNER, stride=SUB), :] = block
                total = block if total is None else total + block
            sums[0, half, pl.ds(pl.multiple_of(k * SUB, SUB), SUB), :] = total
        return carry

    lax.fori_loop(0, levels, level, 0, unroll=4)


def cloud_kernel(incoming, start, sums, outgoing, state, coef, mean, total, square):
    level = lax.broadcasted_iota(jnp.int32, (LEV, LANES), 0)
    top = level == LEV - 1
    rates = []

    def up(x):
        return pltpu.roll(x, LEV - 1, axis=0)

    def down(x):
        return pltpu.roll(x, 1, axis=0)

    def folded(ref, *lead):
        out = None
        for part in range(SUB):
            x = ref[(*lead, pl.ds(part, LEV, stride=SUB), slice(None))]
            out = x if out is None else out + x
        return out

    for half in range(2):
        values = jnp.transpose(incoming[half * LANES : (half + 1) * LANES, :])
        rise = values[3 * LEV :]
        rates.append(rise[LEV - 1 :])
        rise = jnp.where(top, 0.0, rise)
        base = SHIFT * (1.0 - rise + down(rise))
        coef[0, half] = values[:LEV] + SHIFT - 0.75 * base
        coef[1, half] = values[LEV : 2 * LEV]
        coef[2, half] = values[2 * LEV : 3 * LEV]
        coef[3, half] = rise
        coef[7, half] = jnp.broadcast_to(rates[half], (LEV, LANES))
        for f in range(2):
            mean[f, half] = folded(sums, f, half) * (1.0 / NXC)

    def relax():
        for half in range(2):
            rise = coef[3, half]
            for f in range(2):
                now = mean[f, half]
                flux = rise * jnp.where(rise > 0.0, now, up(now))
                now = now - flux + down(flux)
                add = coef[f, half] - 0.25 * now
                coef[4 + f, half] = add
                mean[f, half] = now + add
                if f == 0:
                    coef[6, half] = now + add

    def settle():
        for half in range(2):
            rain = folded(total, half) * (1.0 / NXC)
            mean[0, half] = mean[0, half] + rain
            mean[1, half] = mean[1, half] - rain
            mean[2, half] = mean[2, half] + rain

    def sweep(source, half, last):
        rate = jnp.broadcast_to(coef[7, half, 0:1, :], (SUB, LANES))

        def row(index, k):
            return jnp.broadcast_to(coef[index, half, k : k + 1, :], (SUB, LANES))

        def drifted(f, k, size, positive):
            cells = [
                source[f, half, k * NXC + j * SUB : k * NXC + (j + 1) * SUB, :]
                for j in range(INNER)
            ]
            before = [pltpu.roll(cells[-1], 1, axis=0)] + cells[:-1]
            after = cells[1:] + [pltpu.roll(cells[0], SUB - 1, axis=0)]
            return [
                c + size * (jnp.where(positive, b, a) - c)
                for c, b, a in zip(cells, before, after)
            ]

        def level_of(k):
            drift = row(2, k)
            size, positive = jnp.abs(drift), drift > 0.0
            return [drifted(f, k, size, positive) for f in range(2)]

        now = level_of(0)
        below = None
        for k in range(LEV):
            add = [row(4, k), row(5, k)]
            if k < LEV - 1:
                after = level_of(k + 1)
                rise = row(3, k)
                upward = rise > 0.0
                flux = [
                    [rise * jnp.where(upward, a, b) for a, b in zip(now[f], after[f])]
                    for f in range(2)
                ]
            rained = None
            spread = None
            if last:
                middle = row(6, k)
            for j in range(INNER):
                new = []
                for f in range(2):
                    x = now[f][j]
                    if k < LEV - 1:
                        x = x - flux[f][j]
                    if k > 0:
                        x = x + below[f][j]
                    new.append(x + add[f])
                temper, moisture = new
                rain = rate * jnp.maximum(moisture - jnp.exp2(temper), 0.0)
                temper = temper + rain
                rained = rain if rained is None else rained + rain
                if last:
                    away = temper - middle
                    spread = away * away if spread is None else spread + away * away
                else:
                    at = slice(k * NXC + j * SUB, k * NXC + (j + 1) * SUB)
                    state[0, half, at, :] = temper
                    state[1, half, at, :] = moisture - rain
            total[half, k * SUB : (k + 1) * SUB, :] = rained
            if last:
                square[half, k * SUB : (k + 1) * SUB, :] = spread
            if k < LEV - 1:
                below, now = flux, after

    def substep(source, last):
        relax()

        def half_of(half, carry):
            sweep(source, half, last)
            return carry

        lax.fori_loop(0, 2, half_of, 0)
        if not last:
            settle()

    for half in range(2):
        mean[2, half] = jnp.zeros((LEV, LANES), jnp.float32)
    substep(start, False)

    def middle_step(step, carry):
        substep(state, False)
        return carry

    lax.fori_loop(0, SUBSTEPS - 2, middle_step, 0)
    substep(state, True)
    settle()
    for half in range(2):
        warm, wet, rain = mean[0, half], mean[1, half], mean[2, half]
        gap = warm - coef[6, half]
        spread = folded(square, half) * (1.0 / NXC) - gap * gap
        result = [
            (warm - SHIFT) * (1.0 / ALPHA),
            wet * (1.0 / BETA),
            rain * (1.0 / BETA),
            spread * (1.0 / (ALPHA * ALPHA)),
        ]
        outgoing[half * LANES : (half + 1) * LANES, :] = jnp.transpose(
            jnp.concatenate(result, axis=0)
        )


def home_kernel(returned, routes, advanced, gcm_next, stats):
    del advanced
    home = None
    for slot in range(2):
        back = returned[pl.ds(slot, DEVICES, stride=2), :]
        term = select_dot(jnp.transpose(back), routes[slot], ((1,), (0,)), True)
        home = term if home is None else home + term
    for y in range(2):
        part = home[:, y * LANES : (y + 1) * LANES]
        gcm_next[pl.ds(y, 2 * LEV, stride=2), :] = part[: 2 * LEV]
        stats[pl.ds(y, 2 * LEV, stride=2), :] = part[2 * LEV :]


def whole(shape):
    return pl.BlockSpec(shape, lambda *_: (0,) * len(shape))


def f32(*shape):
    return jax.ShapeDtypeStruct(shape, jnp.float32)


def transfer(rows):
    moved = lax.all_to_all(
        rows.reshape(DEVICES, 2, LANES), ("blk", "sub"), split_axis=0, concat_axis=0, tiled=True
    )
    return moved.reshape(COLS, LANES)


def body(gcm_state, crm_state, owner, branch, diffusion):
    gcm = gcm_state.reshape(GCM_ROWS, LANES)
    n_blk, n_sub = lax.axis_size("blk"), lax.axis_size("sub")

    def ring(n, step):
        return [(i, (i + step) % n) for i in range(n)]

    left = lax.ppermute(gcm, "sub", ring(n_sub, 1))
    right = lax.ppermute(gcm, "sub", ring(n_sub, -1))
    above = lax.ppermute(gcm, "blk", ring(n_blk, 1))
    below = lax.ppermute(gcm, "blk", ring(n_blk, -1))
    number = jnp.broadcast_to(diffusion.reshape(FIELDS * LEV, 1), (FIELDS * LEV, LANES))
    advanced, outgoing, routes = pl.pallas_call(
        prepare_kernel,
        out_shape=(
            f32(GCM_ROWS, LANES),
            f32(COLS, LANES),
            jax.ShapeDtypeStruct((2, DEVICES, COLS), jnp.bfloat16),
        ),
        compiler_params=pltpu.CompilerParams(vmem_limit_bytes=32 * MIB),
        name="prepare",
    )(gcm, above, below, left, right, owner, branch, number)

    chunk = 8
    state, sums = pl.pallas_call(
        spread_kernel,
        grid=(2, LEV // chunk),
        in_specs=[pl.BlockSpec((1, chunk, NXC, COLS), lambda f, k: (f, k, 0, 0))],
        out_specs=(
            pl.BlockSpec((1, 2, chunk * NXC, LANES), lambda f, k: (f, 0, k, 0)),
            pl.BlockSpec((1, 2, chunk * SUB, LANES), lambda f, k: (f, 0, k, 0)),
        ),
        out_shape=(f32(2, 2, LEV * NXC, LANES), f32(2, 2, LEV * SUB, LANES)),
        compiler_params=pltpu.CompilerParams(vmem_limit_bytes=16 * MIB),
        cost_estimate=pl.CostEstimate(
            flops=4 * 2 * LEV * NXC * COLS, bytes_accessed=6 * 2 * LEV * NXC * COLS, transcendentals=0
        ),
        name="spread",
    )(crm_state)

    incoming = transfer(outgoing)
    profiles = pl.pallas_call(
        cloud_kernel,
        out_shape=f32(COLS, LANES),
        scratch_shapes=[
            pltpu.VMEM((2, 2, LEV * NXC, LANES), jnp.float32),
            pltpu.VMEM((8, 2, LEV, LANES), jnp.float32),
            pltpu.VMEM((3, 2, LEV, LANES), jnp.float32),
            pltpu.VMEM((2, LEV * SUB, LANES), jnp.float32),
            pltpu.VMEM((2, LEV * SUB, LANES), jnp.float32),
        ],
        compiler_params=pltpu.CompilerParams(vmem_limit_bytes=32 * MIB),
        name="cloud",
    )(incoming, state, sums)
    returned = transfer(profiles)

    gcm_next, stats = pl.pallas_call(
        home_kernel,
        grid=(1,),
        in_specs=[
            whole((COLS, LANES)),
            whole((2, DEVICES, COLS)),
            pl.BlockSpec(memory_space=pl.ANY),
        ],
        out_specs=(whole((4 * LEV, LANES)), whole((4 * LEV, LANES))),
        out_shape=(f32(GCM_ROWS, LANES), f32(4 * LEV, LANES)),
        input_output_aliases={2: 0},
        compiler_params=pltpu.CompilerParams(vmem_limit_bytes=32 * MIB),
        name="home",
    )(returned, routes, advanced)
    return gcm_next.reshape(gcm_state.shape), stats.reshape(2, LEV, 2, LANES)


def solution(mesh):
    grid = P(None, None, "blk", "sub")
    return jax.shard_map(
        body,
        mesh=mesh,
        in_specs=(grid, P(None, None, None, ("blk", "sub")), P("blk", "sub"), P("blk", "sub"), P()),
        out_specs=(grid, grid),
        check_vma=False,
    )
```

profile of v0, /device:TPU:1, one launch (start us, length us, event | category | flops | bytes accessed | tf_op | source)
XLA Modules:
  0.0 62.1 jit_solution(4972553891903023274)
XLA Ops:
  0.6 3.4 %collective-permute-start.3 = (f32[384,128]{1,0:T(8,128)}, f32[384,128]{1,0:T(8,128)S(1)}, u32[]{:S(2)}, u32[]{:S(2)}) collective-permute-start(f32[384,128]{1,0:T(8,128)} %bitcast.10), channel_id=1, source_target_pairs={{0,3},{1,0},{2,1},{3,2},{4,7},{5,4},{6,5},{7,6},{8,11},{9,8},{10,9... | collective-permute-start | bytes 589832 | tf_op jit(solution)/shard_map/ppermute | solution.py:302
  4.0 0.0 collective-permute-start.2
  4.0 1.0 %collective-permute-start.1 = (f32[384,128]{1,0:T(8,128)}, f32[384,128]{1,0:T(8,128)S(1)}, u32[]{:S(2)}, u32[]{:S(2)}) collective-permute-start(f32[384,128]{1,0:T(8,128)} %bitcast.12), channel_id=1, source_target_pairs={{0,124},{4,0},{8,4},{12,8},{16,12},{20,16},{24,20},{28,24},{32,28}... | collective-permute-start | bytes 589832 | tf_op jit(solution)/shard_map/ppermute | solution.py:304
  5.0 1.2 %collective-permute-start = (f32[384,128]{1,0:T(8,128)}, f32[384,128]{1,0:T(8,128)S(1)}, u32[]{:S(2)}, u32[]{:S(2)}) collective-permute-start(f32[384,128]{1,0:T(8,128)} %bitcast.13), channel_id=1, source_target_pairs={{0,4},{4,8},{8,12},{12,16},{16,20},{20,24},{24,28},{28,32},{32,36}... | collective-permute-start | bytes 589832 | tf_op jit(solution)/shard_map/ppermute | solution.py:303
  6.2 0.8 %broadcast_in_dim.7 = f32[192]{0:T(256)S(1)} reshape(f32[6,32]{1,0:T(8,128)} %param.9) | data formatting | bytes 1536 | tf_op jit(solution)/shard_map/broadcast_in_dim | solution.py:305
  6.9 1.0 %collective-permute-done.3.right = f32[384,128]{1,0:T(8,128)S(1)} collective-permute-done((f32[384,128]{1,0:T(8,128)}, f32[384,128]{1,0:T(8,128)S(1)}, u32[]{:S(2)}, u32[]{:S(2)}) %collective-permute-start.3) | collective-permute-done | bytes 196640 | tf_op jit(solution)/shard_map/ppermute | solution.py:302
  7.9 3.0 %collective-permute-done.2.left = f32[384,128]{1,0:T(8,128)S(1)} collective-permute-done((f32[384,128]{1,0:T(8,128)}, f32[384,128]{1,0:T(8,128)S(1)}, u32[]{:S(2)}, u32[]{:S(2)}) %collective-permute-start.2) | collective-permute-done | bytes 196640 | tf_op jit(solution)/shard_map/ppermute | solution.py:301
  10.9 0.0 collective-permute-done.1.below
  10.9 0.9 %collective-permute-done.above = f32[384,128]{1,0:T(8,128)S(1)} collective-permute-done((f32[384,128]{1,0:T(8,128)}, f32[384,128]{1,0:T(8,128)S(1)}, u32[]{:S(2)}, u32[]{:S(2)}) %collective-permute-start) | collective-permute-done | bytes 196640 | tf_op jit(solution)/shard_map/ppermute | solution.py:303
  11.8 0.1 broadcast_in_dim.8.diffusion
  11.8 0.0 copy-start.3
  11.9 0.9 %copy-done.3 = f32[6,32,2,128]{3,2,1,0:T(2,128)S(1)} copy-done((f32[6,32,2,128]{3,2,1,0:T(2,128)S(1)}, f32[6,32,2,128]{3,2,1,0:T(2,128)}, u32[]{:S(2)}) %copy-start.3) | copy-done | bytes 196632
  12.8 0.0 copy-start.4
  12.8 0.7 %copy-done.4 = s32[2,128]{1,0:T(2,128)S(1)} copy-done((s32[2,128]{1,0:T(2,128)S(1)}, s32[2,128]{1,0:T(2,128)}, u32[]{:S(2)}) %copy-start.4) | copy-done | bytes 1048
  13.5 0.0 copy-start.5
  13.5 0.7 %copy-done.5 = s32[2,128]{1,0:T(2,128)S(1)} copy-done((s32[2,128]{1,0:T(2,128)S(1)}, s32[2,128]{1,0:T(2,128)}, u32[]{:S(2)}) %copy-start.5) | copy-done | bytes 1048
  14.1 1.1 %prepare.1 = (f32[384,128]{1,0:T(8,128)}, f32[256,128]{1,0:T(8,128)}, bf16[2,128,256]{2,1,0:T(8,128)(2,1)S(1)}) custom-call(f32[384,128]{1,0:T(8,128)S(1)} %bitcast.14, f32[384,128]{1,0:T(8,128)S(1)} %collective-permute-done.above, f32[384,128]{1,0:T(8,128)S(1)} %collective-permute-done.1.below, f32[384,128]{1,0:T(8,128)S(1)} %collective-permute-done.2.left, ...), custom_call_target="tpu_custom_call" | custom-call | tf_op jit(solution)/shard_map/prepare/pallas_call | solution.py:306
  15.3 11.3 %all-to-all-start = ((f32[128,2,128]{2,1,0:T(2,128)}), f32[128,2,128]{2,1,0:T(2,128)S(1)}, u32[]{:S(2)}, u32[]{:S(2)}) async-start(f32[128,2,128]{2,1,0:T(2,128)} %bitcast.1), calls=%async_computation | async-start | bytes 262144 | tf_op jit(solution)/shard_map/all_to_all | solution.py:288
  26.6 0.0 copy-start.2
  26.6 1.6 %copy-done.2 = bf16[2,32,64,256]{3,2,1,0:T(8,128)(2,1)S(1)} copy-done((bf16[2,32,64,256]{3,2,1,0:T(8,128)(2,1)S(1)}, bf16[2,32,64,256]{3,2,1,0:T(8,128)(2,1)}, u32[]{:S(2)}) %copy-start.2) | copy-done | bytes 2097176
  28.1 1.2 %spread.1 = (f32[2,2,2048,128]{3,2,1,0:T(8,128)S(1)}, f32[2,2,256,128]{3,2,1,0:T(8,128)S(1)}) custom-call(bf16[2,32,64,256]{3,2,1,0:T(8,128)(2,1)S(1)} %copy-done.2), custom_call_target="tpu_custom_call" | custom-call | flops 4194304 | bytes 6291456 | tf_op jit(solution)/shard_map/spread/pallas_call | solution.py:318
  29.3 0.0 copy-start
  29.4 1.9 %copy-done = f32[2,2,2048,128]{3,2,1,0:T(8,128)} copy-done((f32[2,2,2048,128]{3,2,1,0:T(8,128)}, f32[2,2,2048,128]{3,2,1,0:T(8,128)S(1)}, u32[]{:S(2)}) %copy-start) | copy-done | bytes 4194328
  31.3 5.1 %all-to-all-done = f32[128,2,128]{2,1,0:T(2,128)S(1)} async-done(((f32[128,2,128]{2,1,0:T(2,128)}), f32[128,2,128]{2,1,0:T(2,128)S(1)}, u32[]{:S(2)}, u32[]{:S(2)}) %all-to-all-start) | async-done | bytes 131104 | tf_op jit(solution)/shard_map/all_to_all | solution.py:288
  36.4 0.0 copy-start.1
  36.4 2.2 %copy-done.1 = f32[2,2,2048,128]{3,2,1,0:T(8,128)S(1)} copy-done((f32[2,2,2048,128]{3,2,1,0:T(8,128)S(1)}, f32[2,2,2048,128]{3,2,1,0:T(8,128)}, u32[]{:S(2)}) %copy-start.1) | copy-done | bytes 4194328
  38.6 7.8 %cloud.1 = f32[256,128]{1,0:T(8,128)S(1)} custom-call(f32[256,128]{1,0:T(8,128)S(1)} %bitcast.7, f32[2,2,2048,128]{3,2,1,0:T(8,128)S(1)} %copy-done.1, f32[2,2,256,128]{3,2,1,0:T(8,128)S(1)} %get-tuple-element.11.sums), custom_call_target="tpu_custom_call" | custom-call | tf_op jit(solution)/shard_map/cloud/pallas_call | solution.py:335
  46.4 14.7 %all_to_all.10 = f32[128,2,128]{2,1,0:T(2,128)S(1)} all-to-all(f32[128,2,128]{2,1,0:T(2,128)S(1)} %bitcast.9), channel_id=1, replica_groups=mesh['blk'=32,'sub'=4] {'blk','sub'}, dimensions={0} | all-to-all | bytes 262144 | tf_op jit(solution)/shard_map/all_to_all | solution.py:288
  61.1 0.9 %home.1 = (f32[384,128]{1,0:T(8,128)}, f32[128,128]{1,0:T(8,128)}) custom-call(f32[256,128]{1,0:T(8,128)S(1)} %bitcast.8, bf16[2,128,256]{2,1,0:T(8,128)(2,1)S(1)} %get-tuple-element.12.routes, f32[384,128]{1,0:T(8,128)} %get-tuple-element.13.advanced), custom_call_target="tpu_custom_call", output_to_operand_aliasing={{0}: (2, {})} | custom-call | tf_op jit(solution)/shard_map/home/pallas_call | solution.py:350
Async XLA Ops:
  0.6 7.3 %collective-permute-start.3 = (f32[384,128]{1,0:T(8,128)}, f32[384,128]{1,0:T(8,128)S(1)}, u32[]{:S(2)}, u32[]{:S(2)}) collective-permute-start(f32[384,128]{1,0:T(8,128)} %bitcast.10), channel_id=1, source_target_pairs={{0,3},{1,0},{2,1},{3,2},{4,7},{5,4},{6,5},{7,6},{8,11},{9,8},{10,9... | collective-permute-start | bytes 589832 | tf_op jit(solution)/shard_map/ppermute | solution.py:302
  4.0 6.9 %collective-permute-start.2 = (f32[384,128]{1,0:T(8,128)}, f32[384,128]{1,0:T(8,128)S(1)}, u32[]{:S(2)}, u32[]{:S(2)}) collective-permute-start(f32[384,128]{1,0:T(8,128)} %bitcast.11), channel_id=1, source_target_pairs={{0,1},{1,2},{2,3},{3,0},{4,5},{5,6},{6,7},{7,4},{8,9},{9,10},{10,1... | collective-permute-start | bytes 589832 | tf_op jit(solution)/shard_map/ppermute | solution.py:301
  4.0 6.9 %collective-permute-start.1 = (f32[384,128]{1,0:T(8,128)}, f32[384,128]{1,0:T(8,128)S(1)}, u32[]{:S(2)}, u32[]{:S(2)}) collective-permute-start(f32[384,128]{1,0:T(8,128)} %bitcast.12), channel_id=1, source_target_pairs={{0,124},{4,0},{8,4},{12,8},{16,12},{20,16},{24,20},{28,24},{32,28}... | collective-permute-start | bytes 589832 | tf_op jit(solution)/shard_map/ppermute | solution.py:304
  5.0 6.8 %collective-permute-start = (f32[384,128]{1,0:T(8,128)}, f32[384,128]{1,0:T(8,128)S(1)}, u32[]{:S(2)}, u32[]{:S(2)}) collective-permute-start(f32[384,128]{1,0:T(8,128)} %bitcast.13), channel_id=1, source_target_pairs={{0,4},{4,8},{8,12},{12,16},{16,20},{20,24},{24,28},{28,32},{32,36}... | collective-permute-start | bytes 589832 | tf_op jit(solution)/shard_map/ppermute | solution.py:303
  11.8 0.9 %copy-start.3 = (f32[6,32,2,128]{3,2,1,0:T(2,128)S(1)}, f32[6,32,2,128]{3,2,1,0:T(2,128)}, u32[]{:S(2)}) copy-start(f32[6,32,2,128]{3,2,1,0:T(2,128)} %param.5) | copy-start | bytes 589828
  12.8 0.7 %copy-start.4 = (s32[2,128]{1,0:T(2,128)S(1)}, s32[2,128]{1,0:T(2,128)}, u32[]{:S(2)}) copy-start(s32[2,128]{1,0:T(2,128)} %owner.1) | copy-start | bytes 3076
  13.5 0.7 %copy-start.5 = (s32[2,128]{1,0:T(2,128)S(1)}, s32[2,128]{1,0:T(2,128)}, u32[]{:S(2)}) copy-start(s32[2,128]{1,0:T(2,128)} %branch.1) | copy-start | bytes 3076
  15.3 21.2 %all-to-all-start = ((f32[128,2,128]{2,1,0:T(2,128)}), f32[128,2,128]{2,1,0:T(2,128)S(1)}, u32[]{:S(2)}, u32[]{:S(2)}) async-start(f32[128,2,128]{2,1,0:T(2,128)} %bitcast.1), calls=%async_computation | async-start | bytes 262144 | tf_op jit(solution)/shard_map/all_to_all | solution.py:288
  26.6 1.6 %copy-start.2 = (bf16[2,32,64,256]{3,2,1,0:T(8,128)(2,1)S(1)}, bf16[2,32,64,256]{3,2,1,0:T(8,128)(2,1)}, u32[]{:S(2)}) copy-start(bf16[2,32,64,256]{3,2,1,0:T(8,128)(2,1)} %crm.1) | copy-start | bytes 6291460
  29.3 1.9 %copy-start = (f32[2,2,2048,128]{3,2,1,0:T(8,128)}, f32[2,2,2048,128]{3,2,1,0:T(8,128)S(1)}, u32[]{:S(2)}) copy-start(f32[2,2,2048,128]{3,2,1,0:T(8,128)S(1)} %get-tuple-element.10.start) | copy-start | bytes 12582916
  36.4 2.2 %copy-start.1 = (f32[2,2,2048,128]{3,2,1,0:T(8,128)S(1)}, f32[2,2,2048,128]{3,2,1,0:T(8,128)}, u32[]{:S(2)}) copy-start(f32[2,2,2048,128]{3,2,1,0:T(8,128)} %copy-done) | copy-start | bytes 12582916
where the time goes:
time: 62.4 us; the launch traced here: 62.1 us
  starting transfers between devices  16.8 us (27%)
  blocking collectives  14.7 us (24%)
  Pallas kernels  11.1 us (18%)
  waiting for transfers between devices  9.96 us (16%)
  local copies, waits for them, and re-layouts  8.84 us (14%)
  between operations  0.69 us (1%)
    all_to_all x1, blocking collectives, transfer(): lax.all_to_all(rows.reshape(DEVICES, 2, LANES), ('blk', 'sub'), split_axi...  14.7 us
    all_to_all x1, starting transfers between devices, transfer(): lax.all_to_all(rows.reshape(DEVICES, 2, LANES), ('blk', 'sub'), split_axi...  11.3 us
    unnamed x12, local copies, waits for them, and re-layouts  8 us
    pallas_call x1, Pallas kernels, body(): pl.pallas_call(cloud_kernel, out_shape=f32(COLS, LANES), scratch_shapes=[...  7.81 us
    all_to_all x1, waiting for transfers between devices, transfer(): lax.all_to_all(rows.reshape(DEVICES, 2, LANES), ('blk', 'sub'), split_axi...  5.12 us
    ppermute x1, starting transfers between devices, body(): right = lax.ppermute(gcm, 'sub', ring(n_sub, -1))  3.38 us
    ppermute x1, waiting for transfers between devices, body(): left = lax.ppermute(gcm, 'sub', ring(n_sub, 1))  2.99 us
  transfers between devices with their start and end apart: 5, of which 4 were waited for; matrix products, arithmetic and copies ran while one was open for 1% of the time, Pallas kernels for 2%

commit v1 on v0

--- a/solution.py
+++ b/solution.py
@@ -17,6 +17,7 @@
 SUB = 8
 INNER = NXC // SUB
 GCM_ROWS = FIELDS * LEV * 2
+CRM_CHUNK = 8
 ALPHA = 0.3 * math.log2(math.e)
 BETA = 1.5 * ALPHA
 SHIFT = math.log2(0.5 * BETA)
@@ -40,36 +41,48 @@
     return total
 
 
-def prepare_kernel(
-    gcm, above, below, left, right, owner, branch, diffusion, advanced, outgoing, routes
+def rows_of(ref, y):
+    return ref[pl.ds(y, FIELDS * LEV, stride=2), :]
+
+
+def edge_kernel(gcm_hbm, first, last, gcm, arrival):
+    copy = pltpu.make_async_copy(gcm_hbm, gcm, arrival)
+    copy.start()
+    first[...] = jnp.zeros_like(first)
+    last[...] = jnp.zeros_like(last)
+    copy.wait()
+    rows = jnp.concatenate([rows_of(gcm, 0), rows_of(gcm, 1)], axis=0)
+    for part in range(GCM_ROWS // LANES):
+        turned = jnp.transpose(rows[part * LANES : (part + 1) * LANES])
+        first[part : part + 1, :] = turned[:1]
+        last[part : part + 1, :] = turned[LANES - 1 :]
+
+
+def early_kernel(
+    gcm_hbm, crm_hbm, owner_hbm, branch_hbm, diffusion_hbm,
+    state, sums, partial, number, routes, rates,
+    gcm, crm, owner, branch, diffusion, arrival, crm_arrival,
 ):
-    number = diffusion[...]
-    lane = lax.broadcasted_iota(jnp.int32, (FIELDS * LEV, LANES), 1)
-    level = lax.broadcasted_iota(jnp.int32, (LEV, LANES), 0)
-
-    def rows(ref, y):
-        return ref[pl.ds(y, FIELDS * LEV, stride=2), :]
-
-    own = [rows(gcm, 0), rows(gcm, 1)]
-    vertical = [rows(above, 1) + own[1], own[0] + rows(below, 0)]
-    values = []
-    for y in range(2):
-        before = pltpu.roll(jnp.where(lane == LANES - 1, rows(left, y), own[y]), 1, axis=1)
-        after = pltpu.roll(jnp.where(lane == 0, rows(right, y), own[y]), LANES - 1, axis=1)
-        around = vertical[y] + after + before
-        state = own[y] + number * (around - 4.0 * own[y])
-        advanced[pl.ds(2 * 2 * LEV + y, 4 * LEV, stride=2), :] = state[2 * LEV :]
-        field = [state[f * LEV : (f + 1) * LEV] for f in range(FIELDS)]
-        warm = ALPHA * (0.25 * field[0] + 0.2 * field[4])
-        wet = BETA * (0.25 * field[1] + 0.2 * field[5])
-        drift = 0.45 * jnp.tanh(field[2])
-        tilt = jnp.tanh(field[3])
-        rise = 0.15 * (tilt + pltpu.roll(tilt, LEV - 1, axis=0))
-        rate = jnp.where(branch[y : y + 1, :] == 1, 0.6, 0.2)
-        rise = jnp.where(level == LEV - 1, rate, rise)
-        values.append(jnp.concatenate([warm, wet, drift, rise], axis=0))
-    values = jnp.concatenate(values, axis=1)
-
+    loads = [
+        pltpu.make_async_copy(source, target, arrival.at[n])
+        for n, (source, target) in enumerate(
+            [(owner_hbm, owner), (branch_hbm, branch), (diffusion_hbm, diffusion), (gcm_hbm, gcm)]
+        )
+    ]
+    crm_loads = [
+        pltpu.make_async_copy(
+            crm_hbm.at[f, pl.ds(part * CRM_CHUNK, CRM_CHUNK)],
+            crm.at[f, pl.ds(part * CRM_CHUNK, CRM_CHUNK)],
+            crm_arrival.at[f, part],
+        )
+        for f in range(2)
+        for part in range(LEV // CRM_CHUNK)
+    ]
+    for copy in loads + crm_loads:
+        copy.start()
+
+    for copy in loads[:3]:
+        copy.wait()
     device = lax.broadcasted_iota(jnp.int32, (DEVICES, LANES), 0)
     target = jnp.concatenate(
         [(device == owner[y : y + 1, :]).astype(jnp.float32) for y in range(2)], axis=1
@@ -81,32 +94,70 @@
     count = jnp.dot(target.astype(jnp.bfloat16), earlier, preferred_element_type=jnp.float32)
     for slot in range(2):
         here = jnp.where(count < 0.5, 1.0 - slot, 0.0 + slot)
-        route = (target * here).astype(jnp.bfloat16)
-        routes[slot] = route
+        routes[slot] = (target * here).astype(jnp.bfloat16)
+    rates[...] = jnp.where(branch[...] == 1, 0.6, 0.2)
+    for f in range(FIELDS):
+        spread = jnp.broadcast_to(diffusion[f : f + 1, :], (LANES, LEV))
+        number[f * LEV : (f + 1) * LEV, :] = jnp.transpose(spread)
+
+    loads[3].wait()
+    lane = lax.broadcasted_iota(jnp.int32, (FIELDS * LEV, LANES), 1)
+    own = [rows_of(gcm, 0), rows_of(gcm, 1)]
+    for y in range(2):
+        before = jnp.where(lane == 0, 0.0, pltpu.roll(own[y], 1, axis=1))
+        after = jnp.where(lane == LANES - 1, 0.0, pltpu.roll(own[y], LANES - 1, axis=1))
+        around = own[1 - y] + after + before
+        partial[y] = own[y] + number[...] * (around - 4.0 * own[y])
+
+    for f, (scale, shift) in enumerate([(ALPHA, SHIFT), (BETA, 0.0)]):
+        for part in range(LEV // CRM_CHUNK):
+            crm_loads[f * (LEV // CRM_CHUNK) + part].wait()
+
+            def level(n, carry):
+                k = part * CRM_CHUNK + n
+                for half in range(2):
+                    x = crm[f, k, :, half * LANES : (half + 1) * LANES].astype(jnp.float32)
+                    x = x * scale + shift
+                    total = None
+                    for row in range(SUB):
+                        block = x[row * INNER : (row + 1) * INNER]
+                        state[f, half, pl.ds(k * NXC + row, INNER, stride=SUB), :] = block
+                        total = block if total is None else total + block
+                    sums[f, half, pl.ds(pl.multiple_of(k * SUB, SUB), SUB), :] = total
+                return carry
+
+            lax.fori_loop(0, CRM_CHUNK, level, 0, unroll=4)
+
+
+def prepare_kernel(partial, number, above, below, left, right, routes, rates, advanced, outgoing):
+    lane = lax.broadcasted_iota(jnp.int32, (FIELDS * LEV, LANES), 1)
+    level = lax.broadcasted_iota(jnp.int32, (LEV, LANES), 0)
+
+    def columns(ref):
+        turned = jnp.transpose(ref[...])
+        column = jnp.concatenate([turned[:, n : n + 1] for n in range(GCM_ROWS // LANES)], axis=0)
+        return column[: FIELDS * LEV], column[FIELDS * LEV :]
+
+    vertical = [rows_of(above, 1), rows_of(below, 0)]
+    west, east = columns(left), columns(right)
+    values = []
+    for y in range(2):
+        side = jnp.where(lane == 0, west[y], jnp.where(lane == LANES - 1, east[y], 0.0))
+        state = partial[y] + number[...] * (vertical[y] + side)
+        advanced[pl.ds(2 * 2 * LEV + y, 4 * LEV, stride=2), :] = state[2 * LEV :]
+        field = [state[f * LEV : (f + 1) * LEV] for f in range(FIELDS)]
+        warm = ALPHA * (0.25 * field[0] + 0.2 * field[4])
+        wet = BETA * (0.25 * field[1] + 0.2 * field[5])
+        drift = 0.45 * jnp.tanh(field[2])
+        tilt = jnp.tanh(field[3])
+        rise = 0.15 * (tilt + pltpu.roll(tilt, LEV - 1, axis=0))
+        rise = jnp.where(level == LEV - 1, rates[y : y + 1, :], rise)
+        values.append(jnp.concatenate([warm, wet, drift, rise], axis=0))
+    values = jnp.concatenate(values, axis=1)
+    for slot in range(2):
         outgoing[pl.ds(slot, DEVICES, stride=2), :] = select_dot(
-            values, route, ((1,), (1,)), False
+            values, routes[slot], ((1,), (1,)), False
         )
-
-
-def spread_kernel(crm, state, sums):
-    levels = crm.shape[1]
-    moist = pl.program_id(0)
-    scale = jnp.where(moist == 1, BETA, ALPHA)
-    shift = jnp.where(moist == 1, 0.0, SHIFT)
-
-    def level(k, carry):
-        for half in range(2):
-            x = crm[0, k, :, half * LANES : (half + 1) * LANES].astype(jnp.float32)
-            x = x * scale + shift
-            total = None
-            for part in range(SUB):
-                block = x[part * INNER : (part + 1) * INNER]
-                state[0, half, pl.ds(k * NXC + part, INNER, stride=SUB), :] = block
-                total = block if total is None else total + block
-            sums[0, half, pl.ds(pl.multiple_of(k * SUB, SUB), SUB), :] = total
-        return carry
-
-    lax.fori_loop(0, levels, level, 0, unroll=4)
 
 
 def cloud_kernel(incoming, start, sums, outgoing, state, coef, mean, total, square):
@@ -298,38 +349,50 @@
     def ring(n, step):
         return [(i, (i + step) % n) for i in range(n)]
 
-    left = lax.ppermute(gcm, "sub", ring(n_sub, 1))
-    right = lax.ppermute(gcm, "sub", ring(n_sub, -1))
+    below = lax.ppermute(gcm, "blk", ring(n_blk, -1))
     above = lax.ppermute(gcm, "blk", ring(n_blk, 1))
-    below = lax.ppermute(gcm, "blk", ring(n_blk, -1))
-    number = jnp.broadcast_to(diffusion.reshape(FIELDS * LEV, 1), (FIELDS * LEV, LANES))
-    advanced, outgoing, routes = pl.pallas_call(
+    hbm = pl.BlockSpec(memory_space=pltpu.HBM)
+    first, last = pl.pallas_call(
+        edge_kernel,
+        in_specs=[hbm],
+        out_shape=(f32(SUB, LANES), f32(SUB, LANES)),
+        scratch_shapes=[pltpu.VMEM((GCM_ROWS, LANES), jnp.float32), pltpu.SemaphoreType.DMA(())],
+        compiler_params=pltpu.CompilerParams(vmem_limit_bytes=4 * MIB),
+        name="edges",
+    )(gcm)
+    right = lax.ppermute(first, "sub", ring(n_sub, -1))
+    left = lax.ppermute(last, "sub", ring(n_sub, 1))
+    cells = 2 * LEV * NXC * COLS
+    state, sums, partial, number, routes, rates = pl.pallas_call(
+        early_kernel,
+        in_specs=[hbm] * 5,
+        out_shape=(
+            f32(2, 2, LEV * NXC, LANES),
+            f32(2, 2, LEV * SUB, LANES),
+            f32(2, FIELDS * LEV, LANES),
+            f32(FIELDS * LEV, LANES),
+            jax.ShapeDtypeStruct((2, DEVICES, COLS), jnp.bfloat16),
+            f32(2, LANES),
+        ),
+        scratch_shapes=[
+            pltpu.VMEM((GCM_ROWS, LANES), jnp.float32),
+            pltpu.VMEM((2, LEV, NXC, COLS), jnp.bfloat16),
+            pltpu.VMEM((2, LANES), jnp.int32),
+            pltpu.VMEM((2, LANES), jnp.int32),
+            pltpu.VMEM((FIELDS, LEV), jnp.float32),
+            pltpu.SemaphoreType.DMA((4,)),
+            pltpu.SemaphoreType.DMA((2, LEV // CRM_CHUNK)),
+        ],
+        compiler_params=pltpu.CompilerParams(vmem_limit_bytes=16 * MIB),
+        cost_estimate=pl.CostEstimate(flops=4 * cells, bytes_accessed=6 * cells, transcendentals=0),
+        name="early",
+    )(gcm, crm_state, owner, branch, diffusion)
+    advanced, outgoing = pl.pallas_call(
         prepare_kernel,
-        out_shape=(
-            f32(GCM_ROWS, LANES),
-            f32(COLS, LANES),
-            jax.ShapeDtypeStruct((2, DEVICES, COLS), jnp.bfloat16),
-        ),
-        compiler_params=pltpu.CompilerParams(vmem_limit_bytes=32 * MIB),
+        out_shape=(f32(GCM_ROWS, LANES), f32(COLS, LANES)),
+        compiler_params=pltpu.CompilerParams(vmem_limit_bytes=8 * MIB),
         name="prepare",
-    )(gcm, above, below, left, right, owner, branch, number)
-
-    chunk = 8
-    state, sums = pl.pallas_call(
-        spread_kernel,
-        grid=(2, LEV // chunk),
-        in_specs=[pl.BlockSpec((1, chunk, NXC, COLS), lambda f, k: (f, k, 0, 0))],
-        out_specs=(
-            pl.BlockSpec((1, 2, chunk * NXC, LANES), lambda f, k: (f, 0, k, 0)),
-            pl.BlockSpec((1, 2, chunk * SUB, LANES), lambda f, k: (f, 0, k, 0)),
-        ),
-        out_shape=(f32(2, 2, LEV * NXC, LANES), f32(2, 2, LEV * SUB, LANES)),
-        compiler_params=pltpu.CompilerParams(vmem_limit_bytes=16 * MIB),
-        cost_estimate=pl.CostEstimate(
-            flops=4 * 2 * LEV * NXC * COLS, bytes_accessed=6 * 2 * LEV * NXC * COLS, transcendentals=0
-        ),
-        name="spread",
-    )(crm_state)
+    )(partial, number, above, below, left, right, routes, rates)
 
     incoming = transfer(outgoing)
     profiles = pl.pallas_call(
@@ -342,7 +405,7 @@
             pltpu.VMEM((2, LEV * SUB, LANES), jnp.float32),
             pltpu.VMEM((2, LEV * SUB, LANES), jnp.float32),
         ],
-        compiler_params=pltpu.CompilerParams(vmem_limit_bytes=32 * MIB),
+        compiler_params=pltpu.CompilerParams(vmem_limit_bytes=12 * MIB),
         name="cloud",
     )(incoming, state, sums)
     returned = transfer(profiles)
@@ -358,7 +421,7 @@
         out_specs=(whole((4 * LEV, LANES)), whole((4 * LEV, LANES))),
         out_shape=(f32(GCM_ROWS, LANES), f32(4 * LEV, LANES)),
         input_output_aliases={2: 0},
-        compiler_params=pltpu.CompilerParams(vmem_limit_bytes=32 * MIB),
+        compiler_params=pltpu.CompilerParams(vmem_limit_bytes=8 * MIB),
         name="home",
     )(returned, routes, advanced)
     return gcm_next.reshape(gcm_state.shape), stats.reshape(2, LEV, 2, LANES)

time: 62.4 us -> 60.2 us (0.965)
  blocking collectives: 14.7 us -> 35.9 us
  starting transfers between devices: 16.8 us -> 5.58 us
  waiting for transfers between devices: 9.96 us -> 0.01 us
  local copies, waits for them, and re-layouts: 8.84 us -> 5.52 us
  Pallas kernels: 11.1 us -> 12.1 us
    all_to_all x1 -> x2, blocking collectives: 14.7 us -> 35.9 us  [transfer(): lax.all_to_all(rows.reshape(DEVICES, 2, LANES), ('blk', 'sub'), split_axi...]
    all_to_all x1 -> x0, starting transfers between devices: 11.3 us -> none  [transfer(): lax.all_to_all(rows.reshape(DEVICES, 2, LANES), ('blk', 'sub'), split_axi...]
    all_to_all x1 -> x0, waiting for transfers between devices: 5.12 us -> none  [transfer(): lax.all_to_all(rows.reshape(DEVICES, 2, LANES), ('blk', 'sub'), split_axi...]
    ppermute x2, waiting for transfers between devices: 3.96 us -> 0.01 us  [the longest x1 0.01 us: body(): left = lax.ppermute(last, 'sub', ring(n_sub, 1))]
    unnamed x12, local copies, waits for them, and re-layouts: 8 us -> 5.52 us
    pallas_call x1 -> x2, Pallas kernels: 1.19 us -> 2.18 us  [the longest x1 1.81 us: body(): pl.pallas_call(early_kernel, in_specs=[hbm] * 5, out_shape=(f32(2, 2, LEV...]
    ppermute x1, waiting for transfers between devices: 0.87 us -> 0.01 us  [body(): above = lax.ppermute(gcm, 'blk', ring(n_blk, 1))]
    broadcast_in_dim x2 -> x0, local copies, waits for them, and re-layouts: 0.84 us -> none  [body(): jnp.broadcast_to(diffusion.reshape(FIELDS * LEV, 1), (FIELDS * LEV, LANES))]
  transfers between devices with their start and end apart: 5 -> 4, of which waited for: 4 -> 0; matrix products, arithmetic and copies ran while one was open for 1% -> 0% of each run, Pallas kernels for 2% -> 4%
where the time goes in v1:
time: 60.2 us; the launch traced here: 59.9 us
  blocking collectives  35.9 us (60%)
  Pallas kernels  12.1 us (20%)
  starting transfers between devices  5.58 us (9%)
  local copies, waits for them, and re-layouts  5.52 us (9%)
  between operations  0.69 us (1%)
    all_to_all x2, blocking collectives, transfer(): lax.all_to_all(rows.reshape(DEVICES, 2, LANES), ('blk', 'sub'), split_axi...  35.9 us
    pallas_call x1, Pallas kernels, body(): pl.pallas_call(cloud_kernel, out_shape=f32(COLS, LANES), scratch_shapes=[...  7.84 us
    unnamed x12, local copies, waits for them, and re-layouts  5.52 us
    pallas_call x1, Pallas kernels, body(): pl.pallas_call(early_kernel, in_specs=[hbm] * 5, out_shape=(f32(2, 2, LEV...  1.81 us
    ppermute x1, starting transfers between devices, body(): below = lax.ppermute(gcm, 'blk', ring(n_blk, -1))  1.49 us
    ppermute x1, starting transfers between devices, body(): right = lax.ppermute(first, 'sub', ring(n_sub, -1))  1.47 us
    ppermute x1, starting transfers between devices, body(): above = lax.ppermute(gcm, 'blk', ring(n_blk, 1))  1.35 us
    ppermute x1, starting transfers between devices, body(): left = lax.ppermute(last, 'sub', ring(n_sub, 1))  1.28 us
  transfers between devices with their start and end apart: 4, of which 0 were waited for; matrix products, arithmetic and copies ran while one was open for 0% of the time, Pallas kernels for 4%

profile of v1, /device:TPU:1, one launch (start us, length us, event | category | flops | bytes accessed | tf_op | source)
XLA Modules:
  0.0 59.9 jit_solution(17831653791385802508)
XLA Ops:
  0.6 1.5 %collective-permute-start.1 = (f32[384,128]{1,0:T(8,128)}, f32[384,128]{1,0:T(8,128)S(1)}, u32[]{:S(2)}, u32[]{:S(2)}) collective-permute-start(f32[384,128]{1,0:T(8,128)} %bitcast.7), channel_id=1, source_target_pairs={{0,124},{4,0},{8,4},{12,8},{16,12},{20,16},{24,20},{28,24},{32,28}... | collective-permute-start | bytes 589832 | tf_op jit(solution)/shard_map/ppermute | solution.py:352
  2.1 1.3 %collective-permute-start = (f32[384,128]{1,0:T(8,128)}, f32[384,128]{1,0:T(8,128)S(1)}, u32[]{:S(2)}, u32[]{:S(2)}) collective-permute-start(f32[384,128]{1,0:T(8,128)} %bitcast.8), channel_id=1, source_target_pairs={{0,4},{4,8},{8,12},{12,16},{16,20},{20,24},{24,28},{28,32},{32,36}... | collective-permute-start | bytes 589832 | tf_op jit(solution)/shard_map/ppermute | solution.py:353
  3.5 0.0 copy-start.1
  3.5 1.0 %copy-done.1 = f32[6,32,2,128]{3,2,1,0:T(2,128)S(1)} copy-done((f32[6,32,2,128]{3,2,1,0:T(2,128)S(1)}, f32[6,32,2,128]{3,2,1,0:T(2,128)}, u32[]{:S(2)}) %copy-start.1) | copy-done | bytes 196632
  4.4 0.4 edges.1
  4.8 1.3 %collective-permute-start.2 = (f32[8,128]{1,0:T(8,128)S(1)}, f32[8,128]{1,0:T(8,128)S(1)}, u32[]{:S(2)}, u32[]{:S(2)}) collective-permute-start(f32[8,128]{1,0:T(8,128)S(1)} %get-tuple-element.16), channel_id=1, source_target_pairs={{0,1},{1,2},{2,3},{3,0},{4,5},{5,6},{6,7},{7,4},{8,9},{9,10},{10,1... | collective-permute-start | bytes 12296 | tf_op jit(solution)/shard_map/ppermute | solution.py:364
  6.1 1.5 %collective-permute-start.3 = (f32[8,128]{1,0:T(8,128)S(1)}, f32[8,128]{1,0:T(8,128)S(1)}, u32[]{:S(2)}, u32[]{:S(2)}) collective-permute-start(f32[8,128]{1,0:T(8,128)S(1)} %get-tuple-element.17), channel_id=1, source_target_pairs={{0,3},{1,0},{2,1},{3,2},{4,7},{5,4},{6,5},{7,6},{8,11},{9,8},{10,9... | collective-permute-start | bytes 12296 | tf_op jit(solution)/shard_map/ppermute | solution.py:363
  7.5 0.0 copy-start
  7.5 1.6 %copy-done = bf16[2,32,64,256]{3,2,1,0:T(8,128)(2,1)S(1)} copy-done((bf16[2,32,64,256]{3,2,1,0:T(8,128)(2,1)S(1)}, bf16[2,32,64,256]{3,2,1,0:T(8,128)(2,1)}, u32[]{:S(2)}) %copy-start) | copy-done | bytes 2097176
  9.1 0.0 copy-start.2
  9.1 0.9 %copy-done.2 = f32[6,32,2,128]{3,2,1,0:T(2,128)S(1)} copy-done((f32[6,32,2,128]{3,2,1,0:T(2,128)S(1)}, f32[6,32,2,128]{3,2,1,0:T(2,128)}, u32[]{:S(2)}) %copy-start.2) | copy-done | bytes 196632
  10.1 0.0 copy-start.3
  10.1 0.7 %copy-done.3 = f32[6,32]{1,0:T(8,128)S(1)} copy-done((f32[6,32]{1,0:T(8,128)S(1)}, f32[6,32]{1,0:T(8,128)}, u32[]{:S(2)}) %copy-start.3) | copy-done | bytes 792
  10.8 0.0 copy-start.4
  10.8 0.7 %copy-done.4 = s32[2,128]{1,0:T(2,128)S(1)} copy-done((s32[2,128]{1,0:T(2,128)S(1)}, s32[2,128]{1,0:T(2,128)}, u32[]{:S(2)}) %copy-start.4) | copy-done | bytes 1048
  11.4 0.0 copy-start.5
  11.4 0.7 %copy-done.5 = s32[2,128]{1,0:T(2,128)S(1)} copy-done((s32[2,128]{1,0:T(2,128)S(1)}, s32[2,128]{1,0:T(2,128)}, u32[]{:S(2)}) %copy-start.5) | copy-done | bytes 1048
  12.1 1.8 %early.1 = (f32[2,2,2048,128]{3,2,1,0:T(8,128)S(1)}, f32[2,2,256,128]{3,2,1,0:T(8,128)S(1)}, f32[2,192,128]{2,1,0:T(8,128)S(1)}, f32[192,128]{1,0:T(8,128)S(1)},...) custom-call(f32[384,128]{1,0:T(8,128)S(1)} %bitcast.10, bf16[2,32,64,256]{3,2,1,0:T(8,128)(2,1)S(1)} %copy-done, ...), custom_call_target="tpu_custom_call" | custom-call | flops 4194304 | bytes 6291456 | tf_op jit(solution)/shard_map/early/pallas_call | solution.py:366
  13.9 0.0 collective-permute-done.2.left
  13.9 0.0 collective-permute-done.3.right
  14.0 0.0 collective-permute-done.1.below
  14.0 0.0 collective-permute-done.above
  14.0 1.1 %prepare.1 = (f32[384,128]{1,0:T(8,128)}, f32[256,128]{1,0:T(8,128)S(1)}) custom-call(f32[2,192,128]{2,1,0:T(8,128)S(1)} %get-tuple-element.14.partial, f32[192,128]{1,0:T(8,128)S(1)} %get-tuple-element.15.number, f32[384,128]{1,0:T(8,128)S(1)} %collective-permute-done.above, f32[384,128]{1,0:T(8,128)S(1)} %collective-permute-done.1.below, ...), custom_call_target="tpu_custom_call" | custom-call | tf_op jit(solution)/shard_map/prepare/pallas_call | solution.py:390
  15.1 21.9 %all_to_all.10 = f32[128,2,128]{2,1,0:T(2,128)S(1)} all-to-all(f32[128,2,128]{2,1,0:T(2,128)S(1)} %bitcast.14), channel_id=1, replica_groups=mesh['blk'=32,'sub'=4] {'blk','sub'}, dimensions={0} | all-to-all | bytes 262144 | tf_op jit(solution)/shard_map/all_to_all | solution.py:339
  37.0 7.8 %cloud.1 = f32[256,128]{1,0:T(8,128)S(1)} custom-call(f32[256,128]{1,0:T(8,128)S(1)} %bitcast.12, f32[2,2,2048,128]{3,2,1,0:T(8,128)S(1)} %get-tuple-element.21.start, f32[2,2,256,128]{3,2,1,0:T(8,128)S(1)} %get-tuple-element.22.sums), custom_call_target="tpu_custom_call" | custom-call | tf_op jit(solution)/shard_map/cloud/pallas_call | solution.py:398
  44.9 14.0 %all_to_all.11 = f32[128,2,128]{2,1,0:T(2,128)S(1)} all-to-all(f32[128,2,128]{2,1,0:T(2,128)S(1)} %bitcast.13), channel_id=1, replica_groups=mesh['blk'=32,'sub'=4] {'blk','sub'}, dimensions={0} | all-to-all | bytes 262144 | tf_op jit(solution)/shard_map/all_to_all | solution.py:339
  58.9 0.9 %home.1 = (f32[384,128]{1,0:T(8,128)}, f32[128,128]{1,0:T(8,128)}) custom-call(f32[256,128]{1,0:T(8,128)S(1)} %bitcast.11, bf16[2,128,256]{2,1,0:T(8,128)(2,1)S(1)} %get-tuple-element.18.routes, f32[384,128]{1,0:T(8,128)} %get-tuple-element.23.advanced), custom_call_target="tpu_custom_call", output_to_operand_aliasing={{0}: (2, {})} | custom-call | tf_op jit(solution)/shard_map/home/pallas_call | solution.py:413
Async XLA Ops:
  0.6 13.3 %collective-permute-start.1 = (f32[384,128]{1,0:T(8,128)}, f32[384,128]{1,0:T(8,128)S(1)}, u32[]{:S(2)}, u32[]{:S(2)}) collective-permute-start(f32[384,128]{1,0:T(8,128)} %bitcast.7), channel_id=1, source_target_pairs={{0,124},{4,0},{8,4},{12,8},{16,12},{20,16},{24,20},{28,24},{32,28}... | collective-permute-start | bytes 589832 | tf_op jit(solution)/shard_map/ppermute | solution.py:352
  2.1 11.8 %collective-permute-start = (f32[384,128]{1,0:T(8,128)}, f32[384,128]{1,0:T(8,128)S(1)}, u32[]{:S(2)}, u32[]{:S(2)}) collective-permute-start(f32[384,128]{1,0:T(8,128)} %bitcast.8), channel_id=1, source_target_pairs={{0,4},{4,8},{8,12},{12,16},{16,20},{20,24},{24,28},{28,32},{32,36}... | collective-permute-start | bytes 589832 | tf_op jit(solution)/shard_map/ppermute | solution.py:353
  3.5 1.0 %copy-start.1 = (f32[6,32,2,128]{3,2,1,0:T(2,128)S(1)}, f32[6,32,2,128]{3,2,1,0:T(2,128)}, u32[]{:S(2)}) copy-start(f32[6,32,2,128]{3,2,1,0:T(2,128)} %param.5) | copy-start | bytes 589828
  4.8 9.1 %collective-permute-start.2 = (f32[8,128]{1,0:T(8,128)S(1)}, f32[8,128]{1,0:T(8,128)S(1)}, u32[]{:S(2)}, u32[]{:S(2)}) collective-permute-start(f32[8,128]{1,0:T(8,128)S(1)} %get-tuple-element.16), channel_id=1, source_target_pairs={{0,1},{1,2},{2,3},{3,0},{4,5},{5,6},{6,7},{7,4},{8,9},{9,10},{10,1... | collective-permute-start | bytes 12296 | tf_op jit(solution)/shard_map/ppermute | solution.py:364
  6.1 7.9 %collective-permute-start.3 = (f32[8,128]{1,0:T(8,128)S(1)}, f32[8,128]{1,0:T(8,128)S(1)}, u32[]{:S(2)}, u32[]{:S(2)}) collective-permute-start(f32[8,128]{1,0:T(8,128)S(1)} %get-tuple-element.17), channel_id=1, source_target_pairs={{0,3},{1,0},{2,1},{3,2},{4,7},{5,4},{6,5},{7,6},{8,11},{9,8},{10,9... | collective-permute-start | bytes 12296 | tf_op jit(solution)/shard_map/ppermute | solution.py:363
  7.5 1.6 %copy-start = (bf16[2,32,64,256]{3,2,1,0:T(8,128)(2,1)S(1)}, bf16[2,32,64,256]{3,2,1,0:T(8,128)(2,1)}, u32[]{:S(2)}) copy-start(bf16[2,32,64,256]{3,2,1,0:T(8,128)(2,1)} %crm_hbm.1) | copy-start | bytes 6291460
  9.1 0.9 %copy-start.2 = (f32[6,32,2,128]{3,2,1,0:T(2,128)S(1)}, f32[6,32,2,128]{3,2,1,0:T(2,128)}, u32[]{:S(2)}) copy-start(f32[6,32,2,128]{3,2,1,0:T(2,128)} %param.5) | copy-start | bytes 589828
  10.1 0.7 %copy-start.3 = (f32[6,32]{1,0:T(8,128)S(1)}, f32[6,32]{1,0:T(8,128)}, u32[]{:S(2)}) copy-start(f32[6,32]{1,0:T(8,128)} %diffusion_hbm.1) | copy-start | bytes 2308
  10.8 0.7 %copy-start.4 = (s32[2,128]{1,0:T(2,128)S(1)}, s32[2,128]{1,0:T(2,128)}, u32[]{:S(2)}) copy-start(s32[2,128]{1,0:T(2,128)} %owner_hbm.1) | copy-start | bytes 3076
  11.4 0.7 %copy-start.5 = (s32[2,128]{1,0:T(2,128)S(1)}, s32[2,128]{1,0:T(2,128)}, u32[]{:S(2)}) copy-start(s32[2,128]{1,0:T(2,128)} %branch_hbm.1) | copy-start | bytes 3076

commit v2 on v1

--- a/solution.py
+++ b/solution.py
@@ -129,7 +129,7 @@
             lax.fori_loop(0, CRM_CHUNK, level, 0, unroll=4)
 
 
-def prepare_kernel(partial, number, above, below, left, right, routes, rates, advanced, outgoing):
+def prepare_kernel(partial, number, below, above, left, right, routes, rates, advanced, outgoing):
     lane = lax.broadcasted_iota(jnp.int32, (FIELDS * LEV, LANES), 1)
     level = lax.broadcasted_iota(jnp.int32, (LEV, LANES), 0)
 
@@ -335,6 +335,10 @@
     return jax.ShapeDtypeStruct(shape, jnp.float32)
 
 
+def in_hbm(x):
+    return pltpu.with_memory_space_constraint(x, pltpu.HBM)
+
+
 def transfer(rows):
     moved = lax.all_to_all(
         rows.reshape(DEVICES, 2, LANES), ("blk", "sub"), split_axis=0, concat_axis=0, tiled=True
@@ -349,8 +353,8 @@
     def ring(n, step):
         return [(i, (i + step) % n) for i in range(n)]
 
+    above = lax.ppermute(gcm, "blk", ring(n_blk, 1))
     below = lax.ppermute(gcm, "blk", ring(n_blk, -1))
-    above = lax.ppermute(gcm, "blk", ring(n_blk, 1))
     hbm = pl.BlockSpec(memory_space=pltpu.HBM)
     first, last = pl.pallas_call(
         edge_kernel,
@@ -359,7 +363,7 @@
         scratch_shapes=[pltpu.VMEM((GCM_ROWS, LANES), jnp.float32), pltpu.SemaphoreType.DMA(())],
         compiler_params=pltpu.CompilerParams(vmem_limit_bytes=4 * MIB),
         name="edges",
-    )(gcm)
+    )(in_hbm(gcm))
     right = lax.ppermute(first, "sub", ring(n_sub, -1))
     left = lax.ppermute(last, "sub", ring(n_sub, 1))
     cells = 2 * LEV * NXC * COLS
@@ -386,13 +390,13 @@
         compiler_params=pltpu.CompilerParams(vmem_limit_bytes=16 * MIB),
         cost_estimate=pl.CostEstimate(flops=4 * cells, bytes_accessed=6 * cells, transcendentals=0),
         name="early",
-    )(gcm, crm_state, owner, branch, diffusion)
+    )(*map(in_hbm, (gcm, crm_state, owner, branch, diffusion)))
     advanced, outgoing = pl.pallas_call(
         prepare_kernel,
         out_shape=(f32(GCM_ROWS, LANES), f32(COLS, LANES)),
         compiler_params=pltpu.CompilerParams(vmem_limit_bytes=8 * MIB),
         name="prepare",
-    )(partial, number, above, below, left, right, routes, rates)
+    )(partial, number, below, above, left, right, routes, rates)
 
     incoming = transfer(outgoing)
     profiles = pl.pallas_call(

time: 60.2 us -> 54.5 us (0.905)
  local copies, waits for them, and re-layouts: 5.52 us -> 0 us
  Pallas kernels: 12.1 us -> 13.8 us
  blocking collectives: 35.9 us -> 34.3 us
    unnamed x12 -> x0, local copies, waits for them, and re-layouts: 5.52 us -> none
    all_to_all x2, blocking collectives: 35.9 us -> 34.3 us  [transfer(): lax.all_to_all(rows.reshape(DEVICES, 2, LANES), ('blk', 'sub'), split_axi...]
    ppermute x1, starting transfers between devices: 1.49 us -> 0.01 us  [body(): below = lax.ppermute(gcm, 'blk', ring(n_blk, -1))]
    ppermute x1, starting transfers between devices: 1.35 us -> 2.76 us  [body(): above = lax.ppermute(gcm, 'blk', ring(n_blk, 1))]
    pallas_call x1, Pallas kernels: 1.81 us -> 2.74 us  [body(): pl.pallas_call(early_kernel, in_specs=[hbm] * 5, out_shape=(f32(2, 2, LEV...]
    pallas_call x1, Pallas kernels: 0.36 us -> 1.1 us  [body(): pl.pallas_call(edge_kernel, in_specs=[hbm], out_shape=(f32(SUB, LANES), f...]
  transfers between devices with their start and end apart: 4 -> 4, of which waited for: 0 -> 0; matrix products, arithmetic and copies ran while one was open for 0% -> 0% of each run, Pallas kernels for 4% -> 7%
where the time goes in v2:
time: 54.5 us; the launch traced here: 54.3 us
  blocking collectives  34.3 us (63%)
  Pallas kernels  13.8 us (25%)
  starting transfers between devices  5.5 us (10%)
  between operations  0.68 us (1%)
    all_to_all x2, blocking collectives, transfer(): lax.all_to_all(rows.reshape(DEVICES, 2, LANES), ('blk', 'sub'), split_axi...  34.3 us
    pallas_call x1, Pallas kernels, body(): pl.pallas_call(cloud_kernel, out_shape=f32(COLS, LANES), scratch_shapes=[...  7.84 us
    ppermute x1, starting transfers between devices, body(): above = lax.ppermute(gcm, 'blk', ring(n_blk, 1))  2.76 us
    pallas_call x1, Pallas kernels, body(): pl.pallas_call(early_kernel, in_specs=[hbm] * 5, out_shape=(f32(2, 2, LEV...  2.74 us
    ppermute x1, starting transfers between devices, body(): right = lax.ppermute(first, 'sub', ring(n_sub, -1))  1.47 us
    ppermute x1, starting transfers between devices, body(): left = lax.ppermute(last, 'sub', ring(n_sub, 1))  1.28 us
    pallas_call x1, Pallas kernels, body(): pl.pallas_call(prepare_kernel, out_shape=(f32(GCM_ROWS, LANES), f32(COLS,...  1.14 us
    pallas_call x1, Pallas kernels, body(): pl.pallas_call(edge_kernel, in_specs=[hbm], out_shape=(f32(SUB, LANES), f...  1.1 us
  transfers between devices with their start and end apart: 4, of which 0 were waited for; matrix products, arithmetic and copies ran while one was open for 0% of the time, Pallas kernels for 7%

profile of v2, /device:TPU:1, one launch (start us, length us, event | category | flops | bytes accessed | tf_op | source)
XLA Modules:
  0.0 54.3 jit_solution(6919029631135590833)
XLA Ops:
  0.6 2.8 %collective-permute-start.1 = (f32[384,128]{1,0:T(8,128)}, f32[384,128]{1,0:T(8,128)S(1)}, u32[]{:S(2)}, u32[]{:S(2)}) collective-permute-start(f32[384,128]{1,0:T(8,128)} %bitcast.11), channel_id=1, source_target_pairs={{0,4},{4,8},{8,12},{12,16},{16,20},{20,24},{24,28},{28,32},{32,36}... | collective-permute-start | bytes 589832 | tf_op jit(solution)/shard_map/ppermute | solution.py:356
  3.4 0.0 collective-permute-start
  3.4 1.1 %edges.1 = (f32[8,128]{1,0:T(8,128)S(1)}, f32[8,128]{1,0:T(8,128)S(1)}) custom-call(f32[384,128]{1,0:T(8,128)} %bitcast.13), custom_call_target="tpu_custom_call" | custom-call | tf_op jit(solution)/shard_map/edges/pallas_call | solution.py:359
  4.5 1.3 %collective-permute-start.2 = (f32[8,128]{1,0:T(8,128)S(1)}, f32[8,128]{1,0:T(8,128)S(1)}, u32[]{:S(2)}, u32[]{:S(2)}) collective-permute-start(f32[8,128]{1,0:T(8,128)S(1)} %get-tuple-element.16), channel_id=1, source_target_pairs={{0,1},{1,2},{2,3},{3,0},{4,5},{5,6},{6,7},{7,4},{8,9},{9,10},{10,1... | collective-permute-start | bytes 12296 | tf_op jit(solution)/shard_map/ppermute | solution.py:368
  5.8 1.5 %collective-permute-start.3 = (f32[8,128]{1,0:T(8,128)S(1)}, f32[8,128]{1,0:T(8,128)S(1)}, u32[]{:S(2)}, u32[]{:S(2)}) collective-permute-start(f32[8,128]{1,0:T(8,128)S(1)} %get-tuple-element.17), channel_id=1, source_target_pairs={{0,3},{1,0},{2,1},{3,2},{4,7},{5,4},{6,5},{7,6},{8,11},{9,8},{10,9... | collective-permute-start | bytes 12296 | tf_op jit(solution)/shard_map/ppermute | solution.py:367
  7.2 2.7 %early.1 = (f32[2,2,2048,128]{3,2,1,0:T(8,128)S(1)}, f32[2,2,256,128]{3,2,1,0:T(8,128)S(1)}, f32[2,192,128]{2,1,0:T(8,128)S(1)}, f32[192,128]{1,0:T(8,128)S(1)},...) custom-call(f32[384,128]{1,0:T(8,128)} %bitcast.14, bf16[2,32,64,256]{3,2,1,0:T(8,128)(2,1)} %crm_hbm.1, ...), custom_call_target="tpu_custom_call" | custom-call | flops 4194304 | bytes 6291456 | tf_op jit(solution)/shard_map/early/pallas_call | solution.py:370
  10.0 0.0 collective-permute-done.2.left
  10.0 0.0 collective-permute-done.3.right
  10.0 0.0 collective-permute-done.1.above
  10.0 0.0 collective-permute-done.below
  10.0 1.1 %prepare.1 = (f32[384,128]{1,0:T(8,128)}, f32[256,128]{1,0:T(8,128)S(1)}) custom-call(f32[2,192,128]{2,1,0:T(8,128)S(1)} %get-tuple-element.14.partial, f32[192,128]{1,0:T(8,128)S(1)} %get-tuple-element.15.number, f32[384,128]{1,0:T(8,128)S(1)} %collective-permute-done.below, f32[384,128]{1,0:T(8,128)S(1)} %collective-permute-done.1.above, ...), custom_call_target="tpu_custom_call" | custom-call | tf_op jit(solution)/shard_map/prepare/pallas_call | solution.py:394
  11.2 20.3 %all_to_all.10 = f32[128,2,128]{2,1,0:T(2,128)S(1)} all-to-all(f32[128,2,128]{2,1,0:T(2,128)S(1)} %bitcast.10), channel_id=1, replica_groups=mesh['blk'=32,'sub'=4] {'blk','sub'}, dimensions={0} | all-to-all | bytes 262144 | tf_op jit(solution)/shard_map/all_to_all | solution.py:343
  31.5 7.8 %cloud.1 = f32[256,128]{1,0:T(8,128)S(1)} custom-call(f32[256,128]{1,0:T(8,128)S(1)} %bitcast.8, f32[2,2,2048,128]{3,2,1,0:T(8,128)S(1)} %get-tuple-element.21.start, f32[2,2,256,128]{3,2,1,0:T(8,128)S(1)} %get-tuple-element.22.sums), custom_call_target="tpu_custom_call" | custom-call | tf_op jit(solution)/shard_map/cloud/pallas_call | solution.py:402
  39.3 14.0 %all_to_all.11 = f32[128,2,128]{2,1,0:T(2,128)S(1)} all-to-all(f32[128,2,128]{2,1,0:T(2,128)S(1)} %bitcast.9), channel_id=1, replica_groups=mesh['blk'=32,'sub'=4] {'blk','sub'}, dimensions={0} | all-to-all | bytes 262144 | tf_op jit(solution)/shard_map/all_to_all | solution.py:343
  53.4 0.9 %home.1 = (f32[384,128]{1,0:T(8,128)}, f32[128,128]{1,0:T(8,128)}) custom-call(f32[256,128]{1,0:T(8,128)S(1)} %bitcast.7, bf16[2,128,256]{2,1,0:T(8,128)(2,1)S(1)} %get-tuple-element.18.routes, f32[384,128]{1,0:T(8,128)} %get-tuple-element.23.advanced), custom_call_target="tpu_custom_call", output_to_operand_aliasing={{0}: (2, {})} | custom-call | tf_op jit(solution)/shard_map/home/pallas_call | solution.py:417
Async XLA Ops:
  0.6 9.4 %collective-permute-start.1 = (f32[384,128]{1,0:T(8,128)}, f32[384,128]{1,0:T(8,128)S(1)}, u32[]{:S(2)}, u32[]{:S(2)}) collective-permute-start(f32[384,128]{1,0:T(8,128)} %bitcast.11), channel_id=1, source_target_pairs={{0,4},{4,8},{8,12},{12,16},{16,20},{20,24},{24,28},{28,32},{32,36}... | collective-permute-start | bytes 589832 | tf_op jit(solution)/shard_map/ppermute | solution.py:356
  3.4 6.6 %collective-permute-start = (f32[384,128]{1,0:T(8,128)}, f32[384,128]{1,0:T(8,128)S(1)}, u32[]{:S(2)}, u32[]{:S(2)}) collective-permute-start(f32[384,128]{1,0:T(8,128)} %bitcast.12), channel_id=1, source_target_pairs={{0,124},{4,0},{8,4},{12,8},{16,12},{20,16},{24,20},{28,24},{32,28}... | collective-permute-start | bytes 589832 | tf_op jit(solution)/shard_map/ppermute | solution.py:357
  4.5 5.5 %collective-permute-start.2 = (f32[8,128]{1,0:T(8,128)S(1)}, f32[8,128]{1,0:T(8,128)S(1)}, u32[]{:S(2)}, u32[]{:S(2)}) collective-permute-start(f32[8,128]{1,0:T(8,128)S(1)} %get-tuple-element.16), channel_id=1, source_target_pairs={{0,1},{1,2},{2,3},{3,0},{4,5},{5,6},{6,7},{7,4},{8,9},{9,10},{10,1... | collective-permute-start | bytes 12296 | tf_op jit(solution)/shard_map/ppermute | solution.py:368
  5.8 4.2 %collective-permute-start.3 = (f32[8,128]{1,0:T(8,128)S(1)}, f32[8,128]{1,0:T(8,128)S(1)}, u32[]{:S(2)}, u32[]{:S(2)}) collective-permute-start(f32[8,128]{1,0:T(8,128)S(1)} %get-tuple-element.17), channel_id=1, source_target_pairs={{0,3},{1,0},{2,1},{3,2},{4,7},{5,4},{6,5},{7,6},{8,11},{9,8},{10,9... | collective-permute-start | bytes 12296 | tf_op jit(solution)/shard_map/ppermute | solution.py:367

commit v3 on v2

--- a/solution.py
+++ b/solution.py
@@ -45,23 +45,10 @@
     return ref[pl.ds(y, FIELDS * LEV, stride=2), :]
 
 
-def edge_kernel(gcm_hbm, first, last, gcm, arrival):
-    copy = pltpu.make_async_copy(gcm_hbm, gcm, arrival)
-    copy.start()
-    first[...] = jnp.zeros_like(first)
-    last[...] = jnp.zeros_like(last)
-    copy.wait()
-    rows = jnp.concatenate([rows_of(gcm, 0), rows_of(gcm, 1)], axis=0)
-    for part in range(GCM_ROWS // LANES):
-        turned = jnp.transpose(rows[part * LANES : (part + 1) * LANES])
-        first[part : part + 1, :] = turned[:1]
-        last[part : part + 1, :] = turned[LANES - 1 :]
-
-
-def early_kernel(
-    gcm_hbm, crm_hbm, owner_hbm, branch_hbm, diffusion_hbm,
-    state, sums, partial, number, routes, rates,
-    gcm, crm, owner, branch, diffusion, arrival, crm_arrival,
+def edge_kernel(
+    gcm_hbm, owner_hbm, branch_hbm, diffusion_hbm,
+    gcm, to_chip_mate, to_other, routes, rates, number,
+    owner, branch, diffusion, arrival,
 ):
     loads = [
         pltpu.make_async_copy(source, target, arrival.at[n])
@@ -69,18 +56,10 @@
             [(owner_hbm, owner), (branch_hbm, branch), (diffusion_hbm, diffusion), (gcm_hbm, gcm)]
         )
     ]
-    crm_loads = [
-        pltpu.make_async_copy(
-            crm_hbm.at[f, pl.ds(part * CRM_CHUNK, CRM_CHUNK)],
-            crm.at[f, pl.ds(part * CRM_CHUNK, CRM_CHUNK)],
-            crm_arrival.at[f, part],
-        )
-        for f in range(2)
-        for part in range(LEV // CRM_CHUNK)
-    ]
-    for copy in loads + crm_loads:
+    for copy in loads:
         copy.start()
-
+    to_chip_mate[...] = jnp.zeros_like(to_chip_mate)
+    to_other[...] = jnp.zeros_like(to_other)
     for copy in loads[:3]:
         copy.wait()
     device = lax.broadcasted_iota(jnp.int32, (DEVICES, LANES), 0)
@@ -101,6 +80,27 @@
         number[f * LEV : (f + 1) * LEV, :] = jnp.transpose(spread)
 
     loads[3].wait()
+    even = lax.rem(lax.axis_index("sub"), 2) == 0
+    rows = jnp.concatenate([rows_of(gcm, 0), rows_of(gcm, 1)], axis=0)
+    for part in range(GCM_ROWS // LANES):
+        turned = jnp.transpose(rows[part * LANES : (part + 1) * LANES])
+        first, last = turned[:1], turned[LANES - 1 :]
+        to_chip_mate[part : part + 1, :] = jnp.where(even, last, first)
+        to_other[part : part + 1, :] = jnp.where(even, first, last)
+
+
+def early_kernel(crm_hbm, gcm, number, state, sums, partial, crm, arrival):
+    loads = [
+        pltpu.make_async_copy(
+            crm_hbm.at[f, pl.ds(part * CRM_CHUNK, CRM_CHUNK)],
+            crm.at[f, pl.ds(part * CRM_CHUNK, CRM_CHUNK)],
+            arrival.at[f, part],
+        )
+        for f in range(2)
+        for part in range(LEV // CRM_CHUNK)
+    ]
+    for copy in loads:
+        copy.start()
     lane = lax.broadcasted_iota(jnp.int32, (FIELDS * LEV, LANES), 1)
     own = [rows_of(gcm, 0), rows_of(gcm, 1)]
     for y in range(2):
@@ -111,7 +111,7 @@
 
     for f, (scale, shift) in enumerate([(ALPHA, SHIFT), (BETA, 0.0)]):
         for part in range(LEV // CRM_CHUNK):
-            crm_loads[f * (LEV // CRM_CHUNK) + part].wait()
+            loads[f * (LEV // CRM_CHUNK) + part].wait()
 
             def level(n, carry):
                 k = part * CRM_CHUNK + n
@@ -129,22 +129,31 @@
             lax.fori_loop(0, CRM_CHUNK, level, 0, unroll=4)
 
 
-def prepare_kernel(partial, number, below, above, left, right, routes, rates, advanced, outgoing):
+def prepare_kernel(
+    partial, number, core_mate, neighbour, chip_mate, other, routes, rates, advanced, outgoing
+):
     lane = lax.broadcasted_iota(jnp.int32, (FIELDS * LEV, LANES), 1)
     level = lax.broadcasted_iota(jnp.int32, (LEV, LANES), 0)
 
     def columns(ref):
-        turned = jnp.transpose(ref[...])
+        turned = jnp.transpose(ref)
         column = jnp.concatenate([turned[:, n : n + 1] for n in range(GCM_ROWS // LANES)], axis=0)
         return column[: FIELDS * LEV], column[FIELDS * LEV :]
 
-    vertical = [rows_of(above, 1), rows_of(below, 0)]
-    west, east = columns(left), columns(right)
+    core = lax.rem(lax.axis_index("blk"), 2)
+    inside, outside = rows_of(core_mate, core), rows_of(neighbour, 1 - core)
+    vertical = [
+        jnp.where(core == 0, outside, inside),
+        jnp.where(core == 0, inside, outside),
+    ]
+    even = lax.rem(lax.axis_index("sub"), 2) == 0
+    near, far = chip_mate[...], other[...]
+    west, east = columns(jnp.where(even, far, near)), columns(jnp.where(even, near, far))
     values = []
     for y in range(2):
         side = jnp.where(lane == 0, west[y], jnp.where(lane == LANES - 1, east[y], 0.0))
         state = partial[y] + number[...] * (vertical[y] + side)
-        advanced[pl.ds(2 * 2 * LEV + y, 4 * LEV, stride=2), :] = state[2 * LEV :]
+        advanced[pl.ds(y, 4 * LEV, stride=2), :] = state[2 * LEV :]
         field = [state[f * LEV : (f + 1) * LEV] for f in range(FIELDS)]
         warm = ALPHA * (0.25 * field[0] + 0.2 * field[4])
         wet = BETA * (0.25 * field[1] + 0.2 * field[5])
@@ -160,7 +169,14 @@
         )
 
 
-def cloud_kernel(incoming, start, sums, outgoing, state, coef, mean, total, square):
+def cloud_kernel(
+    incoming, start, sums, advanced, outgoing, gcm_next,
+    state, coef, mean, total, square, departure,
+):
+    leaving = pltpu.make_async_copy(
+        advanced, gcm_next.at[pl.ds(2 * 2 * LEV, 4 * 2 * LEV)], departure
+    )
+    leaving.start()
     level = lax.broadcasted_iota(jnp.int32, (LEV, LANES), 0)
     top = level == LEV - 1
     rates = []
@@ -312,10 +328,11 @@
         outgoing[half * LANES : (half + 1) * LANES, :] = jnp.transpose(
             jnp.concatenate(result, axis=0)
         )
-
-
-def home_kernel(returned, routes, advanced, gcm_next, stats):
-    del advanced
+    leaving.wait()
+
+
+def home_kernel(returned, routes, begun, gcm_next, stats):
+    del begun
     home = None
     for slot in range(2):
         back = returned[pl.ds(slot, DEVICES, stride=2), :]
@@ -348,70 +365,77 @@
 
 def body(gcm_state, crm_state, owner, branch, diffusion):
     gcm = gcm_state.reshape(GCM_ROWS, LANES)
+
+    def pairs(n, first):
+        ahead = [(i, (i + 1) % n) for i in range(first, n, 2)]
+        return ahead + [(j, i) for i, j in ahead]
+
     n_blk, n_sub = lax.axis_size("blk"), lax.axis_size("sub")
-
-    def ring(n, step):
-        return [(i, (i + step) % n) for i in range(n)]
-
-    above = lax.ppermute(gcm, "blk", ring(n_blk, 1))
-    below = lax.ppermute(gcm, "blk", ring(n_blk, -1))
+    neighbour = lax.ppermute(gcm, "blk", pairs(n_blk, 1))
+    core_mate = lax.ppermute(gcm, "blk", pairs(n_blk, 0))
     hbm = pl.BlockSpec(memory_space=pltpu.HBM)
-    first, last = pl.pallas_call(
+    gcm_here, to_chip_mate, to_other, routes, rates, number = pl.pallas_call(
         edge_kernel,
-        in_specs=[hbm],
-        out_shape=(f32(SUB, LANES), f32(SUB, LANES)),
-        scratch_shapes=[pltpu.VMEM((GCM_ROWS, LANES), jnp.float32), pltpu.SemaphoreType.DMA(())],
+        in_specs=[hbm] * 4,
+        out_shape=(
+            f32(GCM_ROWS, LANES),
+            f32(SUB, LANES),
+            f32(SUB, LANES),
+            jax.ShapeDtypeStruct((2, DEVICES, COLS), jnp.bfloat16),
+            f32(2, LANES),
+            f32(FIELDS * LEV, LANES),
+        ),
+        scratch_shapes=[
+            pltpu.VMEM((2, LANES), jnp.int32),
+            pltpu.VMEM((2, LANES), jnp.int32),
+            pltpu.VMEM((FIELDS, LEV), jnp.float32),
+            pltpu.SemaphoreType.DMA((4,)),
+        ],
         compiler_params=pltpu.CompilerParams(vmem_limit_bytes=4 * MIB),
         name="edges",
-    )(in_hbm(gcm))
-    right = lax.ppermute(first, "sub", ring(n_sub, -1))
-    left = lax.ppermute(last, "sub", ring(n_sub, 1))
+    )(*map(in_hbm, (gcm, owner, branch, diffusion)))
+    chip_mate = lax.ppermute(to_chip_mate, "sub", pairs(n_sub, 0))
+    other = lax.ppermute(to_other, "sub", pairs(n_sub, 1))
     cells = 2 * LEV * NXC * COLS
-    state, sums, partial, number, routes, rates = pl.pallas_call(
+    state, sums, partial = pl.pallas_call(
         early_kernel,
-        in_specs=[hbm] * 5,
+        in_specs=[hbm, whole((GCM_ROWS, LANES)), whole((FIELDS * LEV, LANES))],
         out_shape=(
             f32(2, 2, LEV * NXC, LANES),
             f32(2, 2, LEV * SUB, LANES),
             f32(2, FIELDS * LEV, LANES),
-            f32(FIELDS * LEV, LANES),
-            jax.ShapeDtypeStruct((2, DEVICES, COLS), jnp.bfloat16),
-            f32(2, LANES),
         ),
         scratch_shapes=[
-            pltpu.VMEM((GCM_ROWS, LANES), jnp.float32),
             pltpu.VMEM((2, LEV, NXC, COLS), jnp.bfloat16),
-            pltpu.VMEM((2, LANES), jnp.int32),
-            pltpu.VMEM((2, LANES), jnp.int32),
-            pltpu.VMEM((FIELDS, LEV), jnp.float32),
-            pltpu.SemaphoreType.DMA((4,)),
             pltpu.SemaphoreType.DMA((2, LEV // CRM_CHUNK)),
         ],
         compiler_params=pltpu.CompilerParams(vmem_limit_bytes=16 * MIB),
         cost_estimate=pl.CostEstimate(flops=4 * cells, bytes_accessed=6 * cells, transcendentals=0),
         name="early",
-    )(*map(in_hbm, (gcm, crm_state, owner, branch, diffusion)))
+    )(in_hbm(crm_state), gcm_here, number)
     advanced, outgoing = pl.pallas_call(
         prepare_kernel,
-        out_shape=(f32(GCM_ROWS, LANES), f32(COLS, LANES)),
+        out_shape=(f32(4 * 2 * LEV, LANES), f32(COLS, LANES)),
         compiler_params=pltpu.CompilerParams(vmem_limit_bytes=8 * MIB),
         name="prepare",
-    )(partial, number, below, above, left, right, routes, rates)
+    )(partial, number, core_mate, neighbour, chip_mate, other, routes, rates)
 
     incoming = transfer(outgoing)
-    profiles = pl.pallas_call(
+    profiles, gcm_next = pl.pallas_call(
         cloud_kernel,
-        out_shape=f32(COLS, LANES),
+        out_specs=(whole((COLS, LANES)), hbm),
+        out_shape=(f32(COLS, LANES), f32(GCM_ROWS, LANES)),
         scratch_shapes=[
             pltpu.VMEM((2, 2, LEV * NXC, LANES), jnp.float32),
             pltpu.VMEM((8, 2, LEV, LANES), jnp.float32),
             pltpu.VMEM((3, 2, LEV, LANES), jnp.float32),
             pltpu.VMEM((2, LEV * SUB, LANES), jnp.float32),
             pltpu.VMEM((2, LEV * SUB, LANES), jnp.float32),
+            pltpu.SemaphoreType.DMA(()),
         ],
         compiler_params=pltpu.CompilerParams(vmem_limit_bytes=12 * MIB),
         name="cloud",
-    )(incoming, state, sums)
+    )(incoming, state, sums, advanced)
     returned = transfer(profiles)
 
     gcm_next, stats = pl.pallas_call(
@@ -427,7 +451,7 @@
         input_output_aliases={2: 0},
         compiler_params=pltpu.CompilerParams(vmem_limit_bytes=8 * MIB),
         name="home",
-    )(returned, routes, advanced)
+    )(returned, routes, gcm_next)
     return gcm_next.reshape(gcm_state.shape), stats.reshape(2, LEV, 2, LANES)
 
 

time: 54.5 us -> 53.9 us (0.989)
  starting transfers between devices: 5.5 us -> 10.6 us
  blocking collectives: 34.3 us -> 29.8 us
  Pallas kernels: 13.8 us -> 12.6 us
    ppermute x4, starting transfers between devices: 5.5 us -> 10.6 us  [the longest x1 4.75 us: body(): core_mate = lax.ppermute(gcm, 'blk', pairs(n_blk, 0))]
    all_to_all x2, blocking collectives: 34.3 us -> 29.8 us  [transfer(): lax.all_to_all(rows.reshape(DEVICES, 2, LANES), ('blk', 'sub'), split_axi...]
    pallas_call x4, Pallas kernels: 12.8 us -> 11.7 us  [the longest x1 7.82 us: body(): pl.pallas_call(cloud_kernel, out_specs=(whole((COLS, LANES)), hbm), out_s...]
  transfers between devices with their start and end apart: 4 -> 4, of which waited for: 0 -> 0; matrix products, arithmetic and copies ran while one was open for 0% -> 0% of each run, Pallas kernels for 7% -> 6%
where the time goes in v3:
time: 53.9 us; the launch traced here: 53.8 us
  blocking collectives  29.8 us (55%)
  Pallas kernels  12.6 us (23%)
  starting transfers between devices  10.6 us (20%)
  between operations  0.7 us (1%)
    all_to_all x2, blocking collectives, transfer(): lax.all_to_all(rows.reshape(DEVICES, 2, LANES), ('blk', 'sub'), split_axi...  29.8 us
    pallas_call x1, Pallas kernels, body(): pl.pallas_call(cloud_kernel, out_specs=(whole((COLS, LANES)), hbm), out_s...  7.82 us
    ppermute x1, starting transfers between devices, body(): core_mate = lax.ppermute(gcm, 'blk', pairs(n_blk, 0))  4.75 us
    ppermute x1, starting transfers between devices, body(): neighbour = lax.ppermute(gcm, 'blk', pairs(n_blk, 1))  2.77 us
    pallas_call x1, Pallas kernels, body(): pl.pallas_call(early_kernel, in_specs=[hbm, whole((GCM_ROWS, LANES)), who...  2.07 us
    ppermute x1, starting transfers between devices, body(): other = lax.ppermute(to_other, 'sub', pairs(n_sub, 1))  1.82 us
    ppermute x1, starting transfers between devices, body(): chip_mate = lax.ppermute(to_chip_mate, 'sub', pairs(n_sub, 0))  1.29 us
    pallas_call x1, Pallas kernels, body(): pl.pallas_call(edge_kernel, in_specs=[hbm] * 4, out_shape=(f32(GCM_ROWS,...  1.14 us
  transfers between devices with their start and end apart: 4, of which 0 were waited for; matrix products, arithmetic and copies ran while one was open for 0% of the time, Pallas kernels for 6%

profile of v3, /device:TPU:1, one launch (start us, length us, event | category | flops | bytes accessed | tf_op | source)
XLA Modules:
  0.0 53.8 jit_solution(10746246055661877503)
XLA Ops:
  0.6 2.8 %collective-permute-start.1 = (f32[384,128]{1,0:T(8,128)}, f32[384,128]{1,0:T(8,128)S(1)}, u32[]{:S(2)}, u32[]{:S(2)}) collective-permute-start(f32[384,128]{1,0:T(8,128)} %bitcast.12), channel_id=1, source_target_pairs={{4,8},{12,16},{20,24},{28,32},{36,40},{44,48},{52,56},{60,64},{68,... | collective-permute-start | bytes 589832 | tf_op jit(solution)/shard_map/ppermute | solution.py:374
  3.4 4.7 %collective-permute-start = (f32[384,128]{1,0:T(8,128)}, f32[384,128]{1,0:T(8,128)S(1)}, u32[]{:S(2)}, u32[]{:S(2)}) collective-permute-start(f32[384,128]{1,0:T(8,128)} %bitcast.13), channel_id=1, source_target_pairs={{0,4},{8,12},{16,20},{24,28},{32,36},{40,44},{48,52},{56,60},{64,6... | collective-permute-start | bytes 589832 | tf_op jit(solution)/shard_map/ppermute | solution.py:375
  8.1 1.1 %edges.1 = (f32[384,128]{1,0:T(8,128)S(1)}, f32[8,128]{1,0:T(8,128)S(1)}, f32[8,128]{1,0:T(8,128)S(1)}, bf16[2,128,256]{2,1,0:T(8,128)(2,1)S(1)}, f32[2,128]{1,0:T(2,128)S(1)}, /*index=5*/f32[192,128]{1,0:T(8,128)S(1)}) custom-call(f32[384,128]{1,0:T(8,128)} %bitcast.14, s32[2,128]{1,0:T(2,128)} %owner_hbm.1, s32[2,128]{1,0:T(2,128)} %branch_hbm.1, ...), custom_call_target="tpu_custom_call" | custom-call | tf_op jit(solution)/shard_map/edges/pallas_call | solution.py:377
  9.3 1.3 %collective-permute-start.2 = (f32[8,128]{1,0:T(8,128)S(1)}, f32[8,128]{1,0:T(8,128)S(1)}, u32[]{:S(2)}, u32[]{:S(2)}) collective-permute-start(f32[8,128]{1,0:T(8,128)S(1)} %get-tuple-element.20), channel_id=1, source_target_pairs={{0,1},{2,3},{1,0},{3,2},{4,5},{6,7},{5,4},{7,6},{8,9},{10,11},{9,8... | collective-permute-start | bytes 12296 | tf_op jit(solution)/shard_map/ppermute | solution.py:397
  10.6 1.8 %collective-permute-start.3 = (f32[8,128]{1,0:T(8,128)S(1)}, f32[8,128]{1,0:T(8,128)S(1)}, u32[]{:S(2)}, u32[]{:S(2)}) collective-permute-start(f32[8,128]{1,0:T(8,128)S(1)} %get-tuple-element.21), channel_id=1, source_target_pairs={{1,2},{3,0},{2,1},{0,3},{5,6},{7,4},{6,5},{4,7},{9,10},{11,8},{10,... | collective-permute-start | bytes 12296 | tf_op jit(solution)/shard_map/ppermute | solution.py:398
  12.4 2.1 %early.1 = (f32[2,2,2048,128]{3,2,1,0:T(8,128)S(1)}, f32[2,2,256,128]{3,2,1,0:T(8,128)S(1)}, f32[2,192,128]{2,1,0:T(8,128)S(1)}) custom-call(bf16[2,32,64,256]{3,2,1,0:T(8,128)(2,1)} %crm_hbm.1, f32[384,128]{1,0:T(8,128)S(1)} %get-tuple-element.17.gcm, f32[192,128]{1,0:T(8,128)S(1)} %get-tuple-element.18.number), custom_call_target="tpu_custom_call" | custom-call | flops 4194304 | bytes 6291456 | tf_op jit(solution)/shard_map/early/pallas_call | solution.py:400
  14.5 0.0 collective-permute-done.2.chip_mate
  14.5 0.0 collective-permute-done.3.other
  14.5 0.0 collective-permute-done.1.neighbour
  14.5 0.0 collective-permute-done.core_mate
  14.5 0.7 %prepare.1 = (f32[256,128]{1,0:T(8,128)S(1)}, f32[256,128]{1,0:T(8,128)S(1)}) custom-call(f32[2,192,128]{2,1,0:T(8,128)S(1)} %get-tuple-element.19.partial, f32[192,128]{1,0:T(8,128)S(1)} %get-tuple-element.18.number, f32[384,128]{1,0:T(8,128)S(1)} %collective-permute-done.core_mate, f32[384,128]{1,0:T(8,128)S(1)} %collective-permute-done.1.neighbour, ...), custom_call_target="tpu_custom_call" | custom-call | tf_op jit(solution)/shard_map/prepare/pallas_call | solution.py:416
  15.2 15.8 %all_to_all.10 = f32[128,2,128]{2,1,0:T(2,128)S(1)} all-to-all(f32[128,2,128]{2,1,0:T(2,128)S(1)} %bitcast.9), channel_id=1, replica_groups=mesh['blk'=32,'sub'=4] {'blk','sub'}, dimensions={0} | all-to-all | bytes 262144 | tf_op jit(solution)/shard_map/all_to_all | solution.py:360
  31.0 7.8 %cloud.1 = (f32[256,128]{1,0:T(8,128)S(1)}, f32[384,128]{1,0:T(8,128)}) custom-call(f32[256,128]{1,0:T(8,128)S(1)} %bitcast.7, f32[2,2,2048,128]{3,2,1,0:T(8,128)S(1)} %get-tuple-element.25.start, f32[2,2,256,128]{3,2,1,0:T(8,128)S(1)} %get-tuple-element.26.sums, f32[256,128]{1,0:T(8,128)S(1)} %get-tuple-element.27.advanced), custom_call_target="tpu_custom_call" | custom-call | tf_op jit(solution)/shard_map/cloud/pallas_call | solution.py:424
  38.8 14.0 %all_to_all.11 = f32[128,2,128]{2,1,0:T(2,128)S(1)} all-to-all(f32[128,2,128]{2,1,0:T(2,128)S(1)} %bitcast.10), channel_id=1, replica_groups=mesh['blk'=32,'sub'=4] {'blk','sub'}, dimensions={0} | all-to-all | bytes 262144 | tf_op jit(solution)/shard_map/all_to_all | solution.py:360
  52.8 0.9 %home.1 = (f32[384,128]{1,0:T(8,128)}, f32[128,128]{1,0:T(8,128)}) custom-call(f32[256,128]{1,0:T(8,128)S(1)} %bitcast.8, bf16[2,128,256]{2,1,0:T(8,128)(2,1)S(1)} %get-tuple-element.22.routes, f32[384,128]{1,0:T(8,128)} %get-tuple-element.29.begun), custom_call_target="tpu_custom_call", output_to_operand_aliasing={{0}: (2, {})} | custom-call | tf_op jit(solution)/shard_map/home/pallas_call | solution.py:441
Async XLA Ops:
  0.6 13.9 %collective-permute-start.1 = (f32[384,128]{1,0:T(8,128)}, f32[384,128]{1,0:T(8,128)S(1)}, u32[]{:S(2)}, u32[]{:S(2)}) collective-permute-start(f32[384,128]{1,0:T(8,128)} %bitcast.12), channel_id=1, source_target_pairs={{4,8},{12,16},{20,24},{28,32},{36,40},{44,48},{52,56},{60,64},{68,... | collective-permute-start | bytes 589832 | tf_op jit(solution)/shard_map/ppermute | solution.py:374
  3.4 11.1 %collective-permute-start = (f32[384,128]{1,0:T(8,128)}, f32[384,128]{1,0:T(8,128)S(1)}, u32[]{:S(2)}, u32[]{:S(2)}) collective-permute-start(f32[384,128]{1,0:T(8,128)} %bitcast.13), channel_id=1, source_target_pairs={{0,4},{8,12},{16,20},{24,28},{32,36},{40,44},{48,52},{56,60},{64,6... | collective-permute-start | bytes 589832 | tf_op jit(solution)/shard_map/ppermute | solution.py:375
  9.3 5.2 %collective-permute-start.2 = (f32[8,128]{1,0:T(8,128)S(1)}, f32[8,128]{1,0:T(8,128)S(1)}, u32[]{:S(2)}, u32[]{:S(2)}) collective-permute-start(f32[8,128]{1,0:T(8,128)S(1)} %get-tuple-element.20), channel_id=1, source_target_pairs={{0,1},{2,3},{1,0},{3,2},{4,5},{6,7},{5,4},{7,6},{8,9},{10,11},{9,8... | collective-permute-start | bytes 12296 | tf_op jit(solution)/shard_map/ppermute | solution.py:397
  10.6 3.9 %collective-permute-start.3 = (f32[8,128]{1,0:T(8,128)S(1)}, f32[8,128]{1,0:T(8,128)S(1)}, u32[]{:S(2)}, u32[]{:S(2)}) collective-permute-start(f32[8,128]{1,0:T(8,128)S(1)} %get-tuple-element.21), channel_id=1, source_target_pairs={{1,2},{3,0},{2,1},{0,3},{5,6},{7,4},{6,5},{4,7},{9,10},{11,8},{10,... | collective-permute-start | bytes 12296 | tf_op jit(solution)/shard_map/ppermute | solution.py:398

commit v4 on v3

--- a/solution.py
+++ b/solution.py
@@ -18,6 +18,7 @@
 INNER = NXC // SUB
 GCM_ROWS = FIELDS * LEV * 2
 CRM_CHUNK = 8
+PLANE = 8
 ALPHA = 0.3 * math.log2(math.e)
 BETA = 1.5 * ALPHA
 SHIFT = math.log2(0.5 * BETA)
@@ -45,11 +46,22 @@
     return ref[pl.ds(y, FIELDS * LEV, stride=2), :]
 
 
+def cut_kernel(gcm_hbm, row, gcm, arrival):
+    @pl.when(lax.rem(lax.axis_index("blk"), PLANE) == 0)
+    def _():
+        copy = pltpu.make_async_copy(gcm_hbm, gcm, arrival)
+        copy.start()
+        copy.wait()
+        row[: FIELDS * LEV, :] = rows_of(gcm, 0)
+        row[FIELDS * LEV :, :] = jnp.zeros((SUB, LANES), jnp.float32)
+
+
 def edge_kernel(
-    gcm_hbm, owner_hbm, branch_hbm, diffusion_hbm,
-    gcm, to_chip_mate, to_other, routes, rates, number,
+    cut_first, gcm_hbm, owner_hbm, branch_hbm, diffusion_hbm,
+    gcm, to_core_mate, to_chip_mate, to_other, routes, rates, number,
     owner, branch, diffusion, arrival,
 ):
+    del cut_first
     loads = [
         pltpu.make_async_copy(source, target, arrival.at[n])
         for n, (source, target) in enumerate(
@@ -80,6 +92,7 @@
         number[f * LEV : (f + 1) * LEV, :] = jnp.transpose(spread)
 
     loads[3].wait()
+    to_core_mate[...] = rows_of(gcm, 1 - lax.rem(lax.axis_index("blk"), 2))
     even = lax.rem(lax.axis_index("sub"), 2) == 0
     rows = jnp.concatenate([rows_of(gcm, 0), rows_of(gcm, 1)], axis=0)
     for part in range(GCM_ROWS // LANES):
@@ -130,7 +143,8 @@
 
 
 def prepare_kernel(
-    partial, number, core_mate, neighbour, chip_mate, other, routes, rates, advanced, outgoing
+    partial, number, core_mate, other, chip_mate, neighbour, across, routes, rates,
+    advanced, outgoing,
 ):
     lane = lax.broadcasted_iota(jnp.int32, (FIELDS * LEV, LANES), 1)
     level = lax.broadcasted_iota(jnp.int32, (LEV, LANES), 0)
@@ -141,7 +155,9 @@
         return column[: FIELDS * LEV], column[FIELDS * LEV :]
 
     core = lax.rem(lax.axis_index("blk"), 2)
-    inside, outside = rows_of(core_mate, core), rows_of(neighbour, 1 - core)
+    inside = core_mate[...]
+    border = lax.rem(lax.axis_index("blk"), PLANE) == PLANE - 1
+    outside = jnp.where(border, across[: FIELDS * LEV, :], rows_of(neighbour, 1 - core))
     vertical = [
         jnp.where(core == 0, outside, inside),
         jnp.where(core == 0, inside, outside),
@@ -371,14 +387,25 @@
         return ahead + [(j, i) for i, j in ahead]
 
     n_blk, n_sub = lax.axis_size("blk"), lax.axis_size("sub")
-    neighbour = lax.ppermute(gcm, "blk", pairs(n_blk, 1))
-    core_mate = lax.ppermute(gcm, "blk", pairs(n_blk, 0))
     hbm = pl.BlockSpec(memory_space=pltpu.HBM)
-    gcm_here, to_chip_mate, to_other, routes, rates, number = pl.pallas_call(
+    row = pl.pallas_call(
+        cut_kernel,
+        in_specs=[hbm],
+        out_shape=f32(FIELDS * LEV + SUB, LANES),
+        scratch_shapes=[pltpu.VMEM((GCM_ROWS, LANES), jnp.float32), pltpu.SemaphoreType.DMA(())],
+        compiler_params=pltpu.CompilerParams(vmem_limit_bytes=4 * MIB),
+        name="cut",
+    )(in_hbm(gcm))
+    down = [(i, (i - 1) % n_blk) for i in range(0, n_blk, PLANE)]
+    across = lax.ppermute(row, "blk", down)
+    near = [pair for pair in pairs(n_blk, 1) if pair not in down]
+    neighbour = lax.ppermute(gcm, "blk", near)
+    gcm_here, to_core_mate, to_chip_mate, to_other, routes, rates, number = pl.pallas_call(
         edge_kernel,
-        in_specs=[hbm] * 4,
+        in_specs=[pl.BlockSpec(memory_space=pl.ANY)] + [hbm] * 4,
         out_shape=(
             f32(GCM_ROWS, LANES),
+            f32(FIELDS * LEV, LANES),
             f32(SUB, LANES),
             f32(SUB, LANES),
             jax.ShapeDtypeStruct((2, DEVICES, COLS), jnp.bfloat16),
@@ -393,9 +420,10 @@
         ],
         compiler_params=pltpu.CompilerParams(vmem_limit_bytes=4 * MIB),
         name="edges",
-    )(*map(in_hbm, (gcm, owner, branch, diffusion)))
+    )(row, *map(in_hbm, (gcm, owner, branch, diffusion)))
     chip_mate = lax.ppermute(to_chip_mate, "sub", pairs(n_sub, 0))
     other = lax.ppermute(to_other, "sub", pairs(n_sub, 1))
+    core_mate = lax.ppermute(to_core_mate, "blk", pairs(n_blk, 0))
     cells = 2 * LEV * NXC * COLS
     state, sums, partial = pl.pallas_call(
         early_kernel,
@@ -418,7 +446,7 @@
         out_shape=(f32(4 * 2 * LEV, LANES), f32(COLS, LANES)),
         compiler_params=pltpu.CompilerParams(vmem_limit_bytes=8 * MIB),
         name="prepare",
-    )(partial, number, core_mate, neighbour, chip_mate, other, routes, rates)
+    )(partial, number, core_mate, other, chip_mate, neighbour, across, routes, rates)
 
     incoming = transfer(outgoing)
     profiles, gcm_next = pl.pallas_call(

time: 53.9 us -> 56.9 us (1.056)
  starting transfers between devices: 10.6 us -> 13.2 us
    ppermute x2 -> x3, starting transfers between devices: 7.51 us -> 10.7 us  [the longest x1 5.46 us: body(): core_mate = lax.ppermute(to_core_mate, 'blk', pairs(n_blk, 0))]
    ppermute x1, starting transfers between devices: 1.29 us -> 0.01 us  [body(): chip_mate = lax.ppermute(to_chip_mate, 'sub', pairs(n_sub, 0))]
    ppermute x1, starting transfers between devices: 1.82 us -> 2.49 us  [body(): other = lax.ppermute(to_other, 'sub', pairs(n_sub, 1))]
    pallas_call x1 -> x2, Pallas kernels: 1.14 us -> 1.18 us  [the longest x1 1.15 us: body(): pl.pallas_call(edge_kernel, in_specs=[pl.BlockSpec(memory_space=pl.ANY)]...]
  transfers between devices with their start and end apart: 4 -> 5, of which waited for: 0 -> 1; matrix products, arithmetic and copies ran while one was open for 0% -> 0% of each run, Pallas kernels for 6% -> 6%
where the time goes in v4:
time: 56.9 us; the launch traced here: 56.7 us
  blocking collectives  29.7 us (52%)
  starting transfers between devices  13.2 us (23%)
  Pallas kernels  12.7 us (22%)
  between operations  0.7 us (1%)
    all_to_all x2, blocking collectives, transfer(): lax.all_to_all(rows.reshape(DEVICES, 2, LANES), ('blk', 'sub'), split_axi...  29.7 us
    pallas_call x1, Pallas kernels, body(): pl.pallas_call(cloud_kernel, out_specs=(whole((COLS, LANES)), hbm), out_s...  7.82 us
    ppermute x1, starting transfers between devices, body(): core_mate = lax.ppermute(to_core_mate, 'blk', pairs(n_blk, 0))  5.46 us
    ppermute x1, starting transfers between devices, body(): neighbour = lax.ppermute(gcm, 'blk', near)  4.6 us
    ppermute x1, starting transfers between devices, body(): other = lax.ppermute(to_other, 'sub', pairs(n_sub, 1))  2.49 us
    pallas_call x1, Pallas kernels, body(): pl.pallas_call(early_kernel, in_specs=[hbm, whole((GCM_ROWS, LANES)), who...  2.07 us
    pallas_call x1, Pallas kernels, body(): pl.pallas_call(edge_kernel, in_specs=[pl.BlockSpec(memory_space=pl.ANY)]...  1.15 us
  transfers between devices with their start and end apart: 5, of which 1 were waited for; matrix products, arithmetic and copies ran while one was open for 0% of the time, Pallas kernels for 6%

profile of v4, /device:TPU:1, one launch (start us, length us, event | category | flops | bytes accessed | tf_op | source)
XLA Modules:
  0.0 56.7 jit_solution(8413220024487927844)
XLA Ops:
  0.6 4.6 %collective-permute-start.3 = (f32[384,128]{1,0:T(8,128)}, f32[384,128]{1,0:T(8,128)S(1)}, u32[]{:S(2)}, u32[]{:S(2)}) collective-permute-start(f32[384,128]{1,0:T(8,128)} %bitcast.11), channel_id=1, source_target_pairs={{4,8},{12,16},{20,24},{28,32},{36,40},{44,48},{52,56},{60,64},{68,... | collective-permute-start | bytes 589832 | tf_op jit(solution)/shard_map/ppermute | solution.py:402
  5.3 0.7 %collective-permute-start.4 = (f32[200,128]{1,0:T(8,128)S(1)}, f32[200,128]{1,0:T(8,128)S(1)}, u32[]{:S(2)}, u32[]{:S(2)}) collective-permute-start(f32[200,128]{1,0:T(8,128)S(1)} %cut.1.cut_first), channel_id=1, source_target_pairs={{0,124},{32,28},{64,60},{96,92},{1,125},{33,29},{65,61},{97,93},{2... | collective-permute-start | bytes 307208 | tf_op jit(solution)/shard_map/ppermute | solution.py:400
  5.9 1.1 %edges.1 = (f32[384,128]{1,0:T(8,128)S(1)}, f32[192,128]{1,0:T(8,128)S(1)}, f32[8,128]{1,0:T(8,128)S(1)}, f32[8,128]{1,0:T(8,128)S(1)}, bf16[2,128,256]{2,1,0:T(...) custom-call(f32[200,128]{1,0:T(8,128)S(1)} %cut.1.cut_first, f32[384,128]{1,0:T(8,128)} %bitcast.13, ...), custom_call_target="tpu_custom_call" | custom-call | tf_op jit(solution)/shard_map/edges/pallas_call | solution.py:403
  7.1 5.5 %collective-permute-start = (f32[192,128]{1,0:T(8,128)S(1)}, f32[192,128]{1,0:T(8,128)S(1)}, u32[]{:S(2)}, u32[]{:S(2)}) collective-permute-start(f32[192,128]{1,0:T(8,128)S(1)} %get-tuple-element.21), channel_id=1, source_target_pairs={{0,4},{8,12},{16,20},{24,28},{32,36},{40,44},{48,52},{56,60},{64,6... | collective-permute-start | bytes 294920 | tf_op jit(solution)/shard_map/ppermute | solution.py:426
  12.6 2.5 %collective-permute-start.1 = (f32[8,128]{1,0:T(8,128)S(1)}, f32[8,128]{1,0:T(8,128)S(1)}, u32[]{:S(2)}, u32[]{:S(2)}) collective-permute-start(f32[8,128]{1,0:T(8,128)S(1)} %get-tuple-element.22), channel_id=1, source_target_pairs={{1,2},{3,0},{2,1},{0,3},{5,6},{7,4},{6,5},{4,7},{9,10},{11,8},{10,... | collective-permute-start | bytes 12296 | tf_op jit(solution)/shard_map/ppermute | solution.py:425
  15.1 0.0 collective-permute-start.2
  15.1 2.1 %early.1 = (f32[2,2,2048,128]{3,2,1,0:T(8,128)S(1)}, f32[2,2,256,128]{3,2,1,0:T(8,128)S(1)}, f32[2,192,128]{2,1,0:T(8,128)S(1)}) custom-call(bf16[2,32,64,256]{3,2,1,0:T(8,128)(2,1)} %crm_hbm.1, f32[384,128]{1,0:T(8,128)S(1)} %get-tuple-element.18.gcm, f32[192,128]{1,0:T(8,128)S(1)} %get-tuple-element.19.number), custom_call_target="tpu_custom_call" | custom-call | flops 4194304 | bytes 6291456 | tf_op jit(solution)/shard_map/early/pallas_call | solution.py:428
  17.1 0.0 collective-permute-done.1.other
  17.2 0.4 collective-permute-done.2.chip_mate
  17.5 0.0 collective-permute-done.core_mate
  17.5 0.0 collective-permute-done.4.across
  17.5 0.0 collective-permute-done.3.neighbour
  17.5 0.7 %prepare.1 = (f32[256,128]{1,0:T(8,128)S(1)}, f32[256,128]{1,0:T(8,128)S(1)}) custom-call(f32[2,192,128]{2,1,0:T(8,128)S(1)} %get-tuple-element.20.partial, f32[192,128]{1,0:T(8,128)S(1)} %get-tuple-element.19.number, f32[192,128]{1,0:T(8,128)S(1)} %collective-permute-done.core_mate, f32[8,128]{1,0:T(8,128)S(1)} %collective-permute-done.1.other, ...), custom_call_target="tpu_custom_call" | custom-call | tf_op jit(solution)/shard_map/prepare/pallas_call | solution.py:444
  18.2 15.7 %all_to_all.10 = f32[128,2,128]{2,1,0:T(2,128)S(1)} all-to-all(f32[128,2,128]{2,1,0:T(2,128)S(1)} %bitcast.9), channel_id=1, replica_groups=mesh['blk'=32,'sub'=4] {'blk','sub'}, dimensions={0} | all-to-all | bytes 262144 | tf_op jit(solution)/shard_map/all_to_all | solution.py:376
  33.9 7.8 %cloud.1 = (f32[256,128]{1,0:T(8,128)S(1)}, f32[384,128]{1,0:T(8,128)}) custom-call(f32[256,128]{1,0:T(8,128)S(1)} %bitcast.7, f32[2,2,2048,128]{3,2,1,0:T(8,128)S(1)} %get-tuple-element.27.start, f32[2,2,256,128]{3,2,1,0:T(8,128)S(1)} %get-tuple-element.28.sums, f32[256,128]{1,0:T(8,128)S(1)} %get-tuple-element.29.advanced), custom_call_target="tpu_custom_call" | custom-call | tf_op jit(solution)/shard_map/cloud/pallas_call | solution.py:452
  41.7 14.0 %all_to_all.11 = f32[128,2,128]{2,1,0:T(2,128)S(1)} all-to-all(f32[128,2,128]{2,1,0:T(2,128)S(1)} %bitcast.10), channel_id=1, replica_groups=mesh['blk'=32,'sub'=4] {'blk','sub'}, dimensions={0} | all-to-all | bytes 262144 | tf_op jit(solution)/shard_map/all_to_all | solution.py:376
  55.7 0.9 %home.1 = (f32[384,128]{1,0:T(8,128)}, f32[128,128]{1,0:T(8,128)}) custom-call(f32[256,128]{1,0:T(8,128)S(1)} %bitcast.8, bf16[2,128,256]{2,1,0:T(8,128)(2,1)S(1)} %get-tuple-element.24.routes, f32[384,128]{1,0:T(8,128)} %get-tuple-element.31.begun), custom_call_target="tpu_custom_call", output_to_operand_aliasing={{0}: (2, {})} | custom-call | tf_op jit(solution)/shard_map/home/pallas_call | solution.py:469
  (1 shorter events, 0.0 us)
Async XLA Ops:
  0.6 16.9 %collective-permute-start.3 = (f32[384,128]{1,0:T(8,128)}, f32[384,128]{1,0:T(8,128)S(1)}, u32[]{:S(2)}, u32[]{:S(2)}) collective-permute-start(f32[384,128]{1,0:T(8,128)} %bitcast.11), channel_id=1, source_target_pairs={{4,8},{12,16},{20,24},{28,32},{36,40},{44,48},{52,56},{60,64},{68,... | collective-permute-start | bytes 589832 | tf_op jit(solution)/shard_map/ppermute | solution.py:402
  5.3 12.3 %collective-permute-start.4 = (f32[200,128]{1,0:T(8,128)S(1)}, f32[200,128]{1,0:T(8,128)S(1)}, u32[]{:S(2)}, u32[]{:S(2)}) collective-permute-start(f32[200,128]{1,0:T(8,128)S(1)} %cut.1.cut_first), channel_id=1, source_target_pairs={{0,124},{32,28},{64,60},{96,92},{1,125},{33,29},{65,61},{97,93},{2... | collective-permute-start | bytes 307208 | tf_op jit(solution)/shard_map/ppermute | solution.py:400
  7.1 10.4 %collective-permute-start = (f32[192,128]{1,0:T(8,128)S(1)}, f32[192,128]{1,0:T(8,128)S(1)}, u32[]{:S(2)}, u32[]{:S(2)}) collective-permute-start(f32[192,128]{1,0:T(8,128)S(1)} %get-tuple-element.21), channel_id=1, source_target_pairs={{0,4},{8,12},{16,20},{24,28},{32,36},{40,44},{48,52},{56,60},{64,6... | collective-permute-start | bytes 294920 | tf_op jit(solution)/shard_map/ppermute | solution.py:426
  12.6 4.6 %collective-permute-start.1 = (f32[8,128]{1,0:T(8,128)S(1)}, f32[8,128]{1,0:T(8,128)S(1)}, u32[]{:S(2)}, u32[]{:S(2)}) collective-permute-start(f32[8,128]{1,0:T(8,128)S(1)} %get-tuple-element.22), channel_id=1, source_target_pairs={{1,2},{3,0},{2,1},{0,3},{5,6},{7,4},{6,5},{4,7},{9,10},{11,8},{10,... | collective-permute-start | bytes 12296 | tf_op jit(solution)/shard_map/ppermute | solution.py:425
  15.1 2.5 %collective-permute-start.2 = (f32[8,128]{1,0:T(8,128)S(1)}, f32[8,128]{1,0:T(8,128)S(1)}, u32[]{:S(2)}, u32[]{:S(2)}) collective-permute-start(f32[8,128]{1,0:T(8,128)S(1)} %get-tuple-element.23), channel_id=1, source_target_pairs={{0,1},{2,3},{1,0},{3,2},{4,5},{6,7},{5,4},{7,6},{8,9},{10,11},{9,8... | collective-permute-start | bytes 12296 | tf_op jit(solution)/shard_map/ppermute | solution.py:424

commit v5 on v3

--- a/solution.py
+++ b/solution.py
@@ -47,7 +47,7 @@
 
 def edge_kernel(
     gcm_hbm, owner_hbm, branch_hbm, diffusion_hbm,
-    gcm, to_chip_mate, to_other, routes, rates, number,
+    gcm, to_core_mate, to_neighbour, to_chip_mate, to_other, routes, rates, number,
     owner, branch, diffusion, arrival,
 ):
     loads = [
@@ -80,6 +80,9 @@
         number[f * LEV : (f + 1) * LEV, :] = jnp.transpose(spread)
 
     loads[3].wait()
+    core = lax.rem(lax.axis_index("blk"), 2)
+    to_core_mate[...] = rows_of(gcm, 1 - core)
+    to_neighbour[...] = rows_of(gcm, core)
     even = lax.rem(lax.axis_index("sub"), 2) == 0
     rows = jnp.concatenate([rows_of(gcm, 0), rows_of(gcm, 1)], axis=0)
     for part in range(GCM_ROWS // LANES):
@@ -130,7 +133,7 @@
 
 
 def prepare_kernel(
-    partial, number, core_mate, neighbour, chip_mate, other, routes, rates, advanced, outgoing
+    partial, number, neighbour, core_mate, other, chip_mate, routes, rates, advanced, outgoing
 ):
     lane = lax.broadcasted_iota(jnp.int32, (FIELDS * LEV, LANES), 1)
     level = lax.broadcasted_iota(jnp.int32, (LEV, LANES), 0)
@@ -141,7 +144,7 @@
         return column[: FIELDS * LEV], column[FIELDS * LEV :]
 
     core = lax.rem(lax.axis_index("blk"), 2)
-    inside, outside = rows_of(core_mate, core), rows_of(neighbour, 1 - core)
+    inside, outside = core_mate[...], neighbour[...]
     vertical = [
         jnp.where(core == 0, outside, inside),
         jnp.where(core == 0, inside, outside),
@@ -371,14 +374,14 @@
         return ahead + [(j, i) for i, j in ahead]
 
     n_blk, n_sub = lax.axis_size("blk"), lax.axis_size("sub")
-    neighbour = lax.ppermute(gcm, "blk", pairs(n_blk, 1))
-    core_mate = lax.ppermute(gcm, "blk", pairs(n_blk, 0))
     hbm = pl.BlockSpec(memory_space=pltpu.HBM)
-    gcm_here, to_chip_mate, to_other, routes, rates, number = pl.pallas_call(
+    gcm_here, to_core_mate, to_neighbour, to_chip_mate, to_other, routes, rates, number = pl.pallas_call(
         edge_kernel,
         in_specs=[hbm] * 4,
         out_shape=(
             f32(GCM_ROWS, LANES),
+            f32(FIELDS * LEV, LANES),
+            f32(FIELDS * LEV, LANES),
             f32(SUB, LANES),
             f32(SUB, LANES),
             jax.ShapeDtypeStruct((2, DEVICES, COLS), jnp.bfloat16),
@@ -394,6 +397,8 @@
         compiler_params=pltpu.CompilerParams(vmem_limit_bytes=4 * MIB),
         name="edges",
     )(*map(in_hbm, (gcm, owner, branch, diffusion)))
+    neighbour = lax.ppermute(to_neighbour, "blk", pairs(n_blk, 1))
+    core_mate = lax.ppermute(to_core_mate, "blk", pairs(n_blk, 0))
     chip_mate = lax.ppermute(to_chip_mate, "sub", pairs(n_sub, 0))
     other = lax.ppermute(to_other, "sub", pairs(n_sub, 1))
     cells = 2 * LEV * NXC * COLS
@@ -418,7 +423,7 @@
         out_shape=(f32(4 * 2 * LEV, LANES), f32(COLS, LANES)),
         compiler_params=pltpu.CompilerParams(vmem_limit_bytes=8 * MIB),
         name="prepare",
-    )(partial, number, core_mate, neighbour, chip_mate, other, routes, rates)
+    )(partial, number, neighbour, core_mate, other, chip_mate, routes, rates)
 
     incoming = transfer(outgoing)
     profiles, gcm_next = pl.pallas_call(

time: 53.9 us -> 53.7 us (level)
  starting transfers between devices: 10.6 us -> 9.99 us
    ppermute x1, starting transfers between devices: 1.29 us -> 0.01 us  [body(): chip_mate = lax.ppermute(to_chip_mate, 'sub', pairs(n_sub, 0))]
    ppermute x1, starting transfers between devices: 1.82 us -> 2.48 us  [body(): other = lax.ppermute(to_other, 'sub', pairs(n_sub, 1))]
  transfers between devices with their start and end apart: 4 -> 4, of which waited for: 0 -> 1; matrix products, arithmetic and copies ran while one was open for 0% -> 0% of each run, Pallas kernels for 6% -> 4%
where the time goes in v5:
time: 53.7 us; the launch traced here: 53.5 us
  blocking collectives  29.8 us (55%)
  Pallas kernels  12.6 us (23%)
  starting transfers between devices  9.99 us (19%)
  between operations  0.67 us (1%)
    all_to_all x2, blocking collectives, transfer(): lax.all_to_all(rows.reshape(DEVICES, 2, LANES), ('blk', 'sub'), split_axi...  29.8 us
    pallas_call x1, Pallas kernels, body(): pl.pallas_call(cloud_kernel, out_specs=(whole((COLS, LANES)), hbm), out_s...  7.82 us
    ppermute x1, starting transfers between devices, body(): core_mate = lax.ppermute(to_core_mate, 'blk', pairs(n_blk, 0))  4.75 us
    ppermute x1, starting transfers between devices, body(): neighbour = lax.ppermute(to_neighbour, 'blk', pairs(n_blk, 1))  2.77 us
    ppermute x1, starting transfers between devices, body(): other = lax.ppermute(to_other, 'sub', pairs(n_sub, 1))  2.48 us
    pallas_call x1, Pallas kernels, body(): pl.pallas_call(early_kernel, in_specs=[hbm, whole((GCM_ROWS, LANES)), who...  2.07 us
    pallas_call x1, Pallas kernels, body(): pl.pallas_call(edge_kernel, in_specs=[hbm] * 4, out_shape=(f32(GCM_ROWS,...  1.15 us
  transfers between devices with their start and end apart: 4, of which 1 were waited for; matrix products, arithmetic and copies ran while one was open for 0% of the time, Pallas kernels for 4%

profile of v5, /device:TPU:1, one launch (start us, length us, event | category | flops | bytes accessed | tf_op | source)
XLA Modules:
  0.0 53.5 jit_solution(13176155915314417029)
XLA Ops:
  0.6 1.1 %edges.1 = (f32[384,128]{1,0:T(8,128)S(1)}, f32[192,128]{1,0:T(8,128)S(1)}, f32[192,128]{1,0:T(8,128)S(1)}, f32[8,128]{1,0:T(8,128)S(1)}, f32[8,128]{1,0:T(8,128...) custom-call(f32[384,128]{1,0:T(8,128)} %bitcast.12, s32[2,128]{1,0:T(2,128)} %owner_hbm.1, ...), custom_call_target="tpu_custom_call" | custom-call | tf_op jit(solution)/shard_map/edges/pallas_call | solution.py:378
  1.8 2.8 %collective-permute-start = (f32[192,128]{1,0:T(8,128)S(1)}, f32[192,128]{1,0:T(8,128)S(1)}, u32[]{:S(2)}, u32[]{:S(2)}) collective-permute-start(f32[192,128]{1,0:T(8,128)S(1)} %get-tuple-element.22), channel_id=1, source_target_pairs={{4,8},{12,16},{20,24},{28,32},{36,40},{44,48},{52,56},{60,64},{68,... | collective-permute-start | bytes 294920 | tf_op jit(solution)/shard_map/ppermute | solution.py:400
  4.6 4.7 %collective-permute-start.1 = (f32[192,128]{1,0:T(8,128)S(1)}, f32[192,128]{1,0:T(8,128)S(1)}, u32[]{:S(2)}, u32[]{:S(2)}) collective-permute-start(f32[192,128]{1,0:T(8,128)S(1)} %get-tuple-element.23), channel_id=1, source_target_pairs={{0,4},{8,12},{16,20},{24,28},{32,36},{40,44},{48,52},{56,60},{64,6... | collective-permute-start | bytes 294920 | tf_op jit(solution)/shard_map/ppermute | solution.py:401
  9.3 2.5 %collective-permute-start.2 = (f32[8,128]{1,0:T(8,128)S(1)}, f32[8,128]{1,0:T(8,128)S(1)}, u32[]{:S(2)}, u32[]{:S(2)}) collective-permute-start(f32[8,128]{1,0:T(8,128)S(1)} %get-tuple-element.24), channel_id=1, source_target_pairs={{1,2},{3,0},{2,1},{0,3},{5,6},{7,4},{6,5},{4,7},{9,10},{11,8},{10,... | collective-permute-start | bytes 12296 | tf_op jit(solution)/shard_map/ppermute | solution.py:403
  11.8 0.0 collective-permute-start.3
  11.8 2.1 %early.1 = (f32[2,2,2048,128]{3,2,1,0:T(8,128)S(1)}, f32[2,2,256,128]{3,2,1,0:T(8,128)S(1)}, f32[2,192,128]{2,1,0:T(8,128)S(1)}) custom-call(bf16[2,32,64,256]{3,2,1,0:T(8,128)(2,1)} %crm_hbm.1, f32[384,128]{1,0:T(8,128)S(1)} %get-tuple-element.19.gcm, f32[192,128]{1,0:T(8,128)S(1)} %get-tuple-element.20.number), custom_call_target="tpu_custom_call" | custom-call | flops 4194304 | bytes 6291456 | tf_op jit(solution)/shard_map/early/pallas_call | solution.py:405
  13.9 0.0 collective-permute-done.2.other
  13.9 0.4 collective-permute-done.3.chip_mate
  14.2 0.0 collective-permute-done.neighbour
  14.2 0.0 collective-permute-done.1.core_mate
  14.2 0.7 %prepare.1 = (f32[256,128]{1,0:T(8,128)S(1)}, f32[256,128]{1,0:T(8,128)S(1)}) custom-call(f32[2,192,128]{2,1,0:T(8,128)S(1)} %get-tuple-element.21.partial, f32[192,128]{1,0:T(8,128)S(1)} %get-tuple-element.20.number, f32[192,128]{1,0:T(8,128)S(1)} %collective-permute-done.neighbour, f32[192,128]{1,0:T(8,128)S(1)} %collective-permute-done.1.core_mate, ...), custom_call_target="tpu_custom_call" | custom-call | tf_op jit(solution)/shard_map/prepare/pallas_call | solution.py:421
  14.9 15.8 %all_to_all.10 = f32[128,2,128]{2,1,0:T(2,128)S(1)} all-to-all(f32[128,2,128]{2,1,0:T(2,128)S(1)} %bitcast.9), channel_id=1, replica_groups=mesh['blk'=32,'sub'=4] {'blk','sub'}, dimensions={0} | all-to-all | bytes 262144 | tf_op jit(solution)/shard_map/all_to_all | solution.py:363
  30.7 7.8 %cloud.1 = (f32[256,128]{1,0:T(8,128)S(1)}, f32[384,128]{1,0:T(8,128)}) custom-call(f32[256,128]{1,0:T(8,128)S(1)} %bitcast.7, f32[2,2,2048,128]{3,2,1,0:T(8,128)S(1)} %get-tuple-element.29.start, f32[2,2,256,128]{3,2,1,0:T(8,128)S(1)} %get-tuple-element.30.sums, f32[256,128]{1,0:T(8,128)S(1)} %get-tuple-element.31.advanced), custom_call_target="tpu_custom_call" | custom-call | tf_op jit(solution)/shard_map/cloud/pallas_call | solution.py:429
  38.5 14.0 %all_to_all.11 = f32[128,2,128]{2,1,0:T(2,128)S(1)} all-to-all(f32[128,2,128]{2,1,0:T(2,128)S(1)} %bitcast.10), channel_id=1, replica_groups=mesh['blk'=32,'sub'=4] {'blk','sub'}, dimensions={0} | all-to-all | bytes 262144 | tf_op jit(solution)/shard_map/all_to_all | solution.py:363
  52.6 0.9 %home.1 = (f32[384,128]{1,0:T(8,128)}, f32[128,128]{1,0:T(8,128)}) custom-call(f32[256,128]{1,0:T(8,128)S(1)} %bitcast.8, bf16[2,128,256]{2,1,0:T(8,128)(2,1)S(1)} %get-tuple-element.26.routes, f32[384,128]{1,0:T(8,128)} %get-tuple-element.33.begun), custom_call_target="tpu_custom_call", output_to_operand_aliasing={{0}: (2, {})} | custom-call | tf_op jit(solution)/shard_map/home/pallas_call | solution.py:446
Async XLA Ops:
  1.8 12.5 %collective-permute-start = (f32[192,128]{1,0:T(8,128)S(1)}, f32[192,128]{1,0:T(8,128)S(1)}, u32[]{:S(2)}, u32[]{:S(2)}) collective-permute-start(f32[192,128]{1,0:T(8,128)S(1)} %get-tuple-element.22), channel_id=1, source_target_pairs={{4,8},{12,16},{20,24},{28,32},{36,40},{44,48},{52,56},{60,64},{68,... | collective-permute-start | bytes 294920 | tf_op jit(solution)/shard_map/ppermute | solution.py:400
  4.6 9.7 %collective-permute-start.1 = (f32[192,128]{1,0:T(8,128)S(1)}, f32[192,128]{1,0:T(8,128)S(1)}, u32[]{:S(2)}, u32[]{:S(2)}) collective-permute-start(f32[192,128]{1,0:T(8,128)S(1)} %get-tuple-element.23), channel_id=1, source_target_pairs={{0,4},{8,12},{16,20},{24,28},{32,36},{40,44},{48,52},{56,60},{64,6... | collective-permute-start | bytes 294920 | tf_op jit(solution)/shard_map/ppermute | solution.py:401
  9.3 4.6 %collective-permute-start.2 = (f32[8,128]{1,0:T(8,128)S(1)}, f32[8,128]{1,0:T(8,128)S(1)}, u32[]{:S(2)}, u32[]{:S(2)}) collective-permute-start(f32[8,128]{1,0:T(8,128)S(1)} %get-tuple-element.24), channel_id=1, source_target_pairs={{1,2},{3,0},{2,1},{0,3},{5,6},{7,4},{6,5},{4,7},{9,10},{11,8},{10,... | collective-permute-start | bytes 12296 | tf_op jit(solution)/shard_map/ppermute | solution.py:403
  11.8 2.5 %collective-permute-start.3 = (f32[8,128]{1,0:T(8,128)S(1)}, f32[8,128]{1,0:T(8,128)S(1)}, u32[]{:S(2)}, u32[]{:S(2)}) collective-permute-start(f32[8,128]{1,0:T(8,128)S(1)} %get-tuple-element.25), channel_id=1, source_target_pairs={{0,1},{2,3},{1,0},{3,2},{4,5},{6,7},{5,4},{7,6},{8,9},{10,11},{9,8... | collective-permute-start | bytes 12296 | tf_op jit(solution)/shard_map/ppermute | solution.py:402

commit v6 on v4

--- a/solution.py
+++ b/solution.py
@@ -58,7 +58,7 @@
 
 def edge_kernel(
     cut_first, gcm_hbm, owner_hbm, branch_hbm, diffusion_hbm,
-    gcm, to_core_mate, to_chip_mate, to_other, routes, rates, number,
+    gcm, to_core_mate, to_neighbour, to_chip_mate, to_other, routes, rates, number,
     owner, branch, diffusion, arrival,
 ):
     del cut_first
@@ -92,7 +92,9 @@
         number[f * LEV : (f + 1) * LEV, :] = jnp.transpose(spread)
 
     loads[3].wait()
-    to_core_mate[...] = rows_of(gcm, 1 - lax.rem(lax.axis_index("blk"), 2))
+    core = lax.rem(lax.axis_index("blk"), 2)
+    to_core_mate[...] = rows_of(gcm, 1 - core)
+    to_neighbour[...] = rows_of(gcm, core)
     even = lax.rem(lax.axis_index("sub"), 2) == 0
     rows = jnp.concatenate([rows_of(gcm, 0), rows_of(gcm, 1)], axis=0)
     for part in range(GCM_ROWS // LANES):
@@ -143,7 +145,7 @@
 
 
 def prepare_kernel(
-    partial, number, core_mate, other, chip_mate, neighbour, across, routes, rates,
+    partial, number, neighbour, core_mate, other, chip_mate, across, routes, rates,
     advanced, outgoing,
 ):
     lane = lax.broadcasted_iota(jnp.int32, (FIELDS * LEV, LANES), 1)
@@ -155,9 +157,9 @@
         return column[: FIELDS * LEV], column[FIELDS * LEV :]
 
     core = lax.rem(lax.axis_index("blk"), 2)
+    border = lax.rem(lax.axis_index("blk"), PLANE) == PLANE - 1
     inside = core_mate[...]
-    border = lax.rem(lax.axis_index("blk"), PLANE) == PLANE - 1
-    outside = jnp.where(border, across[: FIELDS * LEV, :], rows_of(neighbour, 1 - core))
+    outside = jnp.where(border, across[: FIELDS * LEV, :], neighbour[...])
     vertical = [
         jnp.where(core == 0, outside, inside),
         jnp.where(core == 0, inside, outside),
@@ -396,15 +398,13 @@
         compiler_params=pltpu.CompilerParams(vmem_limit_bytes=4 * MIB),
         name="cut",
     )(in_hbm(gcm))
-    down = [(i, (i - 1) % n_blk) for i in range(0, n_blk, PLANE)]
-    across = lax.ppermute(row, "blk", down)
-    near = [pair for pair in pairs(n_blk, 1) if pair not in down]
-    neighbour = lax.ppermute(gcm, "blk", near)
-    gcm_here, to_core_mate, to_chip_mate, to_other, routes, rates, number = pl.pallas_call(
+    across = lax.ppermute(row, "blk", pairs(n_blk, 1))
+    gcm_here, to_core_mate, to_neighbour, to_chip_mate, to_other, routes, rates, number = pl.pallas_call(
         edge_kernel,
         in_specs=[pl.BlockSpec(memory_space=pl.ANY)] + [hbm] * 4,
         out_shape=(
             f32(GCM_ROWS, LANES),
+            f32(FIELDS * LEV, LANES),
             f32(FIELDS * LEV, LANES),
             f32(SUB, LANES),
             f32(SUB, LANES),
@@ -421,9 +421,10 @@
         compiler_params=pltpu.CompilerParams(vmem_limit_bytes=4 * MIB),
         name="edges",
     )(row, *map(in_hbm, (gcm, owner, branch, diffusion)))
+    neighbour = lax.ppermute(to_neighbour, "blk", pairs(n_blk, 1))
+    core_mate = lax.ppermute(to_core_mate, "blk", pairs(n_blk, 0))
     chip_mate = lax.ppermute(to_chip_mate, "sub", pairs(n_sub, 0))
     other = lax.ppermute(to_other, "sub", pairs(n_sub, 1))
-    core_mate = lax.ppermute(to_core_mate, "blk", pairs(n_blk, 0))
     cells = 2 * LEV * NXC * COLS
     state, sums, partial = pl.pallas_call(
         early_kernel,
@@ -446,7 +447,7 @@
         out_shape=(f32(4 * 2 * LEV, LANES), f32(COLS, LANES)),
         compiler_params=pltpu.CompilerParams(vmem_limit_bytes=8 * MIB),
         name="prepare",
-    )(partial, number, core_mate, other, chip_mate, neighbour, across, routes, rates)
+    )(partial, number, neighbour, core_mate, other, chip_mate, across, routes, rates)
 
     incoming = transfer(outgoing)
     profiles, gcm_next = pl.pallas_call(

time: 56.9 us -> 56.5 us (level)
  starting transfers between devices: 13.2 us -> 10.2 us
  blocking collectives: 29.7 us -> 32.1 us
    all_to_all x2, blocking collectives: 29.7 us -> 32.1 us  [transfer(): lax.all_to_all(rows.reshape(DEVICES, 2, LANES), ('blk', 'sub'), split_axi...]
    ppermute x2, starting transfers between devices: 5.26 us -> 2.86 us  [the longest x1 2.77 us: body(): across = lax.ppermute(row, 'blk', pairs(n_blk, 1))]
    ppermute x1, starting transfers between devices: 5.46 us -> 4.82 us  [body(): core_mate = lax.ppermute(to_core_mate, 'blk', pairs(n_blk, 0))]
where the time goes in v6:
time: 56.5 us; the launch traced here: 56.3 us
  blocking collectives  32.1 us (57%)
  Pallas kernels  12.7 us (22%)
  starting transfers between devices  10.2 us (18%)
  between operations  0.69 us (1%)
  waiting for transfers between devices  0.67 us (1%)
    all_to_all x2, blocking collectives, transfer(): lax.all_to_all(rows.reshape(DEVICES, 2, LANES), ('blk', 'sub'), split_axi...  32.1 us
    pallas_call x1, Pallas kernels, body(): pl.pallas_call(cloud_kernel, out_specs=(whole((COLS, LANES)), hbm), out_s...  7.82 us
    ppermute x1, starting transfers between devices, body(): core_mate = lax.ppermute(to_core_mate, 'blk', pairs(n_blk, 0))  4.82 us
    ppermute x1, starting transfers between devices, body(): across = lax.ppermute(row, 'blk', pairs(n_blk, 1))  2.77 us
    ppermute x1, starting transfers between devices, body(): other = lax.ppermute(to_other, 'sub', pairs(n_sub, 1))  2.49 us
    pallas_call x1, Pallas kernels, body(): pl.pallas_call(early_kernel, in_specs=[hbm, whole((GCM_ROWS, LANES)), who...  2.07 us
    pallas_call x1, Pallas kernels, body(): pl.pallas_call(edge_kernel, in_specs=[pl.BlockSpec(memory_space=pl.ANY)]...  1.14 us
  transfers between devices with their start and end apart: 5, of which 1 were waited for; matrix products, arithmetic and copies ran while one was open for 0% of the time, Pallas kernels for 6%

profile of v6, /device:TPU:1, one launch (start us, length us, event | category | flops | bytes accessed | tf_op | source)
XLA Modules:
  0.0 56.3 jit_solution(7918637003940648145)
XLA Ops:
  0.7 2.8 %collective-permute-start.4 = (f32[200,128]{1,0:T(8,128)S(1)}, f32[200,128]{1,0:T(8,128)S(1)}, u32[]{:S(2)}, u32[]{:S(2)}) collective-permute-start(f32[200,128]{1,0:T(8,128)S(1)} %cut.1.cut_first), channel_id=1, source_target_pairs={{4,8},{12,16},{20,24},{28,32},{36,40},{44,48},{52,56},{60,64},{68,... | collective-permute-start | bytes 307208 | tf_op jit(solution)/shard_map/ppermute | solution.py:401
  3.4 1.1 %edges.1 = (f32[384,128]{1,0:T(8,128)S(1)}, f32[192,128]{1,0:T(8,128)S(1)}, f32[192,128]{1,0:T(8,128)S(1)}, f32[8,128]{1,0:T(8,128)S(1)}, f32[8,128]{1,0:T(8,128...) custom-call(f32[200,128]{1,0:T(8,128)S(1)} %cut.1.cut_first, ...), custom_call_target="tpu_custom_call" | custom-call | tf_op jit(solution)/shard_map/edges/pallas_call | solution.py:402
  4.6 0.1 collective-permute-start
  4.7 4.8 %collective-permute-start.1 = (f32[192,128]{1,0:T(8,128)S(1)}, f32[192,128]{1,0:T(8,128)S(1)}, u32[]{:S(2)}, u32[]{:S(2)}) collective-permute-start(f32[192,128]{1,0:T(8,128)S(1)} %get-tuple-element.23), channel_id=1, source_target_pairs={{0,4},{8,12},{16,20},{24,28},{32,36},{40,44},{48,52},{56,60},{64,6... | collective-permute-start | bytes 294920 | tf_op jit(solution)/shard_map/ppermute | solution.py:425
  9.5 2.5 %collective-permute-start.2 = (f32[8,128]{1,0:T(8,128)S(1)}, f32[8,128]{1,0:T(8,128)S(1)}, u32[]{:S(2)}, u32[]{:S(2)}) collective-permute-start(f32[8,128]{1,0:T(8,128)S(1)} %get-tuple-element.24), channel_id=1, source_target_pairs={{1,2},{3,0},{2,1},{0,3},{5,6},{7,4},{6,5},{4,7},{9,10},{11,8},{10,... | collective-permute-start | bytes 12296 | tf_op jit(solution)/shard_map/ppermute | solution.py:427
  12.0 0.0 collective-permute-start.3
  12.0 2.1 %early.1 = (f32[2,2,2048,128]{3,2,1,0:T(8,128)S(1)}, f32[2,2,256,128]{3,2,1,0:T(8,128)S(1)}, f32[2,192,128]{2,1,0:T(8,128)S(1)}) custom-call(bf16[2,32,64,256]{3,2,1,0:T(8,128)(2,1)} %crm_hbm.1, f32[384,128]{1,0:T(8,128)S(1)} %get-tuple-element.19.gcm, f32[192,128]{1,0:T(8,128)S(1)} %get-tuple-element.20.number), custom_call_target="tpu_custom_call" | custom-call | flops 4194304 | bytes 6291456 | tf_op jit(solution)/shard_map/early/pallas_call | solution.py:429
  14.1 0.0 collective-permute-done.2.other
  14.1 0.7 %collective-permute-done.3.chip_mate = f32[8,128]{1,0:T(8,128)S(1)} collective-permute-done((f32[8,128]{1,0:T(8,128)S(1)}, f32[8,128]{1,0:T(8,128)S(1)}, u32[]{:S(2)}, u32[]{:S(2)}) %collective-permute-start.3) | collective-permute-done | bytes 4128 | tf_op jit(solution)/shard_map/ppermute | solution.py:426
  14.7 0.0 collective-permute-done.neighbour
  14.8 0.0 collective-permute-done.1.core_mate
  14.8 0.0 collective-permute-done.4.across
  14.8 0.7 %prepare.1 = (f32[256,128]{1,0:T(8,128)S(1)}, f32[256,128]{1,0:T(8,128)S(1)}) custom-call(f32[2,192,128]{2,1,0:T(8,128)S(1)} %get-tuple-element.21.partial, f32[192,128]{1,0:T(8,128)S(1)} %get-tuple-element.20.number, f32[192,128]{1,0:T(8,128)S(1)} %collective-permute-done.neighbour, f32[192,128]{1,0:T(8,128)S(1)} %collective-permute-done.1.core_mate, ...), custom_call_target="tpu_custom_call" | custom-call | tf_op jit(solution)/shard_map/prepare/pallas_call | solution.py:445
  15.4 18.1 %all_to_all.10 = f32[128,2,128]{2,1,0:T(2,128)S(1)} all-to-all(f32[128,2,128]{2,1,0:T(2,128)S(1)} %bitcast.9), channel_id=1, replica_groups=mesh['blk'=32,'sub'=4] {'blk','sub'}, dimensions={0} | all-to-all | bytes 262144 | tf_op jit(solution)/shard_map/all_to_all | solution.py:378
  33.5 7.8 %cloud.1 = (f32[256,128]{1,0:T(8,128)S(1)}, f32[384,128]{1,0:T(8,128)}) custom-call(f32[256,128]{1,0:T(8,128)S(1)} %bitcast.7, f32[2,2,2048,128]{3,2,1,0:T(8,128)S(1)} %get-tuple-element.29.start, f32[2,2,256,128]{3,2,1,0:T(8,128)S(1)} %get-tuple-element.30.sums, f32[256,128]{1,0:T(8,128)S(1)} %get-tuple-element.31.advanced), custom_call_target="tpu_custom_call" | custom-call | tf_op jit(solution)/shard_map/cloud/pallas_call | solution.py:453
  41.3 14.0 %all_to_all.11 = f32[128,2,128]{2,1,0:T(2,128)S(1)} all-to-all(f32[128,2,128]{2,1,0:T(2,128)S(1)} %bitcast.10), channel_id=1, replica_groups=mesh['blk'=32,'sub'=4] {'blk','sub'}, dimensions={0} | all-to-all | bytes 262144 | tf_op jit(solution)/shard_map/all_to_all | solution.py:378
  55.4 0.9 %home.1 = (f32[384,128]{1,0:T(8,128)}, f32[128,128]{1,0:T(8,128)}) custom-call(f32[256,128]{1,0:T(8,128)S(1)} %bitcast.8, bf16[2,128,256]{2,1,0:T(8,128)(2,1)S(1)} %get-tuple-element.26.routes, f32[384,128]{1,0:T(8,128)} %get-tuple-element.33.begun), custom_call_target="tpu_custom_call", output_to_operand_aliasing={{0}: (2, {})} | custom-call | tf_op jit(solution)/shard_map/home/pallas_call | solution.py:470
  (1 shorter events, 0.0 us)
Async XLA Ops:
  0.7 14.1 %collective-permute-start.4 = (f32[200,128]{1,0:T(8,128)S(1)}, f32[200,128]{1,0:T(8,128)S(1)}, u32[]{:S(2)}, u32[]{:S(2)}) collective-permute-start(f32[200,128]{1,0:T(8,128)S(1)} %cut.1.cut_first), channel_id=1, source_target_pairs={{4,8},{12,16},{20,24},{28,32},{36,40},{44,48},{52,56},{60,64},{68,... | collective-permute-start | bytes 307208 | tf_op jit(solution)/shard_map/ppermute | solution.py:401
  4.6 10.2 %collective-permute-start = (f32[192,128]{1,0:T(8,128)S(1)}, f32[192,128]{1,0:T(8,128)S(1)}, u32[]{:S(2)}, u32[]{:S(2)}) collective-permute-start(f32[192,128]{1,0:T(8,128)S(1)} %get-tuple-element.22), channel_id=1, source_target_pairs={{4,8},{12,16},{20,24},{28,32},{36,40},{44,48},{52,56},{60,64},{68,... | collective-permute-start | bytes 294920 | tf_op jit(solution)/shard_map/ppermute | solution.py:424
  4.7 10.1 %collective-permute-start.1 = (f32[192,128]{1,0:T(8,128)S(1)}, f32[192,128]{1,0:T(8,128)S(1)}, u32[]{:S(2)}, u32[]{:S(2)}) collective-permute-start(f32[192,128]{1,0:T(8,128)S(1)} %get-tuple-element.23), channel_id=1, source_target_pairs={{0,4},{8,12},{16,20},{24,28},{32,36},{40,44},{48,52},{56,60},{64,6... | collective-permute-start | bytes 294920 | tf_op jit(solution)/shard_map/ppermute | solution.py:425
  9.5 4.6 %collective-permute-start.2 = (f32[8,128]{1,0:T(8,128)S(1)}, f32[8,128]{1,0:T(8,128)S(1)}, u32[]{:S(2)}, u32[]{:S(2)}) collective-permute-start(f32[8,128]{1,0:T(8,128)S(1)} %get-tuple-element.24), channel_id=1, source_target_pairs={{1,2},{3,0},{2,1},{0,3},{5,6},{7,4},{6,5},{4,7},{9,10},{11,8},{10,... | collective-permute-start | bytes 12296 | tf_op jit(solution)/shard_map/ppermute | solution.py:427
  12.0 2.8 %collective-permute-start.3 = (f32[8,128]{1,0:T(8,128)S(1)}, f32[8,128]{1,0:T(8,128)S(1)}, u32[]{:S(2)}, u32[]{:S(2)}) collective-permute-start(f32[8,128]{1,0:T(8,128)S(1)} %get-tuple-element.25), channel_id=1, source_target_pairs={{0,1},{2,3},{1,0},{3,2},{4,5},{6,7},{5,4},{7,6},{8,9},{10,11},{9,8... | collective-permute-start | bytes 12296 | tf_op jit(solution)/shard_map/ppermute | solution.py:426

commit v7 on v5

--- a/solution.py
+++ b/solution.py
@@ -45,23 +45,30 @@
     return ref[pl.ds(y, FIELDS * LEV, stride=2), :]
 
 
-def edge_kernel(
+def load_kernel(
     gcm_hbm, owner_hbm, branch_hbm, diffusion_hbm,
-    gcm, to_core_mate, to_neighbour, to_chip_mate, to_other, routes, rates, number,
-    owner, branch, diffusion, arrival,
+    gcm, to_core_mate, to_neighbour, owner, branch, diffusion, arrival,
 ):
     loads = [
         pltpu.make_async_copy(source, target, arrival.at[n])
         for n, (source, target) in enumerate(
-            [(owner_hbm, owner), (branch_hbm, branch), (diffusion_hbm, diffusion), (gcm_hbm, gcm)]
+            [(gcm_hbm, gcm), (owner_hbm, owner), (branch_hbm, branch), (diffusion_hbm, diffusion)]
         )
     ]
     for copy in loads:
         copy.start()
+    for copy in loads:
+        copy.wait()
+    core = lax.rem(lax.axis_index("blk"), 2)
+    to_core_mate[...] = rows_of(gcm, 1 - core)
+    to_neighbour[...] = rows_of(gcm, core)
+
+
+def edge_kernel(
+    gcm, owner, branch, diffusion, to_chip_mate, to_other, routes, rates, number
+):
     to_chip_mate[...] = jnp.zeros_like(to_chip_mate)
     to_other[...] = jnp.zeros_like(to_other)
-    for copy in loads[:3]:
-        copy.wait()
     device = lax.broadcasted_iota(jnp.int32, (DEVICES, LANES), 0)
     target = jnp.concatenate(
         [(device == owner[y : y + 1, :]).astype(jnp.float32) for y in range(2)], axis=1
@@ -79,10 +86,6 @@
         spread = jnp.broadcast_to(diffusion[f : f + 1, :], (LANES, LEV))
         number[f * LEV : (f + 1) * LEV, :] = jnp.transpose(spread)
 
-    loads[3].wait()
-    core = lax.rem(lax.axis_index("blk"), 2)
-    to_core_mate[...] = rows_of(gcm, 1 - core)
-    to_neighbour[...] = rows_of(gcm, core)
     even = lax.rem(lax.axis_index("sub"), 2) == 0
     rows = jnp.concatenate([rows_of(gcm, 0), rows_of(gcm, 1)], axis=0)
     for part in range(GCM_ROWS // LANES):
@@ -334,7 +337,7 @@
     leaving.wait()
 
 
-def home_kernel(returned, routes, begun, gcm_next, stats):
+def home_kernel(returned, routes, begun, gcm_next, stats, rows, departure):
     del begun
     home = None
     for slot in range(2):
@@ -343,8 +346,17 @@
         home = term if home is None else home + term
     for y in range(2):
         part = home[:, y * LANES : (y + 1) * LANES]
-        gcm_next[pl.ds(y, 2 * LEV, stride=2), :] = part[: 2 * LEV]
-        stats[pl.ds(y, 2 * LEV, stride=2), :] = part[2 * LEV :]
+        rows[pl.ds(y, 4 * LEV, stride=2), :] = part
+    copies = [
+        pltpu.make_async_copy(
+            rows.at[pl.ds(0, 4 * LEV)], gcm_next.at[pl.ds(0, 4 * LEV)], departure.at[0]
+        ),
+        pltpu.make_async_copy(rows.at[pl.ds(4 * LEV, 4 * LEV)], stats, departure.at[1]),
+    ]
+    for copy in copies:
+        copy.start()
+    for copy in copies:
+        copy.wait()
 
 
 def whole(shape):
@@ -375,30 +387,35 @@
 
     n_blk, n_sub = lax.axis_size("blk"), lax.axis_size("sub")
     hbm = pl.BlockSpec(memory_space=pltpu.HBM)
-    gcm_here, to_core_mate, to_neighbour, to_chip_mate, to_other, routes, rates, number = pl.pallas_call(
-        edge_kernel,
+    gcm_here, to_core_mate, to_neighbour, owner_here, branch_here, diffusion_here = pl.pallas_call(
+        load_kernel,
         in_specs=[hbm] * 4,
         out_shape=(
             f32(GCM_ROWS, LANES),
             f32(FIELDS * LEV, LANES),
             f32(FIELDS * LEV, LANES),
+            jax.ShapeDtypeStruct(owner.shape, owner.dtype),
+            jax.ShapeDtypeStruct(branch.shape, branch.dtype),
+            f32(*diffusion.shape),
+        ),
+        scratch_shapes=[pltpu.SemaphoreType.DMA((4,))],
+        compiler_params=pltpu.CompilerParams(vmem_limit_bytes=4 * MIB),
+        name="load",
+    )(*map(in_hbm, (gcm, owner, branch, diffusion)))
+    neighbour = lax.ppermute(to_neighbour, "blk", pairs(n_blk, 1))
+    core_mate = lax.ppermute(to_core_mate, "blk", pairs(n_blk, 0))
+    to_chip_mate, to_other, routes, rates, number = pl.pallas_call(
+        edge_kernel,
+        out_shape=(
             f32(SUB, LANES),
             f32(SUB, LANES),
             jax.ShapeDtypeStruct((2, DEVICES, COLS), jnp.bfloat16),
             f32(2, LANES),
             f32(FIELDS * LEV, LANES),
         ),
-        scratch_shapes=[
-            pltpu.VMEM((2, LANES), jnp.int32),
-            pltpu.VMEM((2, LANES), jnp.int32),
-            pltpu.VMEM((FIELDS, LEV), jnp.float32),
-            pltpu.SemaphoreType.DMA((4,)),
-        ],
         compiler_params=pltpu.CompilerParams(vmem_limit_bytes=4 * MIB),
         name="edges",
-    )(*map(in_hbm, (gcm, owner, branch, diffusion)))
-    neighbour = lax.ppermute(to_neighbour, "blk", pairs(n_blk, 1))
-    core_mate = lax.ppermute(to_core_mate, "blk", pairs(n_blk, 0))
+    )(gcm_here, owner_here, branch_here, diffusion_here)
     chip_mate = lax.ppermute(to_chip_mate, "sub", pairs(n_sub, 0))
     other = lax.ppermute(to_other, "sub", pairs(n_sub, 1))
     cells = 2 * LEV * NXC * COLS
@@ -445,14 +462,13 @@
 
     gcm_next, stats = pl.pallas_call(
         home_kernel,
-        grid=(1,),
-        in_specs=[
-            whole((COLS, LANES)),
-            whole((2, DEVICES, COLS)),
-            pl.BlockSpec(memory_space=pl.ANY),
+        in_specs=[whole((COLS, LANES)), whole((2, DEVICES, COLS)), hbm],
+        out_specs=(hbm, hbm),
+        out_shape=(f32(GCM_ROWS, LANES), f32(4 * LEV, LANES)),
+        scratch_shapes=[
+            pltpu.VMEM((8 * LEV, LANES), jnp.float32),
+            pltpu.SemaphoreType.DMA((2,)),
         ],
-        out_specs=(whole((4 * LEV, LANES)), whole((4 * LEV, LANES))),
-        out_shape=(f32(GCM_ROWS, LANES), f32(4 * LEV, LANES)),
         input_output_aliases={2: 0},
         compiler_params=pltpu.CompilerParams(vmem_limit_bytes=8 * MIB),
         name="home",

time: 53.7 us -> 53.6 us (level)
    pallas_call x2 -> x3, Pallas kernels: 2.09 us -> 2.18 us  [the longest x1 0.98 us: body(): pl.pallas_call(load_kernel, in_specs=[hbm] * 4, out_shape=(f32(GCM_ROWS,...]
where the time goes in v7:
time: 53.6 us; the launch traced here: 53.4 us
  blocking collectives  29.5 us (55%)
  Pallas kernels  12.7 us (24%)
  starting transfers between devices  10.1 us (19%)
  between operations  0.68 us (1%)
    all_to_all x2, blocking collectives, transfer(): lax.all_to_all(rows.reshape(DEVICES, 2, LANES), ('blk', 'sub'), split_axi...  29.5 us
    pallas_call x1, Pallas kernels, body(): pl.pallas_call(cloud_kernel, out_specs=(whole((COLS, LANES)), hbm), out_s...  7.82 us
    ppermute x1, starting transfers between devices, body(): core_mate = lax.ppermute(to_core_mate, 'blk', pairs(n_blk, 0))  4.75 us
    ppermute x1, starting transfers between devices, body(): neighbour = lax.ppermute(to_neighbour, 'blk', pairs(n_blk, 1))  2.77 us
    ppermute x1, starting transfers between devices, body(): other = lax.ppermute(to_other, 'sub', pairs(n_sub, 1))  2.56 us
    pallas_call x1, Pallas kernels, body(): pl.pallas_call(early_kernel, in_specs=[hbm, whole((GCM_ROWS, LANES)), who...  2.07 us
  transfers between devices with their start and end apart: 4, of which 1 were waited for; matrix products, arithmetic and copies ran while one was open for 0% of the time, Pallas kernels for 4%

profile of v7, /device:TPU:1, one launch (start us, length us, event | category | flops | bytes accessed | tf_op | source)
XLA Modules:
  0.0 53.4 jit_solution(3729407068388528124)
XLA Ops:
  0.6 1.0 %load.1 = (f32[384,128]{1,0:T(8,128)S(1)}, f32[192,128]{1,0:T(8,128)S(1)}, f32[192,128]{1,0:T(8,128)S(1)}, s32[2,128]{1,0:T(2,128)S(1)}, s32[2,128]{1,0:T(2,128)S(1)}, /*index=5*/f32[6,32]{1,0:T(8,128)S(1)}) custom-call(f32[384,128]{1,0:T(8,128)} %bitcast.12, s32[2,128]{1,0:T(2,128)} %owner_hbm.1, s32[2,128]{1,0:T(2,128)} %branch_hbm.1, f32[6,32]{1,0:T(8,128)} %diffusion_hbm.1), custom_call_target="tpu_custom_call" | custom-call | tf_op jit(solution)/shard_map/load/pallas_call | solution.py:390
  1.6 2.8 %collective-permute-start = (f32[192,128]{1,0:T(8,128)S(1)}, f32[192,128]{1,0:T(8,128)S(1)}, u32[]{:S(2)}, u32[]{:S(2)}) collective-permute-start(f32[192,128]{1,0:T(8,128)S(1)} %get-tuple-element.28), channel_id=1, source_target_pairs={{4,8},{12,16},{20,24},{28,32},{36,40},{44,48},{52,56},{60,64},{68,... | collective-permute-start | bytes 294920 | tf_op jit(solution)/shard_map/ppermute | solution.py:405
  4.4 4.7 %collective-permute-start.1 = (f32[192,128]{1,0:T(8,128)S(1)}, f32[192,128]{1,0:T(8,128)S(1)}, u32[]{:S(2)}, u32[]{:S(2)}) collective-permute-start(f32[192,128]{1,0:T(8,128)S(1)} %get-tuple-element.29), channel_id=1, source_target_pairs={{0,4},{8,12},{16,20},{24,28},{32,36},{40,44},{48,52},{56,60},{64,6... | collective-permute-start | bytes 294920 | tf_op jit(solution)/shard_map/ppermute | solution.py:406
  9.1 0.2 edges.1
  9.4 2.6 %collective-permute-start.2 = (f32[8,128]{1,0:T(8,128)S(1)}, f32[8,128]{1,0:T(8,128)S(1)}, u32[]{:S(2)}, u32[]{:S(2)}) collective-permute-start(f32[8,128]{1,0:T(8,128)S(1)} %get-tuple-element.30), channel_id=1, source_target_pairs={{1,2},{3,0},{2,1},{0,3},{5,6},{7,4},{6,5},{4,7},{9,10},{11,8},{10,... | collective-permute-start | bytes 12296 | tf_op jit(solution)/shard_map/ppermute | solution.py:420
  11.9 0.0 collective-permute-start.3
  11.9 2.1 %early.1 = (f32[2,2,2048,128]{3,2,1,0:T(8,128)S(1)}, f32[2,2,256,128]{3,2,1,0:T(8,128)S(1)}, f32[2,192,128]{2,1,0:T(8,128)S(1)}) custom-call(bf16[2,32,64,256]{3,2,1,0:T(8,128)(2,1)} %crm_hbm.1, f32[384,128]{1,0:T(8,128)S(1)} %get-tuple-element.22.gcm, f32[192,128]{1,0:T(8,128)S(1)} %get-tuple-element.26.number), custom_call_target="tpu_custom_call" | custom-call | flops 4194304 | bytes 6291456 | tf_op jit(solution)/shard_map/early/pallas_call | solution.py:422
  14.0 0.0 collective-permute-done.2.other
  14.0 0.4 collective-permute-done.3.chip_mate
  14.4 0.0 collective-permute-done.neighbour
  14.4 0.0 collective-permute-done.1.core_mate
  14.4 0.7 %prepare.1 = (f32[256,128]{1,0:T(8,128)S(1)}, f32[256,128]{1,0:T(8,128)S(1)}) custom-call(f32[2,192,128]{2,1,0:T(8,128)S(1)} %get-tuple-element.27.partial, f32[192,128]{1,0:T(8,128)S(1)} %get-tuple-element.26.number, f32[192,128]{1,0:T(8,128)S(1)} %collective-permute-done.neighbour, f32[192,128]{1,0:T(8,128)S(1)} %collective-permute-done.1.core_mate, ...), custom_call_target="tpu_custom_call" | custom-call | tf_op jit(solution)/shard_map/prepare/pallas_call | solution.py:438
  15.0 15.5 %all_to_all.10 = f32[128,2,128]{2,1,0:T(2,128)S(1)} all-to-all(f32[128,2,128]{2,1,0:T(2,128)S(1)} %bitcast.9), channel_id=1, replica_groups=mesh['blk'=32,'sub'=4] {'blk','sub'}, dimensions={0} | all-to-all | bytes 262144 | tf_op jit(solution)/shard_map/all_to_all | solution.py:375
  30.6 7.8 %cloud.1 = (f32[256,128]{1,0:T(8,128)S(1)}, f32[384,128]{1,0:T(8,128)}) custom-call(f32[256,128]{1,0:T(8,128)S(1)} %bitcast.7, f32[2,2,2048,128]{3,2,1,0:T(8,128)S(1)} %get-tuple-element.35.start, f32[2,2,256,128]{3,2,1,0:T(8,128)S(1)} %get-tuple-element.36.sums, f32[256,128]{1,0:T(8,128)S(1)} %get-tuple-element.37.advanced), custom_call_target="tpu_custom_call" | custom-call | tf_op jit(solution)/shard_map/cloud/pallas_call | solution.py:446
  38.4 14.0 %all_to_all.11 = f32[128,2,128]{2,1,0:T(2,128)S(1)} all-to-all(f32[128,2,128]{2,1,0:T(2,128)S(1)} %bitcast.10), channel_id=1, replica_groups=mesh['blk'=32,'sub'=4] {'blk','sub'}, dimensions={0} | all-to-all | bytes 262144 | tf_op jit(solution)/shard_map/all_to_all | solution.py:375
  52.4 1.0 %home.1 = (f32[384,128]{1,0:T(8,128)}, f32[128,128]{1,0:T(8,128)}) custom-call(f32[256,128]{1,0:T(8,128)S(1)} %bitcast.8, bf16[2,128,256]{2,1,0:T(8,128)(2,1)S(1)} %get-tuple-element.32.routes, f32[384,128]{1,0:T(8,128)} %get-tuple-element.39.begun), custom_call_target="tpu_custom_call", output_to_operand_aliasing={{0}: (2, {})} | custom-call | tf_op jit(solution)/shard_map/home/pallas_call | solution.py:463
Async XLA Ops:
  1.6 12.8 %collective-permute-start = (f32[192,128]{1,0:T(8,128)S(1)}, f32[192,128]{1,0:T(8,128)S(1)}, u32[]{:S(2)}, u32[]{:S(2)}) collective-permute-start(f32[192,128]{1,0:T(8,128)S(1)} %get-tuple-element.28), channel_id=1, source_target_pairs={{4,8},{12,16},{20,24},{28,32},{36,40},{44,48},{52,56},{60,64},{68,... | collective-permute-start | bytes 294920 | tf_op jit(solution)/shard_map/ppermute | solution.py:405
  4.4 10.0 %collective-permute-start.1 = (f32[192,128]{1,0:T(8,128)S(1)}, f32[192,128]{1,0:T(8,128)S(1)}, u32[]{:S(2)}, u32[]{:S(2)}) collective-permute-start(f32[192,128]{1,0:T(8,128)S(1)} %get-tuple-element.29), channel_id=1, source_target_pairs={{0,4},{8,12},{16,20},{24,28},{32,36},{40,44},{48,52},{56,60},{64,6... | collective-permute-start | bytes 294920 | tf_op jit(solution)/shard_map/ppermute | solution.py:406
  9.4 4.6 %collective-permute-start.2 = (f32[8,128]{1,0:T(8,128)S(1)}, f32[8,128]{1,0:T(8,128)S(1)}, u32[]{:S(2)}, u32[]{:S(2)}) collective-permute-start(f32[8,128]{1,0:T(8,128)S(1)} %get-tuple-element.30), channel_id=1, source_target_pairs={{1,2},{3,0},{2,1},{0,3},{5,6},{7,4},{6,5},{4,7},{9,10},{11,8},{10,... | collective-permute-start | bytes 12296 | tf_op jit(solution)/shard_map/ppermute | solution.py:420
  11.9 2.5 %collective-permute-start.3 = (f32[8,128]{1,0:T(8,128)S(1)}, f32[8,128]{1,0:T(8,128)S(1)}, u32[]{:S(2)}, u32[]{:S(2)}) collective-permute-start(f32[8,128]{1,0:T(8,128)S(1)} %get-tuple-element.31), channel_id=1, source_target_pairs={{0,1},{2,3},{1,0},{3,2},{4,5},{6,7},{5,4},{7,6},{8,9},{10,11},{9,8... | collective-permute-start | bytes 12296 | tf_op jit(solution)/shard_map/ppermute | solution.py:419

commit v8 on v5

--- a/solution.py
+++ b/solution.py
@@ -82,7 +82,8 @@
     loads[3].wait()
     core = lax.rem(lax.axis_index("blk"), 2)
     to_core_mate[...] = rows_of(gcm, 1 - core)
-    to_neighbour[...] = rows_of(gcm, core)
+    to_neighbour[: FIELDS * LEV, :] = rows_of(gcm, core)
+    to_neighbour[FIELDS * LEV :, :] = jnp.zeros((SUB, LANES), jnp.float32)
     even = lax.rem(lax.axis_index("sub"), 2) == 0
     rows = jnp.concatenate([rows_of(gcm, 0), rows_of(gcm, 1)], axis=0)
     for part in range(GCM_ROWS // LANES):
@@ -132,43 +133,60 @@
             lax.fori_loop(0, CRM_CHUNK, level, 0, unroll=4)
 
 
-def prepare_kernel(
-    partial, number, neighbour, core_mate, other, chip_mate, routes, rates, advanced, outgoing
+def column_values(state, rate):
+    level = lax.broadcasted_iota(jnp.int32, (LEV, LANES), 0)
+    field = [state[f * LEV : (f + 1) * LEV] for f in range(FIELDS)]
+    warm = ALPHA * (0.25 * field[0] + 0.2 * field[4])
+    wet = BETA * (0.25 * field[1] + 0.2 * field[5])
+    drift = 0.45 * jnp.tanh(field[2])
+    tilt = jnp.tanh(field[3])
+    rise = 0.15 * (tilt + pltpu.roll(tilt, LEV - 1, axis=0))
+    rise = jnp.where(level == LEV - 1, rate, rise)
+    return jnp.concatenate([warm, wet, drift, rise], axis=0)
+
+
+def placed(values, routes, slot, y):
+    route = routes[slot, :, pl.ds(pl.multiple_of(y * LANES, LANES), LANES)]
+    return select_dot(values, route, ((1,), (1,)), False)
+
+
+def inner_kernel(
+    partial, number, core_mate, other, chip_mate, routes, rates, outer, done, advanced
 ):
     lane = lax.broadcasted_iota(jnp.int32, (FIELDS * LEV, LANES), 1)
-    level = lax.broadcasted_iota(jnp.int32, (LEV, LANES), 0)
+    core = lax.rem(lax.axis_index("blk"), 2)
 
     def columns(ref):
         turned = jnp.transpose(ref)
         column = jnp.concatenate([turned[:, n : n + 1] for n in range(GCM_ROWS // LANES)], axis=0)
         return column[: FIELDS * LEV], column[FIELDS * LEV :]
 
-    core = lax.rem(lax.axis_index("blk"), 2)
-    inside, outside = core_mate[...], neighbour[...]
-    vertical = [
-        jnp.where(core == 0, outside, inside),
-        jnp.where(core == 0, inside, outside),
-    ]
     even = lax.rem(lax.axis_index("sub"), 2) == 0
     near, far = chip_mate[...], other[...]
     west, east = columns(jnp.where(even, far, near)), columns(jnp.where(even, near, far))
-    values = []
+    rows = []
     for y in range(2):
         side = jnp.where(lane == 0, west[y], jnp.where(lane == LANES - 1, east[y], 0.0))
-        state = partial[y] + number[...] * (vertical[y] + side)
-        advanced[pl.ds(y, 4 * LEV, stride=2), :] = state[2 * LEV :]
-        field = [state[f * LEV : (f + 1) * LEV] for f in range(FIELDS)]
-        warm = ALPHA * (0.25 * field[0] + 0.2 * field[4])
-        wet = BETA * (0.25 * field[1] + 0.2 * field[5])
-        drift = 0.45 * jnp.tanh(field[2])
-        tilt = jnp.tanh(field[3])
-        rise = 0.15 * (tilt + pltpu.roll(tilt, LEV - 1, axis=0))
-        rise = jnp.where(level == LEV - 1, rates[y : y + 1, :], rise)
-        values.append(jnp.concatenate([warm, wet, drift, rise], axis=0))
-    values = jnp.concatenate(values, axis=1)
+        rows.append(partial[y] + number[...] * side)
+    outer[...] = jnp.where(core == 0, rows[0], rows[1])
+    state = jnp.where(core == 0, rows[1], rows[0]) + number[...] * core_mate[...]
+    advanced[...] = state[2 * LEV :]
+    values = column_values(state, rates[pl.ds(1 - core, 1), :])
     for slot in range(2):
-        outgoing[pl.ds(slot, DEVICES, stride=2), :] = select_dot(
-            values, routes[slot], ((1,), (1,)), False
+        done[slot] = placed(values, routes, slot, 1 - core)
+
+
+def outer_kernel(
+    outer, number, neighbour, routes, rates, done, inner_advanced, advanced, outgoing
+):
+    core = lax.rem(lax.axis_index("blk"), 2)
+    state = outer[...] + number[...] * neighbour[: FIELDS * LEV, :]
+    advanced[pl.ds(core, 4 * LEV, stride=2), :] = state[2 * LEV :]
+    advanced[pl.ds(1 - core, 4 * LEV, stride=2), :] = inner_advanced[...]
+    values = column_values(state, rates[pl.ds(core, 1), :])
+    for slot in range(2):
+        outgoing[pl.ds(slot, DEVICES, stride=2), :] = done[slot] + placed(
+            values, routes, slot, core
         )
 
 
@@ -381,7 +399,7 @@
         out_shape=(
             f32(GCM_ROWS, LANES),
             f32(FIELDS * LEV, LANES),
-            f32(FIELDS * LEV, LANES),
+            f32(FIELDS * LEV + SUB, LANES),
             f32(SUB, LANES),
             f32(SUB, LANES),
             jax.ShapeDtypeStruct((2, DEVICES, COLS), jnp.bfloat16),
@@ -418,12 +436,22 @@
         cost_estimate=pl.CostEstimate(flops=4 * cells, bytes_accessed=6 * cells, transcendentals=0),
         name="early",
     )(in_hbm(crm_state), gcm_here, number)
+    outer, done, inner_advanced = pl.pallas_call(
+        inner_kernel,
+        out_shape=(
+            f32(FIELDS * LEV, LANES),
+            f32(2, DEVICES, LANES),
+            f32(4 * LEV, LANES),
+        ),
+        compiler_params=pltpu.CompilerParams(vmem_limit_bytes=8 * MIB),
+        name="inner",
+    )(partial, number, core_mate, other, chip_mate, routes, rates)
     advanced, outgoing = pl.pallas_call(
-        prepare_kernel,
+        outer_kernel,
         out_shape=(f32(4 * 2 * LEV, LANES), f32(COLS, LANES)),
         compiler_params=pltpu.CompilerParams(vmem_limit_bytes=8 * MIB),
-        name="prepare",
-    )(partial, number, neighbour, core_mate, other, chip_mate, routes, rates)
+        name="outer",
+    )(outer, number, neighbour, routes, rates, done, inner_advanced)
 
     incoming = transfer(outgoing)
     profiles, gcm_next = pl.pallas_call(

time: 53.7 us -> 53.4 us (level)
    all_to_all x2, blocking collectives: 29.8 us -> 29.3 us  [transfer(): lax.all_to_all(rows.reshape(DEVICES, 2, LANES), ('blk', 'sub'), split_axi...]
  transfers between devices with their start and end apart: 4 -> 4, of which waited for: 1 -> 1; matrix products, arithmetic and copies ran while one was open for 0% -> 0% of each run, Pallas kernels for 4% -> 5%
where the time goes in v8:
time: 53.4 us; the launch traced here: 53.2 us
  blocking collectives  29.3 us (55%)
  Pallas kernels  12.9 us (24%)
  starting transfers between devices  9.99 us (19%)
  between operations  0.69 us (1%)
    all_to_all x2, blocking collectives, transfer(): lax.all_to_all(rows.reshape(DEVICES, 2, LANES), ('blk', 'sub'), split_axi...  29.3 us
    pallas_call x1, Pallas kernels, body(): pl.pallas_call(cloud_kernel, out_specs=(whole((COLS, LANES)), hbm), out_s...  7.82 us
    ppermute x1, starting transfers between devices, body(): core_mate = lax.ppermute(to_core_mate, 'blk', pairs(n_blk, 0))  4.75 us
    ppermute x1, starting transfers between devices, body(): neighbour = lax.ppermute(to_neighbour, 'blk', pairs(n_blk, 1))  2.77 us
    ppermute x1, starting transfers between devices, body(): other = lax.ppermute(to_other, 'sub', pairs(n_sub, 1))  2.48 us
    pallas_call x1, Pallas kernels, body(): pl.pallas_call(early_kernel, in_specs=[hbm, whole((GCM_ROWS, LANES)), who...  2.07 us
    pallas_call x1, Pallas kernels, body(): pl.pallas_call(edge_kernel, in_specs=[hbm] * 4, out_shape=(f32(GCM_ROWS,...  1.15 us
  transfers between devices with their start and end apart: 4, of which 1 were waited for; matrix products, arithmetic and copies ran while one was open for 0% of the time, Pallas kernels for 5%

profile of v8, /device:TPU:1, one launch (start us, length us, event | category | flops | bytes accessed | tf_op | source)
XLA Modules:
  0.0 53.2 jit_solution(14691104000761882609)
XLA Ops:
  0.6 1.1 %edges.1 = (f32[384,128]{1,0:T(8,128)S(1)}, f32[192,128]{1,0:T(8,128)S(1)}, f32[200,128]{1,0:T(8,128)S(1)}, f32[8,128]{1,0:T(8,128)S(1)}, f32[8,128]{1,0:T(8,128...) custom-call(f32[384,128]{1,0:T(8,128)} %bitcast.12, s32[2,128]{1,0:T(2,128)} %owner_hbm.1, ...), custom_call_target="tpu_custom_call" | custom-call | tf_op jit(solution)/shard_map/edges/pallas_call | solution.py:396
  1.8 2.8 %collective-permute-start.3 = (f32[200,128]{1,0:T(8,128)S(1)}, f32[200,128]{1,0:T(8,128)S(1)}, u32[]{:S(2)}, u32[]{:S(2)}) collective-permute-start(f32[200,128]{1,0:T(8,128)S(1)} %get-tuple-element.31), channel_id=1, source_target_pairs={{4,8},{12,16},{20,24},{28,32},{36,40},{44,48},{52,56},{60,64},{68,... | collective-permute-start | bytes 307208 | tf_op jit(solution)/shard_map/ppermute | solution.py:418
  4.6 4.7 %collective-permute-start = (f32[192,128]{1,0:T(8,128)S(1)}, f32[192,128]{1,0:T(8,128)S(1)}, u32[]{:S(2)}, u32[]{:S(2)}) collective-permute-start(f32[192,128]{1,0:T(8,128)S(1)} %get-tuple-element.25), channel_id=1, source_target_pairs={{0,4},{8,12},{16,20},{24,28},{32,36},{40,44},{48,52},{56,60},{64,6... | collective-permute-start | bytes 294920 | tf_op jit(solution)/shard_map/ppermute | solution.py:419
  9.3 2.5 %collective-permute-start.1 = (f32[8,128]{1,0:T(8,128)S(1)}, f32[8,128]{1,0:T(8,128)S(1)}, u32[]{:S(2)}, u32[]{:S(2)}) collective-permute-start(f32[8,128]{1,0:T(8,128)S(1)} %get-tuple-element.26), channel_id=1, source_target_pairs={{1,2},{3,0},{2,1},{0,3},{5,6},{7,4},{6,5},{4,7},{9,10},{11,8},{10,... | collective-permute-start | bytes 12296 | tf_op jit(solution)/shard_map/ppermute | solution.py:421
  11.8 0.0 collective-permute-start.2
  11.8 2.1 %early.1 = (f32[2,2,2048,128]{3,2,1,0:T(8,128)S(1)}, f32[2,2,256,128]{3,2,1,0:T(8,128)S(1)}, f32[2,192,128]{2,1,0:T(8,128)S(1)}) custom-call(bf16[2,32,64,256]{3,2,1,0:T(8,128)(2,1)} %crm_hbm.1, f32[384,128]{1,0:T(8,128)S(1)} %get-tuple-element.22.gcm, f32[192,128]{1,0:T(8,128)S(1)} %get-tuple-element.23.number), custom_call_target="tpu_custom_call" | custom-call | flops 4194304 | bytes 6291456 | tf_op jit(solution)/shard_map/early/pallas_call | solution.py:423
  13.9 0.0 collective-permute-done.1.other
  13.9 0.4 collective-permute-done.2.chip_mate
  14.2 0.0 collective-permute-done.core_mate
  14.2 0.6 %inner.1 = (f32[192,128]{1,0:T(8,128)S(1)}, f32[2,128,128]{2,1,0:T(8,128)S(1)}, f32[128,128]{1,0:T(8,128)S(1)}) custom-call(f32[2,192,128]{2,1,0:T(8,128)S(1)} %get-tuple-element.24.partial, f32[192,128]{1,0:T(8,128)S(1)} %get-tuple-element.23.number, f32[192,128]{1,0:T(8,128)S(1)} %collective-permute-done.core_mate, ...), custom_call_target="tpu_custom_call" | custom-call | tf_op jit(solution)/shard_map/inner/pallas_call | solution.py:439
  14.9 0.0 collective-permute-done.3.neighbour
  14.9 0.3 outer.1
  15.2 15.2 %all_to_all.10 = f32[128,2,128]{2,1,0:T(2,128)S(1)} all-to-all(f32[128,2,128]{2,1,0:T(2,128)S(1)} %bitcast.9), channel_id=1, replica_groups=mesh['blk'=32,'sub'=4] {'blk','sub'}, dimensions={0} | all-to-all | bytes 262144 | tf_op jit(solution)/shard_map/all_to_all | solution.py:381
  30.4 7.8 %cloud.1 = (f32[256,128]{1,0:T(8,128)S(1)}, f32[384,128]{1,0:T(8,128)}) custom-call(f32[256,128]{1,0:T(8,128)S(1)} %bitcast.7, f32[2,2,2048,128]{3,2,1,0:T(8,128)S(1)} %get-tuple-element.35.start, f32[2,2,256,128]{3,2,1,0:T(8,128)S(1)} %get-tuple-element.36.sums, f32[256,128]{1,0:T(8,128)S(1)} %get-tuple-element.37.advanced), custom_call_target="tpu_custom_call" | custom-call | tf_op jit(solution)/shard_map/cloud/pallas_call | solution.py:457
  38.2 14.0 %all_to_all.11 = f32[128,2,128]{2,1,0:T(2,128)S(1)} all-to-all(f32[128,2,128]{2,1,0:T(2,128)S(1)} %bitcast.10), channel_id=1, replica_groups=mesh['blk'=32,'sub'=4] {'blk','sub'}, dimensions={0} | all-to-all | bytes 262144 | tf_op jit(solution)/shard_map/all_to_all | solution.py:381
  52.2 0.9 %home.1 = (f32[384,128]{1,0:T(8,128)}, f32[128,128]{1,0:T(8,128)}) custom-call(f32[256,128]{1,0:T(8,128)S(1)} %bitcast.8, bf16[2,128,256]{2,1,0:T(8,128)(2,1)S(1)} %get-tuple-element.28.routes, f32[384,128]{1,0:T(8,128)} %get-tuple-element.39.begun), custom_call_target="tpu_custom_call", output_to_operand_aliasing={{0}: (2, {})} | custom-call | tf_op jit(solution)/shard_map/home/pallas_call | solution.py:474
Async XLA Ops:
  1.8 13.1 %collective-permute-start.3 = (f32[200,128]{1,0:T(8,128)S(1)}, f32[200,128]{1,0:T(8,128)S(1)}, u32[]{:S(2)}, u32[]{:S(2)}) collective-permute-start(f32[200,128]{1,0:T(8,128)S(1)} %get-tuple-element.31), channel_id=1, source_target_pairs={{4,8},{12,16},{20,24},{28,32},{36,40},{44,48},{52,56},{60,64},{68,... | collective-permute-start | bytes 307208 | tf_op jit(solution)/shard_map/ppermute | solution.py:418
  4.6 9.7 %collective-permute-start = (f32[192,128]{1,0:T(8,128)S(1)}, f32[192,128]{1,0:T(8,128)S(1)}, u32[]{:S(2)}, u32[]{:S(2)}) collective-permute-start(f32[192,128]{1,0:T(8,128)S(1)} %get-tuple-element.25), channel_id=1, source_target_pairs={{0,4},{8,12},{16,20},{24,28},{32,36},{40,44},{48,52},{56,60},{64,6... | collective-permute-start | bytes 294920 | tf_op jit(solution)/shard_map/ppermute | solution.py:419
  9.3 4.6 %collective-permute-start.1 = (f32[8,128]{1,0:T(8,128)S(1)}, f32[8,128]{1,0:T(8,128)S(1)}, u32[]{:S(2)}, u32[]{:S(2)}) collective-permute-start(f32[8,128]{1,0:T(8,128)S(1)} %get-tuple-element.26), channel_id=1, source_target_pairs={{1,2},{3,0},{2,1},{0,3},{5,6},{7,4},{6,5},{4,7},{9,10},{11,8},{10,... | collective-permute-start | bytes 12296 | tf_op jit(solution)/shard_map/ppermute | solution.py:421
  11.8 2.5 %collective-permute-start.2 = (f32[8,128]{1,0:T(8,128)S(1)}, f32[8,128]{1,0:T(8,128)S(1)}, u32[]{:S(2)}, u32[]{:S(2)}) collective-permute-start(f32[8,128]{1,0:T(8,128)S(1)} %get-tuple-element.27), channel_id=1, source_target_pairs={{0,1},{2,3},{1,0},{3,2},{4,5},{6,7},{5,4},{7,6},{8,9},{10,11},{9,8... | collective-permute-start | bytes 12296 | tf_op jit(solution)/shard_map/ppermute | solution.py:420

commit v9 on v8

--- a/solution.py
+++ b/solution.py
@@ -45,23 +45,31 @@
     return ref[pl.ds(y, FIELDS * LEV, stride=2), :]
 
 
-def edge_kernel(
+def load_kernel(
     gcm_hbm, owner_hbm, branch_hbm, diffusion_hbm,
-    gcm, to_core_mate, to_neighbour, to_chip_mate, to_other, routes, rates, number,
-    owner, branch, diffusion, arrival,
+    gcm, to_core_mate, to_neighbour, owner, branch, diffusion, arrival,
 ):
     loads = [
         pltpu.make_async_copy(source, target, arrival.at[n])
         for n, (source, target) in enumerate(
-            [(owner_hbm, owner), (branch_hbm, branch), (diffusion_hbm, diffusion), (gcm_hbm, gcm)]
+            [(gcm_hbm, gcm), (owner_hbm, owner), (branch_hbm, branch), (diffusion_hbm, diffusion)]
         )
     ]
     for copy in loads:
         copy.start()
+    for copy in loads:
+        copy.wait()
+    core = lax.rem(lax.axis_index("blk"), 2)
+    to_core_mate[...] = rows_of(gcm, 1 - core)
+    to_neighbour[: FIELDS * LEV, :] = rows_of(gcm, core)
+    to_neighbour[FIELDS * LEV :, :] = jnp.zeros((SUB, LANES), jnp.float32)
+
+
+def edge_kernel(
+    gcm, owner, branch, diffusion, to_chip_mate, to_other, routes, rates, number
+):
     to_chip_mate[...] = jnp.zeros_like(to_chip_mate)
     to_other[...] = jnp.zeros_like(to_other)
-    for copy in loads[:3]:
-        copy.wait()
     device = lax.broadcasted_iota(jnp.int32, (DEVICES, LANES), 0)
     target = jnp.concatenate(
         [(device == owner[y : y + 1, :]).astype(jnp.float32) for y in range(2)], axis=1
@@ -79,11 +87,6 @@
         spread = jnp.broadcast_to(diffusion[f : f + 1, :], (LANES, LEV))
         number[f * LEV : (f + 1) * LEV, :] = jnp.transpose(spread)
 
-    loads[3].wait()
-    core = lax.rem(lax.axis_index("blk"), 2)
-    to_core_mate[...] = rows_of(gcm, 1 - core)
-    to_neighbour[: FIELDS * LEV, :] = rows_of(gcm, core)
-    to_neighbour[FIELDS * LEV :, :] = jnp.zeros((SUB, LANES), jnp.float32)
     even = lax.rem(lax.axis_index("sub"), 2) == 0
     rows = jnp.concatenate([rows_of(gcm, 0), rows_of(gcm, 1)], axis=0)
     for part in range(GCM_ROWS // LANES):
@@ -393,30 +396,35 @@
 
     n_blk, n_sub = lax.axis_size("blk"), lax.axis_size("sub")
     hbm = pl.BlockSpec(memory_space=pltpu.HBM)
-    gcm_here, to_core_mate, to_neighbour, to_chip_mate, to_other, routes, rates, number = pl.pallas_call(
-        edge_kernel,
+    gcm_here, to_core_mate, to_neighbour, owner_here, branch_here, diffusion_here = pl.pallas_call(
+        load_kernel,
         in_specs=[hbm] * 4,
         out_shape=(
             f32(GCM_ROWS, LANES),
             f32(FIELDS * LEV, LANES),
             f32(FIELDS * LEV + SUB, LANES),
+            jax.ShapeDtypeStruct(owner.shape, owner.dtype),
+            jax.ShapeDtypeStruct(branch.shape, branch.dtype),
+            f32(*diffusion.shape),
+        ),
+        scratch_shapes=[pltpu.SemaphoreType.DMA((4,))],
+        compiler_params=pltpu.CompilerParams(vmem_limit_bytes=4 * MIB),
+        name="load",
+    )(*map(in_hbm, (gcm, owner, branch, diffusion)))
+    neighbour = lax.ppermute(to_neighbour, "blk", pairs(n_blk, 1))
+    core_mate = lax.ppermute(to_core_mate, "blk", pairs(n_blk, 0))
+    to_chip_mate, to_other, routes, rates, number = pl.pallas_call(
+        edge_kernel,
+        out_shape=(
             f32(SUB, LANES),
             f32(SUB, LANES),
             jax.ShapeDtypeStruct((2, DEVICES, COLS), jnp.bfloat16),
             f32(2, LANES),
             f32(FIELDS * LEV, LANES),
         ),
-        scratch_shapes=[
-            pltpu.VMEM((2, LANES), jnp.int32),
-            pltpu.VMEM((2, LANES), jnp.int32),
-            pltpu.VMEM((FIELDS, LEV), jnp.float32),
-            pltpu.SemaphoreType.DMA((4,)),
-        ],
         compiler_params=pltpu.CompilerParams(vmem_limit_bytes=4 * MIB),
         name="edges",
-    )(*map(in_hbm, (gcm, owner, branch, diffusion)))
-    neighbour = lax.ppermute(to_neighbour, "blk", pairs(n_blk, 1))
-    core_mate = lax.ppermute(to_core_mate, "blk", pairs(n_blk, 0))
+    )(gcm_here, owner_here, branch_here, diffusion_here)
     chip_mate = lax.ppermute(to_chip_mate, "sub", pairs(n_sub, 0))
     other = lax.ppermute(to_other, "sub", pairs(n_sub, 1))
     cells = 2 * LEV * NXC * COLS

time: 53.4 us -> 53.5 us (level)
    pallas_call x1 -> x2, Pallas kernels: 1.15 us -> 1.21 us  [the longest x1 0.98 us: body(): pl.pallas_call(load_kernel, in_specs=[hbm] * 4, out_shape=(f32(GCM_ROWS,...]
  transfers between devices with their start and end apart: 4 -> 4, of which waited for: 1 -> 1; matrix products, arithmetic and copies ran while one was open for 0% -> 0% of each run, Pallas kernels for 5% -> 6%
where the time goes in v9:
time: 53.5 us; the launch traced here: 53.3 us
  blocking collectives  29.2 us (55%)
  Pallas kernels  12.9 us (24%)
  starting transfers between devices  10.1 us (19%)
  between operations  0.69 us (1%)
    all_to_all x2, blocking collectives, transfer(): lax.all_to_all(rows.reshape(DEVICES, 2, LANES), ('blk', 'sub'), split_axi...  29.2 us
    pallas_call x1, Pallas kernels, body(): pl.pallas_call(cloud_kernel, out_specs=(whole((COLS, LANES)), hbm), out_s...  7.82 us
    ppermute x1, starting transfers between devices, body(): core_mate = lax.ppermute(to_core_mate, 'blk', pairs(n_blk, 0))  4.75 us
    ppermute x1, starting transfers between devices, body(): neighbour = lax.ppermute(to_neighbour, 'blk', pairs(n_blk, 1))  2.77 us
    ppermute x1, starting transfers between devices, body(): other = lax.ppermute(to_other, 'sub', pairs(n_sub, 1))  2.55 us
    pallas_call x1, Pallas kernels, body(): pl.pallas_call(early_kernel, in_specs=[hbm, whole((GCM_ROWS, LANES)), who...  2.07 us
  transfers between devices with their start and end apart: 4, of which 1 were waited for; matrix products, arithmetic and copies ran while one was open for 0% of the time, Pallas kernels for 6%

profile of v9, /device:TPU:1, one launch (start us, length us, event | category | flops | bytes accessed | tf_op | source)
XLA Modules:
  0.0 53.3 jit_solution(16386528766095062711)
XLA Ops:
  0.6 1.0 %load.1 = (f32[384,128]{1,0:T(8,128)S(1)}, f32[192,128]{1,0:T(8,128)S(1)}, f32[200,128]{1,0:T(8,128)S(1)}, s32[2,128]{1,0:T(2,128)S(1)}, s32[2,128]{1,0:T(2,128)S(1)}, /*index=5*/f32[6,32]{1,0:T(8,128)S(1)}) custom-call(f32[384,128]{1,0:T(8,128)} %bitcast.12, s32[2,128]{1,0:T(2,128)} %owner_hbm.1, s32[2,128]{1,0:T(2,128)} %branch_hbm.1, f32[6,32]{1,0:T(8,128)} %diffusion_hbm.1), custom_call_target="tpu_custom_call" | custom-call | tf_op jit(solution)/shard_map/load/pallas_call | solution.py:399
  1.6 2.8 %collective-permute-start.3 = (f32[200,128]{1,0:T(8,128)S(1)}, f32[200,128]{1,0:T(8,128)S(1)}, u32[]{:S(2)}, u32[]{:S(2)}) collective-permute-start(f32[200,128]{1,0:T(8,128)S(1)} %get-tuple-element.37), channel_id=1, source_target_pairs={{4,8},{12,16},{20,24},{28,32},{36,40},{44,48},{52,56},{60,64},{68,... | collective-permute-start | bytes 307208 | tf_op jit(solution)/shard_map/ppermute | solution.py:414
  4.4 4.7 %collective-permute-start = (f32[192,128]{1,0:T(8,128)S(1)}, f32[192,128]{1,0:T(8,128)S(1)}, u32[]{:S(2)}, u32[]{:S(2)}) collective-permute-start(f32[192,128]{1,0:T(8,128)S(1)} %get-tuple-element.31), channel_id=1, source_target_pairs={{0,4},{8,12},{16,20},{24,28},{32,36},{40,44},{48,52},{56,60},{64,6... | collective-permute-start | bytes 294920 | tf_op jit(solution)/shard_map/ppermute | solution.py:415
  9.1 0.2 edges.1
  9.4 2.6 %collective-permute-start.1 = (f32[8,128]{1,0:T(8,128)S(1)}, f32[8,128]{1,0:T(8,128)S(1)}, u32[]{:S(2)}, u32[]{:S(2)}) collective-permute-start(f32[8,128]{1,0:T(8,128)S(1)} %get-tuple-element.32), channel_id=1, source_target_pairs={{1,2},{3,0},{2,1},{0,3},{5,6},{7,4},{6,5},{4,7},{9,10},{11,8},{10,... | collective-permute-start | bytes 12296 | tf_op jit(solution)/shard_map/ppermute | solution.py:429
  11.9 0.0 collective-permute-start.2
  11.9 2.1 %early.1 = (f32[2,2,2048,128]{3,2,1,0:T(8,128)S(1)}, f32[2,2,256,128]{3,2,1,0:T(8,128)S(1)}, f32[2,192,128]{2,1,0:T(8,128)S(1)}) custom-call(bf16[2,32,64,256]{3,2,1,0:T(8,128)(2,1)} %crm_hbm.1, f32[384,128]{1,0:T(8,128)S(1)} %get-tuple-element.25.gcm, f32[192,128]{1,0:T(8,128)S(1)} %get-tuple-element.29.number), custom_call_target="tpu_custom_call" | custom-call | flops 4194304 | bytes 6291456 | tf_op jit(solution)/shard_map/early/pallas_call | solution.py:431
  14.0 0.0 collective-permute-done.1.other
  14.0 0.4 collective-permute-done.2.chip_mate
  14.4 0.0 collective-permute-done.core_mate
  14.4 0.6 %inner.1 = (f32[192,128]{1,0:T(8,128)S(1)}, f32[2,128,128]{2,1,0:T(8,128)S(1)}, f32[128,128]{1,0:T(8,128)S(1)}) custom-call(f32[2,192,128]{2,1,0:T(8,128)S(1)} %get-tuple-element.30.partial, f32[192,128]{1,0:T(8,128)S(1)} %get-tuple-element.29.number, f32[192,128]{1,0:T(8,128)S(1)} %collective-permute-done.core_mate, ...), custom_call_target="tpu_custom_call" | custom-call | tf_op jit(solution)/shard_map/inner/pallas_call | solution.py:447
  15.0 0.0 collective-permute-done.3.neighbour
  15.0 0.3 outer.1
  15.3 15.2 %all_to_all.10 = f32[128,2,128]{2,1,0:T(2,128)S(1)} all-to-all(f32[128,2,128]{2,1,0:T(2,128)S(1)} %bitcast.9), channel_id=1, replica_groups=mesh['blk'=32,'sub'=4] {'blk','sub'}, dimensions={0} | all-to-all | bytes 262144 | tf_op jit(solution)/shard_map/all_to_all | solution.py:384
  30.5 7.8 %cloud.1 = (f32[256,128]{1,0:T(8,128)S(1)}, f32[384,128]{1,0:T(8,128)}) custom-call(f32[256,128]{1,0:T(8,128)S(1)} %bitcast.7, f32[2,2,2048,128]{3,2,1,0:T(8,128)S(1)} %get-tuple-element.41.start, f32[2,2,256,128]{3,2,1,0:T(8,128)S(1)} %get-tuple-element.42.sums, f32[256,128]{1,0:T(8,128)S(1)} %get-tuple-element.43.advanced), custom_call_target="tpu_custom_call" | custom-call | tf_op jit(solution)/shard_map/cloud/pallas_call | solution.py:465
  38.3 14.0 %all_to_all.11 = f32[128,2,128]{2,1,0:T(2,128)S(1)} all-to-all(f32[128,2,128]{2,1,0:T(2,128)S(1)} %bitcast.10), channel_id=1, replica_groups=mesh['blk'=32,'sub'=4] {'blk','sub'}, dimensions={0} | all-to-all | bytes 262144 | tf_op jit(solution)/shard_map/all_to_all | solution.py:384
  52.3 0.9 %home.1 = (f32[384,128]{1,0:T(8,128)}, f32[128,128]{1,0:T(8,128)}) custom-call(f32[256,128]{1,0:T(8,128)S(1)} %bitcast.8, bf16[2,128,256]{2,1,0:T(8,128)(2,1)S(1)} %get-tuple-element.34.routes, f32[384,128]{1,0:T(8,128)} %get-tuple-element.45.begun), custom_call_target="tpu_custom_call", output_to_operand_aliasing={{0}: (2, {})} | custom-call | tf_op jit(solution)/shard_map/home/pallas_call | solution.py:482
Async XLA Ops:
  1.6 13.4 %collective-permute-start.3 = (f32[200,128]{1,0:T(8,128)S(1)}, f32[200,128]{1,0:T(8,128)S(1)}, u32[]{:S(2)}, u32[]{:S(2)}) collective-permute-start(f32[200,128]{1,0:T(8,128)S(1)} %get-tuple-element.37), channel_id=1, source_target_pairs={{4,8},{12,16},{20,24},{28,32},{36,40},{44,48},{52,56},{60,64},{68,... | collective-permute-start | bytes 307208 | tf_op jit(solution)/shard_map/ppermute | solution.py:414
  4.4 10.0 %collective-permute-start = (f32[192,128]{1,0:T(8,128)S(1)}, f32[192,128]{1,0:T(8,128)S(1)}, u32[]{:S(2)}, u32[]{:S(2)}) collective-permute-start(f32[192,128]{1,0:T(8,128)S(1)} %get-tuple-element.31), channel_id=1, source_target_pairs={{0,4},{8,12},{16,20},{24,28},{32,36},{40,44},{48,52},{56,60},{64,6... | collective-permute-start | bytes 294920 | tf_op jit(solution)/shard_map/ppermute | solution.py:415
  9.4 4.6 %collective-permute-start.1 = (f32[8,128]{1,0:T(8,128)S(1)}, f32[8,128]{1,0:T(8,128)S(1)}, u32[]{:S(2)}, u32[]{:S(2)}) collective-permute-start(f32[8,128]{1,0:T(8,128)S(1)} %get-tuple-element.32), channel_id=1, source_target_pairs={{1,2},{3,0},{2,1},{0,3},{5,6},{7,4},{6,5},{4,7},{9,10},{11,8},{10,... | collective-permute-start | bytes 12296 | tf_op jit(solution)/shard_map/ppermute | solution.py:429
  11.9 2.5 %collective-permute-start.2 = (f32[8,128]{1,0:T(8,128)S(1)}, f32[8,128]{1,0:T(8,128)S(1)}, u32[]{:S(2)}, u32[]{:S(2)}) collective-permute-start(f32[8,128]{1,0:T(8,128)S(1)} %get-tuple-element.33), channel_id=1, source_target_pairs={{0,1},{2,3},{1,0},{3,2},{4,5},{6,7},{5,4},{7,6},{8,9},{10,11},{9,8... | collective-permute-start | bytes 12296 | tf_op jit(solution)/shard_map/ppermute | solution.py:428

commit v10 on v9

--- a/solution.py
+++ b/solution.py
@@ -60,8 +60,9 @@
     for copy in loads:
         copy.wait()
     core = lax.rem(lax.axis_index("blk"), 2)
-    to_core_mate[...] = rows_of(gcm, 1 - core)
-    to_neighbour[: FIELDS * LEV, :] = rows_of(gcm, core)
+    rows = [rows_of(gcm, 0), rows_of(gcm, 1)]
+    to_core_mate[...] = jnp.where(core == 0, rows[1], rows[0])
+    to_neighbour[: FIELDS * LEV, :] = jnp.where(core == 0, rows[0], rows[1])
     to_neighbour[FIELDS * LEV :, :] = jnp.zeros((SUB, LANES), jnp.float32)
 
 
@@ -184,8 +185,9 @@
 ):
     core = lax.rem(lax.axis_index("blk"), 2)
     state = outer[...] + number[...] * neighbour[: FIELDS * LEV, :]
-    advanced[pl.ds(core, 4 * LEV, stride=2), :] = state[2 * LEV :]
-    advanced[pl.ds(1 - core, 4 * LEV, stride=2), :] = inner_advanced[...]
+    here, there = state[2 * LEV :], inner_advanced[...]
+    advanced[pl.ds(0, 4 * LEV, stride=2), :] = jnp.where(core == 0, here, there)
+    advanced[pl.ds(1, 4 * LEV, stride=2), :] = jnp.where(core == 0, there, here)
     values = column_values(state, rates[pl.ds(core, 1), :])
     for slot in range(2):
         outgoing[pl.ds(slot, DEVICES, stride=2), :] = done[slot] + placed(
@@ -211,12 +213,15 @@
     def down(x):
         return pltpu.roll(x, 1, axis=0)
 
+    def tree(parts):
+        while len(parts) > 1:
+            parts = [a + b for a, b in zip(parts[::2], parts[1::2])]
+        return parts[0]
+
     def folded(ref, *lead):
-        out = None
-        for part in range(SUB):
-            x = ref[(*lead, pl.ds(part, LEV, stride=SUB), slice(None))]
-            out = x if out is None else out + x
-        return out
+        return tree(
+            [ref[(*lead, pl.ds(part, LEV, stride=SUB), slice(None))] for part in range(SUB)]
+        )
 
     for half in range(2):
         values = jnp.transpose(incoming[half * LANES : (half + 1) * LANES, :])
@@ -232,22 +237,34 @@
         for f in range(2):
             mean[f, half] = folded(sums, f, half) * (1.0 / NXC)
 
-    def relax():
+    def lifted(x, rise):
+        flux = rise * jnp.where(rise > 0.0, x, up(x))
+        return x - flux + down(flux)
+
+    def relax(first):
         for half in range(2):
-            rise = coef[3, half]
-            for f in range(2):
-                now = mean[f, half]
-                flux = rise * jnp.where(rise > 0.0, now, up(now))
-                now = now - flux + down(flux)
-                add = coef[f, half] - 0.25 * now
-                coef[4 + f, half] = add
-                mean[f, half] = now + add
-                if f == 0:
-                    coef[6, half] = now + add
+            rise, rate = coef[3, half], coef[7, half]
+            now = [lifted(mean[f, half], rise) for f in range(2)]
+            add = [coef[f, half] - 0.25 * now[f] for f in range(2)]
+            offset = add[1]
+            if not first:
+                kept = lifted(mean[3, half], rise)
+                owed = rate * kept
+                offset = offset + (kept - owed)
+                coef[4, half] = add[0] + owed
+            else:
+                coef[4, half] = add[0]
+            mean[3, half] = offset
+            coef[5, half] = -offset
+            lacking = rate * offset
+            coef[8, half] = lacking
+            mean[0, half] = now[0] + add[0]
+            mean[1, half] = now[1] + add[1]
+            coef[6, half] = now[0] + add[0] - lacking
 
     def settle():
         for half in range(2):
-            rain = folded(total, half) * (1.0 / NXC)
+            rain = folded(total, half) * (1.0 / NXC) + coef[8, half]
             mean[0, half] = mean[0, half] + rain
             mean[1, half] = mean[1, half] - rain
             mean[2, half] = mean[2, half] + rain
@@ -278,7 +295,7 @@
         now = level_of(0)
         below = None
         for k in range(LEV):
-            add = [row(4, k), row(5, k)]
+            gain, least = row(4, k), row(5, k)
             if k < LEV - 1:
                 after = level_of(k + 1)
                 rise = row(3, k)
@@ -287,8 +304,7 @@
                     [rise * jnp.where(upward, a, b) for a, b in zip(now[f], after[f])]
                     for f in range(2)
                 ]
-            rained = None
-            spread = None
+            rained, spread = [], []
             if last:
                 middle = row(6, k)
             for j in range(INNER):
@@ -299,26 +315,27 @@
                         x = x - flux[f][j]
                     if k > 0:
                         x = x + below[f][j]
-                    new.append(x + add[f])
+                    new.append(x)
                 temper, moisture = new
-                rain = rate * jnp.maximum(moisture - jnp.exp2(temper), 0.0)
+                temper = temper + gain
+                rain = rate * jnp.maximum(moisture - jnp.exp2(temper), least)
                 temper = temper + rain
-                rained = rain if rained is None else rained + rain
+                rained.append(rain)
                 if last:
                     away = temper - middle
-                    spread = away * away if spread is None else spread + away * away
+                    spread.append(away * away)
                 else:
                     at = slice(k * NXC + j * SUB, k * NXC + (j + 1) * SUB)
                     state[0, half, at, :] = temper
                     state[1, half, at, :] = moisture - rain
-            total[half, k * SUB : (k + 1) * SUB, :] = rained
+            total[half, k * SUB : (k + 1) * SUB, :] = tree(rained)
             if last:
-                square[half, k * SUB : (k + 1) * SUB, :] = spread
+                square[half, k * SUB : (k + 1) * SUB, :] = tree(spread)
             if k < LEV - 1:
                 below, now = flux, after
 
-    def substep(source, last):
-        relax()
+    def substep(source, first, last):
+        relax(first)
 
         def half_of(half, carry):
             sweep(source, half, last)
@@ -330,18 +347,18 @@
 
     for half in range(2):
         mean[2, half] = jnp.zeros((LEV, LANES), jnp.float32)
-    substep(start, False)
+    substep(start, True, False)
 
     def middle_step(step, carry):
-        substep(state, False)
+        substep(state, False, False)
         return carry
 
     lax.fori_loop(0, SUBSTEPS - 2, middle_step, 0)
-    substep(state, True)
+    substep(state, False, True)
     settle()
     for half in range(2):
         warm, wet, rain = mean[0, half], mean[1, half], mean[2, half]
-        gap = warm - coef[6, half]
+        gap = warm - coef[6, half] - coef[8, half]
         spread = folded(square, half) * (1.0 / NXC) - gap * gap
         result = [
             (warm - SHIFT) * (1.0 / ALPHA),
@@ -468,8 +485,8 @@
         out_shape=(f32(COLS, LANES), f32(GCM_ROWS, LANES)),
         scratch_shapes=[
             pltpu.VMEM((2, 2, LEV * NXC, LANES), jnp.float32),
-            pltpu.VMEM((8, 2, LEV, LANES), jnp.float32),
-            pltpu.VMEM((3, 2, LEV, LANES), jnp.float32),
+            pltpu.VMEM((9, 2, LEV, LANES), jnp.float32),
+            pltpu.VMEM((4, 2, LEV, LANES), jnp.float32),
             pltpu.VMEM((2, LEV * SUB, LANES), jnp.float32),
             pltpu.VMEM((2, LEV * SUB, LANES), jnp.float32),
             pltpu.SemaphoreType.DMA(()),

time: 53.5 us -> 53.2 us (level)
  no operation moved by 1% of the time
where the time goes in v10:
time: 53.2 us; the launch traced here: 53.1 us
  blocking collectives  29.2 us (55%)
  Pallas kernels  12.7 us (24%)
  starting transfers between devices  10.1 us (19%)
  between operations  0.7 us (1%)
    all_to_all x2, blocking collectives, transfer(): lax.all_to_all(rows.reshape(DEVICES, 2, LANES), ('blk', 'sub'), split_axi...  29.2 us
    pallas_call x1, Pallas kernels, body(): pl.pallas_call(cloud_kernel, out_specs=(whole((COLS, LANES)), hbm), out_s...  7.59 us
    ppermute x1, starting transfers between devices, body(): core_mate = lax.ppermute(to_core_mate, 'blk', pairs(n_blk, 0))  4.75 us
    ppermute x1, starting transfers between devices, body(): neighbour = lax.ppermute(to_neighbour, 'blk', pairs(n_blk, 1))  2.77 us
    ppermute x1, starting transfers between devices, body(): other = lax.ppermute(to_other, 'sub', pairs(n_sub, 1))  2.56 us
    pallas_call x1, Pallas kernels, body(): pl.pallas_call(early_kernel, in_specs=[hbm, whole((GCM_ROWS, LANES)), who...  2.07 us
  transfers between devices with their start and end apart: 4, of which 1 were waited for; matrix products, arithmetic and copies ran while one was open for 0% of the time, Pallas kernels for 6%

profile of v10, /device:TPU:1, one launch (start us, length us, event | category | flops | bytes accessed | tf_op | source)
XLA Modules:
  0.0 53.1 jit_solution(14526515642072407313)
XLA Ops:
  0.6 1.0 %load.1 = (f32[384,128]{1,0:T(8,128)S(1)}, f32[192,128]{1,0:T(8,128)S(1)}, f32[200,128]{1,0:T(8,128)S(1)}, s32[2,128]{1,0:T(2,128)S(1)}, s32[2,128]{1,0:T(2,128)S(1)}, /*index=5*/f32[6,32]{1,0:T(8,128)S(1)}) custom-call(f32[384,128]{1,0:T(8,128)} %bitcast.12, s32[2,128]{1,0:T(2,128)} %owner_hbm.1, s32[2,128]{1,0:T(2,128)} %branch_hbm.1, f32[6,32]{1,0:T(8,128)} %diffusion_hbm.1), custom_call_target="tpu_custom_call" | custom-call | tf_op jit(solution)/shard_map/load/pallas_call | solution.py:416
  1.6 2.8 %collective-permute-start.3 = (f32[200,128]{1,0:T(8,128)S(1)}, f32[200,128]{1,0:T(8,128)S(1)}, u32[]{:S(2)}, u32[]{:S(2)}) collective-permute-start(f32[200,128]{1,0:T(8,128)S(1)} %get-tuple-element.37), channel_id=1, source_target_pairs={{4,8},{12,16},{20,24},{28,32},{36,40},{44,48},{52,56},{60,64},{68,... | collective-permute-start | bytes 307208 | tf_op jit(solution)/shard_map/ppermute | solution.py:431
  4.4 4.7 %collective-permute-start = (f32[192,128]{1,0:T(8,128)S(1)}, f32[192,128]{1,0:T(8,128)S(1)}, u32[]{:S(2)}, u32[]{:S(2)}) collective-permute-start(f32[192,128]{1,0:T(8,128)S(1)} %get-tuple-element.31), channel_id=1, source_target_pairs={{0,4},{8,12},{16,20},{24,28},{32,36},{40,44},{48,52},{56,60},{64,6... | collective-permute-start | bytes 294920 | tf_op jit(solution)/shard_map/ppermute | solution.py:432
  9.1 0.2 edges.1
  9.4 2.6 %collective-permute-start.1 = (f32[8,128]{1,0:T(8,128)S(1)}, f32[8,128]{1,0:T(8,128)S(1)}, u32[]{:S(2)}, u32[]{:S(2)}) collective-permute-start(f32[8,128]{1,0:T(8,128)S(1)} %get-tuple-element.32), channel_id=1, source_target_pairs={{1,2},{3,0},{2,1},{0,3},{5,6},{7,4},{6,5},{4,7},{9,10},{11,8},{10,... | collective-permute-start | bytes 12296 | tf_op jit(solution)/shard_map/ppermute | solution.py:446
  11.9 0.0 collective-permute-start.2
  11.9 2.1 %early.1 = (f32[2,2,2048,128]{3,2,1,0:T(8,128)S(1)}, f32[2,2,256,128]{3,2,1,0:T(8,128)S(1)}, f32[2,192,128]{2,1,0:T(8,128)S(1)}) custom-call(bf16[2,32,64,256]{3,2,1,0:T(8,128)(2,1)} %crm_hbm.1, f32[384,128]{1,0:T(8,128)S(1)} %get-tuple-element.25.gcm, f32[192,128]{1,0:T(8,128)S(1)} %get-tuple-element.29.number), custom_call_target="tpu_custom_call" | custom-call | flops 4194304 | bytes 6291456 | tf_op jit(solution)/shard_map/early/pallas_call | solution.py:448
  14.0 0.0 collective-permute-done.1.other
  14.0 0.4 collective-permute-done.2.chip_mate
  14.4 0.0 collective-permute-done.core_mate
  14.4 0.6 %inner.1 = (f32[192,128]{1,0:T(8,128)S(1)}, f32[2,128,128]{2,1,0:T(8,128)S(1)}, f32[128,128]{1,0:T(8,128)S(1)}) custom-call(f32[2,192,128]{2,1,0:T(8,128)S(1)} %get-tuple-element.30.partial, f32[192,128]{1,0:T(8,128)S(1)} %get-tuple-element.29.number, f32[192,128]{1,0:T(8,128)S(1)} %collective-permute-done.core_mate, ...), custom_call_target="tpu_custom_call" | custom-call | tf_op jit(solution)/shard_map/inner/pallas_call | solution.py:464
  15.0 0.0 collective-permute-done.3.neighbour
  15.0 0.3 outer.1
  15.3 15.2 %all_to_all.10 = f32[128,2,128]{2,1,0:T(2,128)S(1)} all-to-all(f32[128,2,128]{2,1,0:T(2,128)S(1)} %bitcast.9), channel_id=1, replica_groups=mesh['blk'=32,'sub'=4] {'blk','sub'}, dimensions={0} | all-to-all | bytes 262144 | tf_op jit(solution)/shard_map/all_to_all | solution.py:401
  30.5 7.6 %cloud.1 = (f32[256,128]{1,0:T(8,128)S(1)}, f32[384,128]{1,0:T(8,128)}) custom-call(f32[256,128]{1,0:T(8,128)S(1)} %bitcast.7, f32[2,2,2048,128]{3,2,1,0:T(8,128)S(1)} %get-tuple-element.41.start, f32[2,2,256,128]{3,2,1,0:T(8,128)S(1)} %get-tuple-element.42.sums, f32[256,128]{1,0:T(8,128)S(1)} %get-tuple-element.43.advanced), custom_call_target="tpu_custom_call" | custom-call | tf_op jit(solution)/shard_map/cloud/pallas_call | solution.py:482
  38.1 14.0 %all_to_all.11 = f32[128,2,128]{2,1,0:T(2,128)S(1)} all-to-all(f32[128,2,128]{2,1,0:T(2,128)S(1)} %bitcast.10), channel_id=1, replica_groups=mesh['blk'=32,'sub'=4] {'blk','sub'}, dimensions={0} | all-to-all | bytes 262144 | tf_op jit(solution)/shard_map/all_to_all | solution.py:401
  52.1 0.9 %home.1 = (f32[384,128]{1,0:T(8,128)}, f32[128,128]{1,0:T(8,128)}) custom-call(f32[256,128]{1,0:T(8,128)S(1)} %bitcast.8, bf16[2,128,256]{2,1,0:T(8,128)(2,1)S(1)} %get-tuple-element.34.routes, f32[384,128]{1,0:T(8,128)} %get-tuple-element.45.begun), custom_call_target="tpu_custom_call", output_to_operand_aliasing={{0}: (2, {})} | custom-call | tf_op jit(solution)/shard_map/home/pallas_call | solution.py:499
Async XLA Ops:
  1.6 13.4 %collective-permute-start.3 = (f32[200,128]{1,0:T(8,128)S(1)}, f32[200,128]{1,0:T(8,128)S(1)}, u32[]{:S(2)}, u32[]{:S(2)}) collective-permute-start(f32[200,128]{1,0:T(8,128)S(1)} %get-tuple-element.37), channel_id=1, source_target_pairs={{4,8},{12,16},{20,24},{28,32},{36,40},{44,48},{52,56},{60,64},{68,... | collective-permute-start | bytes 307208 | tf_op jit(solution)/shard_map/ppermute | solution.py:431
  4.4 10.0 %collective-permute-start = (f32[192,128]{1,0:T(8,128)S(1)}, f32[192,128]{1,0:T(8,128)S(1)}, u32[]{:S(2)}, u32[]{:S(2)}) collective-permute-start(f32[192,128]{1,0:T(8,128)S(1)} %get-tuple-element.31), channel_id=1, source_target_pairs={{0,4},{8,12},{16,20},{24,28},{32,36},{40,44},{48,52},{56,60},{64,6... | collective-permute-start | bytes 294920 | tf_op jit(solution)/shard_map/ppermute | solution.py:432
  9.4 4.6 %collective-permute-start.1 = (f32[8,128]{1,0:T(8,128)S(1)}, f32[8,128]{1,0:T(8,128)S(1)}, u32[]{:S(2)}, u32[]{:S(2)}) collective-permute-start(f32[8,128]{1,0:T(8,128)S(1)} %get-tuple-element.32), channel_id=1, source_target_pairs={{1,2},{3,0},{2,1},{0,3},{5,6},{7,4},{6,5},{4,7},{9,10},{11,8},{10,... | collective-permute-start | bytes 12296 | tf_op jit(solution)/shard_map/ppermute | solution.py:446
  11.9 2.5 %collective-permute-start.2 = (f32[8,128]{1,0:T(8,128)S(1)}, f32[8,128]{1,0:T(8,128)S(1)}, u32[]{:S(2)}, u32[]{:S(2)}) collective-permute-start(f32[8,128]{1,0:T(8,128)S(1)} %get-tuple-element.33), channel_id=1, source_target_pairs={{0,1},{2,3},{1,0},{3,2},{4,5},{6,7},{5,4},{7,6},{8,9},{10,11},{9,8... | collective-permute-start | bytes 12296 | tf_op jit(solution)/shard_map/ppermute | solution.py:445

commit v11 on v10

--- a/solution.py
+++ b/solution.py
@@ -97,7 +97,17 @@
         to_other[part : part + 1, :] = jnp.where(even, first, last)
 
 
-def early_kernel(crm_hbm, gcm, number, state, sums, partial, crm, arrival):
+def tree(parts):
+    while len(parts) > 1:
+        parts = [a + b for a, b in zip(parts[::2], parts[1::2])]
+    return parts[0]
+
+
+def folded(ref, *lead):
+    return tree([ref[(*lead, pl.ds(part, LEV, stride=SUB), slice(None))] for part in range(SUB)])
+
+
+def early_kernel(crm_hbm, gcm, number, state, means, partial, crm, sums, arrival):
     loads = [
         pltpu.make_async_copy(
             crm_hbm.at[f, pl.ds(part * CRM_CHUNK, CRM_CHUNK)],
@@ -135,6 +145,9 @@
                 return carry
 
             lax.fori_loop(0, CRM_CHUNK, level, 0, unroll=4)
+    for f in range(2):
+        for half in range(2):
+            means[f, half] = folded(sums, f, half) * (1.0 / NXC)
 
 
 def column_values(state, rate):
@@ -196,7 +209,7 @@
 
 
 def cloud_kernel(
-    incoming, start, sums, advanced, outgoing, gcm_next,
+    incoming, start, means, advanced, outgoing, gcm_next,
     state, coef, mean, total, square, departure,
 ):
     leaving = pltpu.make_async_copy(
@@ -212,16 +225,6 @@
 
     def down(x):
         return pltpu.roll(x, 1, axis=0)
-
-    def tree(parts):
-        while len(parts) > 1:
-            parts = [a + b for a, b in zip(parts[::2], parts[1::2])]
-        return parts[0]
-
-    def folded(ref, *lead):
-        return tree(
-            [ref[(*lead, pl.ds(part, LEV, stride=SUB), slice(None))] for part in range(SUB)]
-        )
 
     for half in range(2):
         values = jnp.transpose(incoming[half * LANES : (half + 1) * LANES, :])
@@ -234,26 +237,34 @@
         coef[2, half] = values[2 * LEV : 3 * LEV]
         coef[3, half] = rise
         coef[7, half] = jnp.broadcast_to(rates[half], (LEV, LANES))
-        for f in range(2):
-            mean[f, half] = folded(sums, f, half) * (1.0 / NXC)
+        coef[9, half] = jnp.abs(coef[2, half])
 
     def lifted(x, rise):
         flux = rise * jnp.where(rise > 0.0, x, up(x))
         return x - flux + down(flux)
 
+    def settled(half):
+        rain = folded(total, half) * (1.0 / NXC) + coef[8, half]
+        return mean[0, half] + rain, mean[1, half] - rain, mean[2, half] + rain
+
     def relax(first):
         for half in range(2):
             rise, rate = coef[3, half], coef[7, half]
-            now = [lifted(mean[f, half], rise) for f in range(2)]
+            if first:
+                before = means[0, half], means[1, half]
+                mean[2, half] = jnp.zeros((LEV, LANES), jnp.float32)
+            else:
+                *before, mean[2, half] = settled(half)
+            now = [lifted(x, rise) for x in before]
             add = [coef[f, half] - 0.25 * now[f] for f in range(2)]
             offset = add[1]
-            if not first:
+            if first:
+                coef[4, half] = add[0]
+            else:
                 kept = lifted(mean[3, half], rise)
                 owed = rate * kept
                 offset = offset + (kept - owed)
                 coef[4, half] = add[0] + owed
-            else:
-                coef[4, half] = add[0]
             mean[3, half] = offset
             coef[5, half] = -offset
             lacking = rate * offset
@@ -261,13 +272,6 @@
             mean[0, half] = now[0] + add[0]
             mean[1, half] = now[1] + add[1]
             coef[6, half] = now[0] + add[0] - lacking
-
-    def settle():
-        for half in range(2):
-            rain = folded(total, half) * (1.0 / NXC) + coef[8, half]
-            mean[0, half] = mean[0, half] + rain
-            mean[1, half] = mean[1, half] - rain
-            mean[2, half] = mean[2, half] + rain
 
     def sweep(source, half, last):
         rate = jnp.broadcast_to(coef[7, half, 0:1, :], (SUB, LANES))
@@ -289,7 +293,7 @@
 
         def level_of(k):
             drift = row(2, k)
-            size, positive = jnp.abs(drift), drift > 0.0
+            size, positive = row(9, k), drift > 0.0
             return [drifted(f, k, size, positive) for f in range(2)]
 
         now = level_of(0)
@@ -342,11 +346,7 @@
             return carry
 
         lax.fori_loop(0, 2, half_of, 0)
-        if not last:
-            settle()
-
-    for half in range(2):
-        mean[2, half] = jnp.zeros((LEV, LANES), jnp.float32)
+
     substep(start, True, False)
 
     def middle_step(step, carry):
@@ -355,9 +355,8 @@
 
     lax.fori_loop(0, SUBSTEPS - 2, middle_step, 0)
     substep(state, False, True)
-    settle()
     for half in range(2):
-        warm, wet, rain = mean[0, half], mean[1, half], mean[2, half]
+        warm, wet, rain = settled(half)
         gap = warm - coef[6, half] - coef[8, half]
         spread = folded(square, half) * (1.0 / NXC) - gap * gap
         result = [
@@ -445,16 +444,17 @@
     chip_mate = lax.ppermute(to_chip_mate, "sub", pairs(n_sub, 0))
     other = lax.ppermute(to_other, "sub", pairs(n_sub, 1))
     cells = 2 * LEV * NXC * COLS
-    state, sums, partial = pl.pallas_call(
+    state, means, partial = pl.pallas_call(
         early_kernel,
         in_specs=[hbm, whole((GCM_ROWS, LANES)), whole((FIELDS * LEV, LANES))],
         out_shape=(
             f32(2, 2, LEV * NXC, LANES),
-            f32(2, 2, LEV * SUB, LANES),
+            f32(2, 2, LEV, LANES),
             f32(2, FIELDS * LEV, LANES),
         ),
         scratch_shapes=[
             pltpu.VMEM((2, LEV, NXC, COLS), jnp.bfloat16),
+            pltpu.VMEM((2, 2, LEV * SUB, LANES), jnp.float32),
             pltpu.SemaphoreType.DMA((2, LEV // CRM_CHUNK)),
         ],
         compiler_params=pltpu.CompilerParams(vmem_limit_bytes=16 * MIB),
@@ -485,7 +485,7 @@
         out_shape=(f32(COLS, LANES), f32(GCM_ROWS, LANES)),
         scratch_shapes=[
             pltpu.VMEM((2, 2, LEV * NXC, LANES), jnp.float32),
-            pltpu.VMEM((9, 2, LEV, LANES), jnp.float32),
+            pltpu.VMEM((10, 2, LEV, LANES), jnp.float32),
             pltpu.VMEM((4, 2, LEV, LANES), jnp.float32),
             pltpu.VMEM((2, LEV * SUB, LANES), jnp.float32),
             pltpu.VMEM((2, LEV * SUB, LANES), jnp.float32),
@@ -493,7 +493,7 @@
         ],
         compiler_params=pltpu.CompilerParams(vmem_limit_bytes=12 * MIB),
         name="cloud",
-    )(incoming, state, sums, advanced)
+    )(incoming, state, means, advanced)
     returned = transfer(profiles)
 
     gcm_next, stats = pl.pallas_call(

time: 53.2 us -> 53.2 us (level)
  no operation moved by 1% of the time
where the time goes in v11:
time: 53.2 us; the launch traced here: 53 us
  blocking collectives  29.2 us (55%)
  Pallas kernels  12.7 us (24%)
  starting transfers between devices  10.1 us (19%)
  between operations  0.7 us (1%)
    all_to_all x2, blocking collectives, transfer(): lax.all_to_all(rows.reshape(DEVICES, 2, LANES), ('blk', 'sub'), split_axi...  29.2 us
    pallas_call x1, Pallas kernels, body(): pl.pallas_call(cloud_kernel, out_specs=(whole((COLS, LANES)), hbm), out_s...  7.54 us
    ppermute x1, starting transfers between devices, body(): core_mate = lax.ppermute(to_core_mate, 'blk', pairs(n_blk, 0))  4.75 us
    ppermute x1, starting transfers between devices, body(): neighbour = lax.ppermute(to_neighbour, 'blk', pairs(n_blk, 1))  2.77 us
    ppermute x1, starting transfers between devices, body(): other = lax.ppermute(to_other, 'sub', pairs(n_sub, 1))  2.56 us
    pallas_call x1, Pallas kernels, body(): pl.pallas_call(early_kernel, in_specs=[hbm, whole((GCM_ROWS, LANES)), who...  2.16 us
  transfers between devices with their start and end apart: 4, of which 1 were waited for; matrix products, arithmetic and copies ran while one was open for 0% of the time, Pallas kernels for 6%

profile of v11, /device:TPU:1, one launch (start us, length us, event | category | flops | bytes accessed | tf_op | source)
XLA Modules:
  0.0 53.0 jit_solution(10429978988478118108)
XLA Ops:
  0.6 1.0 %load.1 = (f32[384,128]{1,0:T(8,128)S(1)}, f32[192,128]{1,0:T(8,128)S(1)}, f32[200,128]{1,0:T(8,128)S(1)}, s32[2,128]{1,0:T(2,128)S(1)}, s32[2,128]{1,0:T(2,128)S(1)}, /*index=5*/f32[6,32]{1,0:T(8,128)S(1)}) custom-call(f32[384,128]{1,0:T(8,128)} %bitcast.12, s32[2,128]{1,0:T(2,128)} %owner_hbm.1, s32[2,128]{1,0:T(2,128)} %branch_hbm.1, f32[6,32]{1,0:T(8,128)} %diffusion_hbm.1), custom_call_target="tpu_custom_call" | custom-call | tf_op jit(solution)/shard_map/load/pallas_call | solution.py:415
  1.6 2.8 %collective-permute-start.3 = (f32[200,128]{1,0:T(8,128)S(1)}, f32[200,128]{1,0:T(8,128)S(1)}, u32[]{:S(2)}, u32[]{:S(2)}) collective-permute-start(f32[200,128]{1,0:T(8,128)S(1)} %get-tuple-element.37), channel_id=1, source_target_pairs={{4,8},{12,16},{20,24},{28,32},{36,40},{44,48},{52,56},{60,64},{68,... | collective-permute-start | bytes 307208 | tf_op jit(solution)/shard_map/ppermute | solution.py:430
  4.4 4.7 %collective-permute-start = (f32[192,128]{1,0:T(8,128)S(1)}, f32[192,128]{1,0:T(8,128)S(1)}, u32[]{:S(2)}, u32[]{:S(2)}) collective-permute-start(f32[192,128]{1,0:T(8,128)S(1)} %get-tuple-element.31), channel_id=1, source_target_pairs={{0,4},{8,12},{16,20},{24,28},{32,36},{40,44},{48,52},{56,60},{64,6... | collective-permute-start | bytes 294920 | tf_op jit(solution)/shard_map/ppermute | solution.py:431
  9.1 0.2 edges.1
  9.4 2.6 %collective-permute-start.1 = (f32[8,128]{1,0:T(8,128)S(1)}, f32[8,128]{1,0:T(8,128)S(1)}, u32[]{:S(2)}, u32[]{:S(2)}) collective-permute-start(f32[8,128]{1,0:T(8,128)S(1)} %get-tuple-element.32), channel_id=1, source_target_pairs={{1,2},{3,0},{2,1},{0,3},{5,6},{7,4},{6,5},{4,7},{9,10},{11,8},{10,... | collective-permute-start | bytes 12296 | tf_op jit(solution)/shard_map/ppermute | solution.py:445
  11.9 0.0 collective-permute-start.2
  11.9 2.2 %early.1 = (f32[2,2,2048,128]{3,2,1,0:T(8,128)S(1)}, f32[2,2,32,128]{3,2,1,0:T(8,128)S(1)}, f32[2,192,128]{2,1,0:T(8,128)S(1)}) custom-call(bf16[2,32,64,256]{3,2,1,0:T(8,128)(2,1)} %crm_hbm.1, f32[384,128]{1,0:T(8,128)S(1)} %get-tuple-element.25.gcm, f32[192,128]{1,0:T(8,128)S(1)} %get-tuple-element.29.number), custom_call_target="tpu_custom_call" | custom-call | flops 4194304 | bytes 6291456 | tf_op jit(solution)/shard_map/early/pallas_call | solution.py:447
  14.1 0.0 collective-permute-done.1.other
  14.1 0.3 collective-permute-done.2.chip_mate
  14.4 0.0 collective-permute-done.core_mate
  14.4 0.6 %inner.1 = (f32[192,128]{1,0:T(8,128)S(1)}, f32[2,128,128]{2,1,0:T(8,128)S(1)}, f32[128,128]{1,0:T(8,128)S(1)}) custom-call(f32[2,192,128]{2,1,0:T(8,128)S(1)} %get-tuple-element.30.partial, f32[192,128]{1,0:T(8,128)S(1)} %get-tuple-element.29.number, f32[192,128]{1,0:T(8,128)S(1)} %collective-permute-done.core_mate, ...), custom_call_target="tpu_custom_call" | custom-call | tf_op jit(solution)/shard_map/inner/pallas_call | solution.py:464
  15.0 0.0 collective-permute-done.3.neighbour
  15.0 0.3 outer.1
  15.3 15.2 %all_to_all.10 = f32[128,2,128]{2,1,0:T(2,128)S(1)} all-to-all(f32[128,2,128]{2,1,0:T(2,128)S(1)} %bitcast.9), channel_id=1, replica_groups=mesh['blk'=32,'sub'=4] {'blk','sub'}, dimensions={0} | all-to-all | bytes 262144 | tf_op jit(solution)/shard_map/all_to_all | solution.py:400
  30.5 7.5 %cloud.1 = (f32[256,128]{1,0:T(8,128)S(1)}, f32[384,128]{1,0:T(8,128)}) custom-call(f32[256,128]{1,0:T(8,128)S(1)} %bitcast.7, f32[2,2,2048,128]{3,2,1,0:T(8,128)S(1)} %get-tuple-element.41.start, f32[2,2,32,128]{3,2,1,0:T(8,128)S(1)} %get-tuple-element.42.means, f32[256,128]{1,0:T(8,128)S(1)} %get-tuple-element.43.advanced), custom_call_target="tpu_custom_call" | custom-call | tf_op jit(solution)/shard_map/cloud/pallas_call | solution.py:482
  38.0 14.0 %all_to_all.11 = f32[128,2,128]{2,1,0:T(2,128)S(1)} all-to-all(f32[128,2,128]{2,1,0:T(2,128)S(1)} %bitcast.10), channel_id=1, replica_groups=mesh['blk'=32,'sub'=4] {'blk','sub'}, dimensions={0} | all-to-all | bytes 262144 | tf_op jit(solution)/shard_map/all_to_all | solution.py:400
  52.1 0.9 %home.1 = (f32[384,128]{1,0:T(8,128)}, f32[128,128]{1,0:T(8,128)}) custom-call(f32[256,128]{1,0:T(8,128)S(1)} %bitcast.8, bf16[2,128,256]{2,1,0:T(8,128)(2,1)S(1)} %get-tuple-element.34.routes, f32[384,128]{1,0:T(8,128)} %get-tuple-element.45.begun), custom_call_target="tpu_custom_call", output_to_operand_aliasing={{0}: (2, {})} | custom-call | tf_op jit(solution)/shard_map/home/pallas_call | solution.py:499
Async XLA Ops:
  1.6 13.4 %collective-permute-start.3 = (f32[200,128]{1,0:T(8,128)S(1)}, f32[200,128]{1,0:T(8,128)S(1)}, u32[]{:S(2)}, u32[]{:S(2)}) collective-permute-start(f32[200,128]{1,0:T(8,128)S(1)} %get-tuple-element.37), channel_id=1, source_target_pairs={{4,8},{12,16},{20,24},{28,32},{36,40},{44,48},{52,56},{60,64},{68,... | collective-permute-start | bytes 307208 | tf_op jit(solution)/shard_map/ppermute | solution.py:430
  4.4 10.0 %collective-permute-start = (f32[192,128]{1,0:T(8,128)S(1)}, f32[192,128]{1,0:T(8,128)S(1)}, u32[]{:S(2)}, u32[]{:S(2)}) collective-permute-start(f32[192,128]{1,0:T(8,128)S(1)} %get-tuple-element.31), channel_id=1, source_target_pairs={{0,4},{8,12},{16,20},{24,28},{32,36},{40,44},{48,52},{56,60},{64,6... | collective-permute-start | bytes 294920 | tf_op jit(solution)/shard_map/ppermute | solution.py:431
  9.4 4.7 %collective-permute-start.1 = (f32[8,128]{1,0:T(8,128)S(1)}, f32[8,128]{1,0:T(8,128)S(1)}, u32[]{:S(2)}, u32[]{:S(2)}) collective-permute-start(f32[8,128]{1,0:T(8,128)S(1)} %get-tuple-element.32), channel_id=1, source_target_pairs={{1,2},{3,0},{2,1},{0,3},{5,6},{7,4},{6,5},{4,7},{9,10},{11,8},{10,... | collective-permute-start | bytes 12296 | tf_op jit(solution)/shard_map/ppermute | solution.py:445
  11.9 2.5 %collective-permute-start.2 = (f32[8,128]{1,0:T(8,128)S(1)}, f32[8,128]{1,0:T(8,128)S(1)}, u32[]{:S(2)}, u32[]{:S(2)}) collective-permute-start(f32[8,128]{1,0:T(8,128)S(1)} %get-tuple-element.33), channel_id=1, source_target_pairs={{0,1},{2,3},{1,0},{3,2},{4,5},{6,7},{5,4},{7,6},{8,9},{10,11},{9,8... | collective-permute-start | bytes 12296 | tf_op jit(solution)/shard_map/ppermute | solution.py:444

commit v12 on v11

--- a/solution.py
+++ b/solution.py
@@ -47,7 +47,7 @@
 
 def load_kernel(
     gcm_hbm, owner_hbm, branch_hbm, diffusion_hbm,
-    gcm, to_core_mate, to_neighbour, owner, branch, diffusion, arrival,
+    gcm, to_neighbour, owner, branch, diffusion, arrival,
 ):
     loads = [
         pltpu.make_async_copy(source, target, arrival.at[n])
@@ -60,14 +60,13 @@
     for copy in loads:
         copy.wait()
     core = lax.rem(lax.axis_index("blk"), 2)
-    rows = [rows_of(gcm, 0), rows_of(gcm, 1)]
-    to_core_mate[...] = jnp.where(core == 0, rows[1], rows[0])
-    to_neighbour[: FIELDS * LEV, :] = jnp.where(core == 0, rows[0], rows[1])
+    to_neighbour[: FIELDS * LEV, :] = jnp.where(core == 0, rows_of(gcm, 0), rows_of(gcm, 1))
     to_neighbour[FIELDS * LEV :, :] = jnp.zeros((SUB, LANES), jnp.float32)
 
 
 def edge_kernel(
-    gcm, owner, branch, diffusion, to_chip_mate, to_other, routes, rates, number
+    gcm, owner, branch, diffusion,
+    to_core_mate, to_chip_mate, to_other, routes, rates, number,
 ):
     to_chip_mate[...] = jnp.zeros_like(to_chip_mate)
     to_other[...] = jnp.zeros_like(to_other)
@@ -89,7 +88,10 @@
         number[f * LEV : (f + 1) * LEV, :] = jnp.transpose(spread)
 
     even = lax.rem(lax.axis_index("sub"), 2) == 0
-    rows = jnp.concatenate([rows_of(gcm, 0), rows_of(gcm, 1)], axis=0)
+    pair = [rows_of(gcm, 0), rows_of(gcm, 1)]
+    core = lax.rem(lax.axis_index("blk"), 2)
+    to_core_mate[...] = jnp.where(core == 0, pair[1], pair[0])
+    rows = jnp.concatenate(pair, axis=0)
     for part in range(GCM_ROWS // LANES):
         turned = jnp.transpose(rows[part * LANES : (part + 1) * LANES])
         first, last = turned[:1], turned[LANES - 1 :]
@@ -412,12 +414,11 @@
 
     n_blk, n_sub = lax.axis_size("blk"), lax.axis_size("sub")
     hbm = pl.BlockSpec(memory_space=pltpu.HBM)
-    gcm_here, to_core_mate, to_neighbour, owner_here, branch_here, diffusion_here = pl.pallas_call(
+    gcm_here, to_neighbour, owner_here, branch_here, diffusion_here = pl.pallas_call(
         load_kernel,
         in_specs=[hbm] * 4,
         out_shape=(
             f32(GCM_ROWS, LANES),
-            f32(FIELDS * LEV, LANES),
             f32(FIELDS * LEV + SUB, LANES),
             jax.ShapeDtypeStruct(owner.shape, owner.dtype),
             jax.ShapeDtypeStruct(branch.shape, branch.dtype),
@@ -428,10 +429,10 @@
         name="load",
     )(*map(in_hbm, (gcm, owner, branch, diffusion)))
     neighbour = lax.ppermute(to_neighbour, "blk", pairs(n_blk, 1))
-    core_mate = lax.ppermute(to_core_mate, "blk", pairs(n_blk, 0))
-    to_chip_mate, to_other, routes, rates, number = pl.pallas_call(
+    to_core_mate, to_chip_mate, to_other, routes, rates, number = pl.pallas_call(
         edge_kernel,
         out_shape=(
+            f32(FIELDS * LEV, LANES),
             f32(SUB, LANES),
             f32(SUB, LANES),
             jax.ShapeDtypeStruct((2, DEVICES, COLS), jnp.bfloat16),
@@ -443,6 +444,7 @@
     )(gcm_here, owner_here, branch_here, diffusion_here)
     chip_mate = lax.ppermute(to_chip_mate, "sub", pairs(n_sub, 0))
     other = lax.ppermute(to_other, "sub", pairs(n_sub, 1))
+    core_mate = lax.ppermute(to_core_mate, "blk", pairs(n_blk, 0))
     cells = 2 * LEV * NXC * COLS
     state, means, partial = pl.pallas_call(
         early_kernel,

time: 53.2 us -> 53.2 us (level)
  no operation moved by 1% of the time
where the time goes in v12:
time: 53.2 us; the launch traced here: 53 us
  blocking collectives  29.2 us (55%)
  Pallas kernels  12.7 us (24%)
  starting transfers between devices  10.1 us (19%)
  between operations  0.7 us (1%)
    all_to_all x2, blocking collectives, transfer(): lax.all_to_all(rows.reshape(DEVICES, 2, LANES), ('blk', 'sub'), split_axi...  29.2 us
    pallas_call x1, Pallas kernels, body(): pl.pallas_call(cloud_kernel, out_specs=(whole((COLS, LANES)), hbm), out_s...  7.54 us
    ppermute x1, starting transfers between devices, body(): core_mate = lax.ppermute(to_core_mate, 'blk', pairs(n_blk, 0))  4.83 us
    ppermute x1, starting transfers between devices, body(): neighbour = lax.ppermute(to_neighbour, 'blk', pairs(n_blk, 1))  2.77 us
    ppermute x1, starting transfers between devices, body(): other = lax.ppermute(to_other, 'sub', pairs(n_sub, 1))  2.49 us
    pallas_call x1, Pallas kernels, body(): pl.pallas_call(early_kernel, in_specs=[hbm, whole((GCM_ROWS, LANES)), who...  2.16 us
  transfers between devices with their start and end apart: 4, of which 1 were waited for; matrix products, arithmetic and copies ran while one was open for 0% of the time, Pallas kernels for 6%

profile of v12, /device:TPU:1, one launch (start us, length us, event | category | flops | bytes accessed | tf_op | source)
XLA Modules:
  0.0 53.0 jit_solution(3176005861356488296)
XLA Ops:
  0.6 1.0 %load.1 = (f32[384,128]{1,0:T(8,128)S(1)}, f32[200,128]{1,0:T(8,128)S(1)}, s32[2,128]{1,0:T(2,128)S(1)}, s32[2,128]{1,0:T(2,128)S(1)}, f32[6,32]{1,0:T(8,128)S(1)}) custom-call(f32[384,128]{1,0:T(8,128)} %bitcast.12, s32[2,128]{1,0:T(2,128)} %owner_hbm.1, s32[2,128]{1,0:T(2,128)} %branch_hbm.1, f32[6,32]{1,0:T(8,128)} %diffusion_hbm.1), custom_call_target="tpu_custom_call" | custom-call | tf_op jit(solution)/shard_map/load/pallas_call | solution.py:417
  1.6 2.8 %collective-permute-start.3 = (f32[200,128]{1,0:T(8,128)S(1)}, f32[200,128]{1,0:T(8,128)S(1)}, u32[]{:S(2)}, u32[]{:S(2)}) collective-permute-start(f32[200,128]{1,0:T(8,128)S(1)} %get-tuple-element.37), channel_id=1, source_target_pairs={{4,8},{12,16},{20,24},{28,32},{36,40},{44,48},{52,56},{60,64},{68,... | collective-permute-start | bytes 307208 | tf_op jit(solution)/shard_map/ppermute | solution.py:431
  4.4 0.2 edges.1
  4.6 4.8 %collective-permute-start = (f32[192,128]{1,0:T(8,128)S(1)}, f32[192,128]{1,0:T(8,128)S(1)}, u32[]{:S(2)}, u32[]{:S(2)}) collective-permute-start(f32[192,128]{1,0:T(8,128)S(1)} %get-tuple-element.31), channel_id=1, source_target_pairs={{0,4},{8,12},{16,20},{24,28},{32,36},{40,44},{48,52},{56,60},{64,6... | collective-permute-start | bytes 294920 | tf_op jit(solution)/shard_map/ppermute | solution.py:447
  9.4 2.5 %collective-permute-start.1 = (f32[8,128]{1,0:T(8,128)S(1)}, f32[8,128]{1,0:T(8,128)S(1)}, u32[]{:S(2)}, u32[]{:S(2)}) collective-permute-start(f32[8,128]{1,0:T(8,128)S(1)} %get-tuple-element.32), channel_id=1, source_target_pairs={{1,2},{3,0},{2,1},{0,3},{5,6},{7,4},{6,5},{4,7},{9,10},{11,8},{10,... | collective-permute-start | bytes 12296 | tf_op jit(solution)/shard_map/ppermute | solution.py:446
  11.9 0.0 collective-permute-start.2
  11.9 2.2 %early.1 = (f32[2,2,2048,128]{3,2,1,0:T(8,128)S(1)}, f32[2,2,32,128]{3,2,1,0:T(8,128)S(1)}, f32[2,192,128]{2,1,0:T(8,128)S(1)}) custom-call(bf16[2,32,64,256]{3,2,1,0:T(8,128)(2,1)} %crm_hbm.1, f32[384,128]{1,0:T(8,128)S(1)} %get-tuple-element.25.gcm, f32[192,128]{1,0:T(8,128)S(1)} %get-tuple-element.29.number), custom_call_target="tpu_custom_call" | custom-call | flops 4194304 | bytes 6291456 | tf_op jit(solution)/shard_map/early/pallas_call | solution.py:449
  14.1 0.0 collective-permute-done.1.other
  14.1 0.3 collective-permute-done.2.chip_mate
  14.4 0.0 collective-permute-done.core_mate
  14.4 0.6 %inner.1 = (f32[192,128]{1,0:T(8,128)S(1)}, f32[2,128,128]{2,1,0:T(8,128)S(1)}, f32[128,128]{1,0:T(8,128)S(1)}) custom-call(f32[2,192,128]{2,1,0:T(8,128)S(1)} %get-tuple-element.30.partial, f32[192,128]{1,0:T(8,128)S(1)} %get-tuple-element.29.number, f32[192,128]{1,0:T(8,128)S(1)} %collective-permute-done.core_mate, ...), custom_call_target="tpu_custom_call" | custom-call | tf_op jit(solution)/shard_map/inner/pallas_call | solution.py:466
  15.0 0.0 collective-permute-done.3.neighbour
  15.1 0.3 outer.1
  15.3 15.1 %all_to_all.10 = f32[128,2,128]{2,1,0:T(2,128)S(1)} all-to-all(f32[128,2,128]{2,1,0:T(2,128)S(1)} %bitcast.9), channel_id=1, replica_groups=mesh['blk'=32,'sub'=4] {'blk','sub'}, dimensions={0} | all-to-all | bytes 262144 | tf_op jit(solution)/shard_map/all_to_all | solution.py:402
  30.5 7.5 %cloud.1 = (f32[256,128]{1,0:T(8,128)S(1)}, f32[384,128]{1,0:T(8,128)}) custom-call(f32[256,128]{1,0:T(8,128)S(1)} %bitcast.7, f32[2,2,2048,128]{3,2,1,0:T(8,128)S(1)} %get-tuple-element.41.start, f32[2,2,32,128]{3,2,1,0:T(8,128)S(1)} %get-tuple-element.42.means, f32[256,128]{1,0:T(8,128)S(1)} %get-tuple-element.43.advanced), custom_call_target="tpu_custom_call" | custom-call | tf_op jit(solution)/shard_map/cloud/pallas_call | solution.py:484
  38.0 14.0 %all_to_all.11 = f32[128,2,128]{2,1,0:T(2,128)S(1)} all-to-all(f32[128,2,128]{2,1,0:T(2,128)S(1)} %bitcast.10), channel_id=1, replica_groups=mesh['blk'=32,'sub'=4] {'blk','sub'}, dimensions={0} | all-to-all | bytes 262144 | tf_op jit(solution)/shard_map/all_to_all | solution.py:402
  52.1 0.9 %home.1 = (f32[384,128]{1,0:T(8,128)}, f32[128,128]{1,0:T(8,128)}) custom-call(f32[256,128]{1,0:T(8,128)S(1)} %bitcast.8, bf16[2,128,256]{2,1,0:T(8,128)(2,1)S(1)} %get-tuple-element.34.routes, f32[384,128]{1,0:T(8,128)} %get-tuple-element.45.begun), custom_call_target="tpu_custom_call", output_to_operand_aliasing={{0}: (2, {})} | custom-call | tf_op jit(solution)/shard_map/home/pallas_call | solution.py:501
Async XLA Ops:
  1.6 13.4 %collective-permute-start.3 = (f32[200,128]{1,0:T(8,128)S(1)}, f32[200,128]{1,0:T(8,128)S(1)}, u32[]{:S(2)}, u32[]{:S(2)}) collective-permute-start(f32[200,128]{1,0:T(8,128)S(1)} %get-tuple-element.37), channel_id=1, source_target_pairs={{4,8},{12,16},{20,24},{28,32},{36,40},{44,48},{52,56},{60,64},{68,... | collective-permute-start | bytes 307208 | tf_op jit(solution)/shard_map/ppermute | solution.py:431
  4.6 9.8 %collective-permute-start = (f32[192,128]{1,0:T(8,128)S(1)}, f32[192,128]{1,0:T(8,128)S(1)}, u32[]{:S(2)}, u32[]{:S(2)}) collective-permute-start(f32[192,128]{1,0:T(8,128)S(1)} %get-tuple-element.31), channel_id=1, source_target_pairs={{0,4},{8,12},{16,20},{24,28},{32,36},{40,44},{48,52},{56,60},{64,6... | collective-permute-start | bytes 294920 | tf_op jit(solution)/shard_map/ppermute | solution.py:447
  9.4 4.7 %collective-permute-start.1 = (f32[8,128]{1,0:T(8,128)S(1)}, f32[8,128]{1,0:T(8,128)S(1)}, u32[]{:S(2)}, u32[]{:S(2)}) collective-permute-start(f32[8,128]{1,0:T(8,128)S(1)} %get-tuple-element.32), channel_id=1, source_target_pairs={{1,2},{3,0},{2,1},{0,3},{5,6},{7,4},{6,5},{4,7},{9,10},{11,8},{10,... | collective-permute-start | bytes 12296 | tf_op jit(solution)/shard_map/ppermute | solution.py:446
  11.9 2.5 %collective-permute-start.2 = (f32[8,128]{1,0:T(8,128)S(1)}, f32[8,128]{1,0:T(8,128)S(1)}, u32[]{:S(2)}, u32[]{:S(2)}) collective-permute-start(f32[8,128]{1,0:T(8,128)S(1)} %get-tuple-element.33), channel_id=1, source_target_pairs={{0,1},{2,3},{1,0},{3,2},{4,5},{6,7},{5,4},{7,6},{8,9},{10,11},{9,8... | collective-permute-start | bytes 12296 | tf_op jit(solution)/shard_map/ppermute | solution.py:445

commit v13 on v12

--- a/solution.py
+++ b/solution.py
@@ -49,11 +49,14 @@
     gcm_hbm, owner_hbm, branch_hbm, diffusion_hbm,
     gcm, to_neighbour, owner, branch, diffusion, arrival,
 ):
+    step = GCM_ROWS // FIELDS
+    pairs = [
+        (gcm_hbm.at[pl.ds(f * step, step)], gcm.at[pl.ds(f * step, step)]) for f in range(FIELDS)
+    ]
+    pairs += [(owner_hbm, owner), (branch_hbm, branch), (diffusion_hbm, diffusion)]
     loads = [
         pltpu.make_async_copy(source, target, arrival.at[n])
-        for n, (source, target) in enumerate(
-            [(gcm_hbm, gcm), (owner_hbm, owner), (branch_hbm, branch), (diffusion_hbm, diffusion)]
-        )
+        for n, (source, target) in enumerate(pairs)
     ]
     for copy in loads:
         copy.start()
@@ -424,7 +427,7 @@
             jax.ShapeDtypeStruct(branch.shape, branch.dtype),
             f32(*diffusion.shape),
         ),
-        scratch_shapes=[pltpu.SemaphoreType.DMA((4,))],
+        scratch_shapes=[pltpu.SemaphoreType.DMA((FIELDS + 3,))],
         compiler_params=pltpu.CompilerParams(vmem_limit_bytes=4 * MIB),
         name="load",
     )(*map(in_hbm, (gcm, owner, branch, diffusion)))

time: 53.2 us -> 53.2 us (level)
  no operation moved by 1% of the time
where the time goes in v13:
time: 53.2 us; the launch traced here: 53 us
  blocking collectives  29.2 us (55%)
  Pallas kernels  12.7 us (24%)
  starting transfers between devices  10.1 us (19%)
  between operations  0.69 us (1%)
    all_to_all x2, blocking collectives, transfer(): lax.all_to_all(rows.reshape(DEVICES, 2, LANES), ('blk', 'sub'), split_axi...  29.2 us
    pallas_call x1, Pallas kernels, body(): pl.pallas_call(cloud_kernel, out_specs=(whole((COLS, LANES)), hbm), out_s...  7.54 us
    ppermute x1, starting transfers between devices, body(): core_mate = lax.ppermute(to_core_mate, 'blk', pairs(n_blk, 0))  4.83 us
    ppermute x1, starting transfers between devices, body(): neighbour = lax.ppermute(to_neighbour, 'blk', pairs(n_blk, 1))  2.77 us
    ppermute x1, starting transfers between devices, body(): other = lax.ppermute(to_other, 'sub', pairs(n_sub, 1))  2.49 us
    pallas_call x1, Pallas kernels, body(): pl.pallas_call(early_kernel, in_specs=[hbm, whole((GCM_ROWS, LANES)), who...  2.16 us
  transfers between devices with their start and end apart: 4, of which 1 were waited for; matrix products, arithmetic and copies ran while one was open for 0% of the time, Pallas kernels for 6%

profile of v13, /device:TPU:1, one launch (start us, length us, event | category | flops | bytes accessed | tf_op | source)
XLA Modules:
  0.0 53.0 jit_solution(14090311710369520165)
XLA Ops:
  0.6 0.9 %load.1 = (f32[384,128]{1,0:T(8,128)S(1)}, f32[200,128]{1,0:T(8,128)S(1)}, s32[2,128]{1,0:T(2,128)S(1)}, s32[2,128]{1,0:T(2,128)S(1)}, f32[6,32]{1,0:T(8,128)S(1)}) custom-call(f32[384,128]{1,0:T(8,128)} %bitcast.12, s32[2,128]{1,0:T(2,128)} %owner_hbm.1, s32[2,128]{1,0:T(2,128)} %branch_hbm.1, f32[6,32]{1,0:T(8,128)} %diffusion_hbm.1), custom_call_target="tpu_custom_call" | custom-call | tf_op jit(solution)/shard_map/load/pallas_call | solution.py:420
  1.6 2.8 %collective-permute-start.3 = (f32[200,128]{1,0:T(8,128)S(1)}, f32[200,128]{1,0:T(8,128)S(1)}, u32[]{:S(2)}, u32[]{:S(2)}) collective-permute-start(f32[200,128]{1,0:T(8,128)S(1)} %get-tuple-element.37), channel_id=1, source_target_pairs={{4,8},{12,16},{20,24},{28,32},{36,40},{44,48},{52,56},{60,64},{68,... | collective-permute-start | bytes 307208 | tf_op jit(solution)/shard_map/ppermute | solution.py:434
  4.3 0.2 edges.1
  4.6 4.8 %collective-permute-start = (f32[192,128]{1,0:T(8,128)S(1)}, f32[192,128]{1,0:T(8,128)S(1)}, u32[]{:S(2)}, u32[]{:S(2)}) collective-permute-start(f32[192,128]{1,0:T(8,128)S(1)} %get-tuple-element.31), channel_id=1, source_target_pairs={{0,4},{8,12},{16,20},{24,28},{32,36},{40,44},{48,52},{56,60},{64,6... | collective-permute-start | bytes 294920 | tf_op jit(solution)/shard_map/ppermute | solution.py:450
  9.4 2.5 %collective-permute-start.1 = (f32[8,128]{1,0:T(8,128)S(1)}, f32[8,128]{1,0:T(8,128)S(1)}, u32[]{:S(2)}, u32[]{:S(2)}) collective-permute-start(f32[8,128]{1,0:T(8,128)S(1)} %get-tuple-element.32), channel_id=1, source_target_pairs={{1,2},{3,0},{2,1},{0,3},{5,6},{7,4},{6,5},{4,7},{9,10},{11,8},{10,... | collective-permute-start | bytes 12296 | tf_op jit(solution)/shard_map/ppermute | solution.py:449
  11.9 0.0 collective-permute-start.2
  11.9 2.2 %early.1 = (f32[2,2,2048,128]{3,2,1,0:T(8,128)S(1)}, f32[2,2,32,128]{3,2,1,0:T(8,128)S(1)}, f32[2,192,128]{2,1,0:T(8,128)S(1)}) custom-call(bf16[2,32,64,256]{3,2,1,0:T(8,128)(2,1)} %crm_hbm.1, f32[384,128]{1,0:T(8,128)S(1)} %get-tuple-element.25.gcm, f32[192,128]{1,0:T(8,128)S(1)} %get-tuple-element.29.number), custom_call_target="tpu_custom_call" | custom-call | flops 4194304 | bytes 6291456 | tf_op jit(solution)/shard_map/early/pallas_call | solution.py:452
  14.1 0.0 collective-permute-done.1.other
  14.1 0.3 collective-permute-done.2.chip_mate
  14.4 0.0 collective-permute-done.core_mate
  14.4 0.6 %inner.1 = (f32[192,128]{1,0:T(8,128)S(1)}, f32[2,128,128]{2,1,0:T(8,128)S(1)}, f32[128,128]{1,0:T(8,128)S(1)}) custom-call(f32[2,192,128]{2,1,0:T(8,128)S(1)} %get-tuple-element.30.partial, f32[192,128]{1,0:T(8,128)S(1)} %get-tuple-element.29.number, f32[192,128]{1,0:T(8,128)S(1)} %collective-permute-done.core_mate, ...), custom_call_target="tpu_custom_call" | custom-call | tf_op jit(solution)/shard_map/inner/pallas_call | solution.py:469
  15.0 0.0 collective-permute-done.3.neighbour
  15.0 0.3 outer.1
  15.3 15.2 %all_to_all.10 = f32[128,2,128]{2,1,0:T(2,128)S(1)} all-to-all(f32[128,2,128]{2,1,0:T(2,128)S(1)} %bitcast.9), channel_id=1, replica_groups=mesh['blk'=32,'sub'=4] {'blk','sub'}, dimensions={0} | all-to-all | bytes 262144 | tf_op jit(solution)/shard_map/all_to_all | solution.py:405
  30.4 7.5 %cloud.1 = (f32[256,128]{1,0:T(8,128)S(1)}, f32[384,128]{1,0:T(8,128)}) custom-call(f32[256,128]{1,0:T(8,128)S(1)} %bitcast.7, f32[2,2,2048,128]{3,2,1,0:T(8,128)S(1)} %get-tuple-element.41.start, f32[2,2,32,128]{3,2,1,0:T(8,128)S(1)} %get-tuple-element.42.means, f32[256,128]{1,0:T(8,128)S(1)} %get-tuple-element.43.advanced), custom_call_target="tpu_custom_call" | custom-call | tf_op jit(solution)/shard_map/cloud/pallas_call | solution.py:487
  38.0 14.0 %all_to_all.11 = f32[128,2,128]{2,1,0:T(2,128)S(1)} all-to-all(f32[128,2,128]{2,1,0:T(2,128)S(1)} %bitcast.10), channel_id=1, replica_groups=mesh['blk'=32,'sub'=4] {'blk','sub'}, dimensions={0} | all-to-all | bytes 262144 | tf_op jit(solution)/shard_map/all_to_all | solution.py:405
  52.0 0.9 %home.1 = (f32[384,128]{1,0:T(8,128)}, f32[128,128]{1,0:T(8,128)}) custom-call(f32[256,128]{1,0:T(8,128)S(1)} %bitcast.8, bf16[2,128,256]{2,1,0:T(8,128)(2,1)S(1)} %get-tuple-element.34.routes, f32[384,128]{1,0:T(8,128)} %get-tuple-element.45.begun), custom_call_target="tpu_custom_call", output_to_operand_aliasing={{0}: (2, {})} | custom-call | tf_op jit(solution)/shard_map/home/pallas_call | solution.py:504
Async XLA Ops:
  1.6 13.4 %collective-permute-start.3 = (f32[200,128]{1,0:T(8,128)S(1)}, f32[200,128]{1,0:T(8,128)S(1)}, u32[]{:S(2)}, u32[]{:S(2)}) collective-permute-start(f32[200,128]{1,0:T(8,128)S(1)} %get-tuple-element.37), channel_id=1, source_target_pairs={{4,8},{12,16},{20,24},{28,32},{36,40},{44,48},{52,56},{60,64},{68,... | collective-permute-start | bytes 307208 | tf_op jit(solution)/shard_map/ppermute | solution.py:434
  4.6 9.8 %collective-permute-start = (f32[192,128]{1,0:T(8,128)S(1)}, f32[192,128]{1,0:T(8,128)S(1)}, u32[]{:S(2)}, u32[]{:S(2)}) collective-permute-start(f32[192,128]{1,0:T(8,128)S(1)} %get-tuple-element.31), channel_id=1, source_target_pairs={{0,4},{8,12},{16,20},{24,28},{32,36},{40,44},{48,52},{56,60},{64,6... | collective-permute-start | bytes 294920 | tf_op jit(solution)/shard_map/ppermute | solution.py:450
  9.4 4.7 %collective-permute-start.1 = (f32[8,128]{1,0:T(8,128)S(1)}, f32[8,128]{1,0:T(8,128)S(1)}, u32[]{:S(2)}, u32[]{:S(2)}) collective-permute-start(f32[8,128]{1,0:T(8,128)S(1)} %get-tuple-element.32), channel_id=1, source_target_pairs={{1,2},{3,0},{2,1},{0,3},{5,6},{7,4},{6,5},{4,7},{9,10},{11,8},{10,... | collective-permute-start | bytes 12296 | tf_op jit(solution)/shard_map/ppermute | solution.py:449
  11.9 2.5 %collective-permute-start.2 = (f32[8,128]{1,0:T(8,128)S(1)}, f32[8,128]{1,0:T(8,128)S(1)}, u32[]{:S(2)}, u32[]{:S(2)}) collective-permute-start(f32[8,128]{1,0:T(8,128)S(1)} %get-tuple-element.33), channel_id=1, source_target_pairs={{0,1},{2,3},{1,0},{3,2},{4,5},{6,7},{5,4},{7,6},{8,9},{10,11},{9,8... | collective-permute-start | bytes 12296 | tf_op jit(solution)/shard_map/ppermute | solution.py:448

commit v14 on v11

--- a/solution.py
+++ b/solution.py
@@ -49,11 +49,14 @@
     gcm_hbm, owner_hbm, branch_hbm, diffusion_hbm,
     gcm, to_core_mate, to_neighbour, owner, branch, diffusion, arrival,
 ):
+    step = GCM_ROWS // FIELDS
+    pairs = [
+        (gcm_hbm.at[pl.ds(f * step, step)], gcm.at[pl.ds(f * step, step)]) for f in range(FIELDS)
+    ]
+    pairs += [(owner_hbm, owner), (branch_hbm, branch), (diffusion_hbm, diffusion)]
     loads = [
         pltpu.make_async_copy(source, target, arrival.at[n])
-        for n, (source, target) in enumerate(
-            [(gcm_hbm, gcm), (owner_hbm, owner), (branch_hbm, branch), (diffusion_hbm, diffusion)]
-        )
+        for n, (source, target) in enumerate(pairs)
     ]
     for copy in loads:
         copy.start()
@@ -423,7 +426,7 @@
             jax.ShapeDtypeStruct(branch.shape, branch.dtype),
             f32(*diffusion.shape),
         ),
-        scratch_shapes=[pltpu.SemaphoreType.DMA((4,))],
+        scratch_shapes=[pltpu.SemaphoreType.DMA((FIELDS + 3,))],
         compiler_params=pltpu.CompilerParams(vmem_limit_bytes=4 * MIB),
         name="load",
     )(*map(in_hbm, (gcm, owner, branch, diffusion)))

time: 53.2 us -> 53.2 us (level)
  no operation moved by 1% of the time
where the time goes in v14:
time: 53.2 us; the launch traced here: 53 us
  blocking collectives  29.2 us (55%)
  Pallas kernels  12.7 us (24%)
  starting transfers between devices  10.1 us (19%)
  between operations  0.7 us (1%)
    all_to_all x2, blocking collectives, transfer(): lax.all_to_all(rows.reshape(DEVICES, 2, LANES), ('blk', 'sub'), split_axi...  29.2 us
    pallas_call x1, Pallas kernels, body(): pl.pallas_call(cloud_kernel, out_specs=(whole((COLS, LANES)), hbm), out_s...  7.54 us
    ppermute x1, starting transfers between devices, body(): core_mate = lax.ppermute(to_core_mate, 'blk', pairs(n_blk, 0))  4.75 us
    ppermute x1, starting transfers between devices, body(): neighbour = lax.ppermute(to_neighbour, 'blk', pairs(n_blk, 1))  2.77 us
    ppermute x1, starting transfers between devices, body(): other = lax.ppermute(to_other, 'sub', pairs(n_sub, 1))  2.56 us
    pallas_call x1, Pallas kernels, body(): pl.pallas_call(early_kernel, in_specs=[hbm, whole((GCM_ROWS, LANES)), who...  2.16 us
  transfers between devices with their start and end apart: 4, of which 1 were waited for; matrix products, arithmetic and copies ran while one was open for 0% of the time, Pallas kernels for 6%

profile of v14, /device:TPU:1, one launch (start us, length us, event | category | flops | bytes accessed | tf_op | source)
XLA Modules:
  0.0 53.0 jit_solution(16981053113676163034)
XLA Ops:
  0.6 0.9 %load.1 = (f32[384,128]{1,0:T(8,128)S(1)}, f32[192,128]{1,0:T(8,128)S(1)}, f32[200,128]{1,0:T(8,128)S(1)}, s32[2,128]{1,0:T(2,128)S(1)}, s32[2,128]{1,0:T(2,128)S(1)}, /*index=5*/f32[6,32]{1,0:T(8,128)S(1)}) custom-call(f32[384,128]{1,0:T(8,128)} %bitcast.12, s32[2,128]{1,0:T(2,128)} %owner_hbm.1, s32[2,128]{1,0:T(2,128)} %branch_hbm.1, f32[6,32]{1,0:T(8,128)} %diffusion_hbm.1), custom_call_target="tpu_custom_call" | custom-call | tf_op jit(solution)/shard_map/load/pallas_call | solution.py:418
  1.6 2.8 %collective-permute-start.3 = (f32[200,128]{1,0:T(8,128)S(1)}, f32[200,128]{1,0:T(8,128)S(1)}, u32[]{:S(2)}, u32[]{:S(2)}) collective-permute-start(f32[200,128]{1,0:T(8,128)S(1)} %get-tuple-element.37), channel_id=1, source_target_pairs={{4,8},{12,16},{20,24},{28,32},{36,40},{44,48},{52,56},{60,64},{68,... | collective-permute-start | bytes 307208 | tf_op jit(solution)/shard_map/ppermute | solution.py:433
  4.4 4.7 %collective-permute-start = (f32[192,128]{1,0:T(8,128)S(1)}, f32[192,128]{1,0:T(8,128)S(1)}, u32[]{:S(2)}, u32[]{:S(2)}) collective-permute-start(f32[192,128]{1,0:T(8,128)S(1)} %get-tuple-element.31), channel_id=1, source_target_pairs={{0,4},{8,12},{16,20},{24,28},{32,36},{40,44},{48,52},{56,60},{64,6... | collective-permute-start | bytes 294920 | tf_op jit(solution)/shard_map/ppermute | solution.py:434
  9.1 0.2 edges.1
  9.3 2.6 %collective-permute-start.1 = (f32[8,128]{1,0:T(8,128)S(1)}, f32[8,128]{1,0:T(8,128)S(1)}, u32[]{:S(2)}, u32[]{:S(2)}) collective-permute-start(f32[8,128]{1,0:T(8,128)S(1)} %get-tuple-element.32), channel_id=1, source_target_pairs={{1,2},{3,0},{2,1},{0,3},{5,6},{7,4},{6,5},{4,7},{9,10},{11,8},{10,... | collective-permute-start | bytes 12296 | tf_op jit(solution)/shard_map/ppermute | solution.py:448
  11.9 0.0 collective-permute-start.2
  11.9 2.2 %early.1 = (f32[2,2,2048,128]{3,2,1,0:T(8,128)S(1)}, f32[2,2,32,128]{3,2,1,0:T(8,128)S(1)}, f32[2,192,128]{2,1,0:T(8,128)S(1)}) custom-call(bf16[2,32,64,256]{3,2,1,0:T(8,128)(2,1)} %crm_hbm.1, f32[384,128]{1,0:T(8,128)S(1)} %get-tuple-element.25.gcm, f32[192,128]{1,0:T(8,128)S(1)} %get-tuple-element.29.number), custom_call_target="tpu_custom_call" | custom-call | flops 4194304 | bytes 6291456 | tf_op jit(solution)/shard_map/early/pallas_call | solution.py:450
  14.1 0.0 collective-permute-done.1.other
  14.1 0.3 collective-permute-done.2.chip_mate
  14.3 0.0 collective-permute-done.core_mate
  14.4 0.6 %inner.1 = (f32[192,128]{1,0:T(8,128)S(1)}, f32[2,128,128]{2,1,0:T(8,128)S(1)}, f32[128,128]{1,0:T(8,128)S(1)}) custom-call(f32[2,192,128]{2,1,0:T(8,128)S(1)} %get-tuple-element.30.partial, f32[192,128]{1,0:T(8,128)S(1)} %get-tuple-element.29.number, f32[192,128]{1,0:T(8,128)S(1)} %collective-permute-done.core_mate, ...), custom_call_target="tpu_custom_call" | custom-call | tf_op jit(solution)/shard_map/inner/pallas_call | solution.py:467
  15.0 0.0 collective-permute-done.3.neighbour
  15.0 0.3 outer.1
  15.3 15.2 %all_to_all.10 = f32[128,2,128]{2,1,0:T(2,128)S(1)} all-to-all(f32[128,2,128]{2,1,0:T(2,128)S(1)} %bitcast.9), channel_id=1, replica_groups=mesh['blk'=32,'sub'=4] {'blk','sub'}, dimensions={0} | all-to-all | bytes 262144 | tf_op jit(solution)/shard_map/all_to_all | solution.py:403
  30.4 7.5 %cloud.1 = (f32[256,128]{1,0:T(8,128)S(1)}, f32[384,128]{1,0:T(8,128)}) custom-call(f32[256,128]{1,0:T(8,128)S(1)} %bitcast.7, f32[2,2,2048,128]{3,2,1,0:T(8,128)S(1)} %get-tuple-element.41.start, f32[2,2,32,128]{3,2,1,0:T(8,128)S(1)} %get-tuple-element.42.means, f32[256,128]{1,0:T(8,128)S(1)} %get-tuple-element.43.advanced), custom_call_target="tpu_custom_call" | custom-call | tf_op jit(solution)/shard_map/cloud/pallas_call | solution.py:485
  38.0 14.0 %all_to_all.11 = f32[128,2,128]{2,1,0:T(2,128)S(1)} all-to-all(f32[128,2,128]{2,1,0:T(2,128)S(1)} %bitcast.10), channel_id=1, replica_groups=mesh['blk'=32,'sub'=4] {'blk','sub'}, dimensions={0} | all-to-all | bytes 262144 | tf_op jit(solution)/shard_map/all_to_all | solution.py:403
  52.0 0.9 %home.1 = (f32[384,128]{1,0:T(8,128)}, f32[128,128]{1,0:T(8,128)}) custom-call(f32[256,128]{1,0:T(8,128)S(1)} %bitcast.8, bf16[2,128,256]{2,1,0:T(8,128)(2,1)S(1)} %get-tuple-element.34.routes, f32[384,128]{1,0:T(8,128)} %get-tuple-element.45.begun), custom_call_target="tpu_custom_call", output_to_operand_aliasing={{0}: (2, {})} | custom-call | tf_op jit(solution)/shard_map/home/pallas_call | solution.py:502
Async XLA Ops:
  1.6 13.4 %collective-permute-start.3 = (f32[200,128]{1,0:T(8,128)S(1)}, f32[200,128]{1,0:T(8,128)S(1)}, u32[]{:S(2)}, u32[]{:S(2)}) collective-permute-start(f32[200,128]{1,0:T(8,128)S(1)} %get-tuple-element.37), channel_id=1, source_target_pairs={{4,8},{12,16},{20,24},{28,32},{36,40},{44,48},{52,56},{60,64},{68,... | collective-permute-start | bytes 307208 | tf_op jit(solution)/shard_map/ppermute | solution.py:433
  4.4 10.0 %collective-permute-start = (f32[192,128]{1,0:T(8,128)S(1)}, f32[192,128]{1,0:T(8,128)S(1)}, u32[]{:S(2)}, u32[]{:S(2)}) collective-permute-start(f32[192,128]{1,0:T(8,128)S(1)} %get-tuple-element.31), channel_id=1, source_target_pairs={{0,4},{8,12},{16,20},{24,28},{32,36},{40,44},{48,52},{56,60},{64,6... | collective-permute-start | bytes 294920 | tf_op jit(solution)/shard_map/ppermute | solution.py:434
  9.3 4.7 %collective-permute-start.1 = (f32[8,128]{1,0:T(8,128)S(1)}, f32[8,128]{1,0:T(8,128)S(1)}, u32[]{:S(2)}, u32[]{:S(2)}) collective-permute-start(f32[8,128]{1,0:T(8,128)S(1)} %get-tuple-element.32), channel_id=1, source_target_pairs={{1,2},{3,0},{2,1},{0,3},{5,6},{7,4},{6,5},{4,7},{9,10},{11,8},{10,... | collective-permute-start | bytes 12296 | tf_op jit(solution)/shard_map/ppermute | solution.py:448
  11.9 2.5 %collective-permute-start.2 = (f32[8,128]{1,0:T(8,128)S(1)}, f32[8,128]{1,0:T(8,128)S(1)}, u32[]{:S(2)}, u32[]{:S(2)}) collective-permute-start(f32[8,128]{1,0:T(8,128)S(1)} %get-tuple-element.33), channel_id=1, source_target_pairs={{0,1},{2,3},{1,0},{3,2},{4,5},{6,7},{5,4},{7,6},{8,9},{10,11},{9,8... | collective-permute-start | bytes 12296 | tf_op jit(solution)/shard_map/ppermute | solution.py:447

commit v15 on v11

--- a/solution.py
+++ b/solution.py
@@ -26,10 +26,7 @@
 
 def pieces(x):
     first = x.astype(jnp.bfloat16)
-    rest = x - first.astype(jnp.float32)
-    second = rest.astype(jnp.bfloat16)
-    third = (rest - second.astype(jnp.float32)).astype(jnp.bfloat16)
-    return first, second, third
+    return first, (x - first.astype(jnp.float32)).astype(jnp.bfloat16)
 
 
 def select_dot(x, chosen, dims, x_first):

time: 53.2 us -> 53 us (level)
  transfers between devices with their start and end apart: 4 -> 4, of which waited for: 1 -> 1; matrix products, arithmetic and copies ran while one was open for 0% -> 0% of each run, Pallas kernels for 6% -> 5%
where the time goes in v15:
time: 53 us; the launch traced here: 52.8 us
  blocking collectives  29.2 us (55%)
  Pallas kernels  12.5 us (24%)
  starting transfers between devices  10.1 us (19%)
  between operations  0.7 us (1%)
    all_to_all x2, blocking collectives, transfer(): lax.all_to_all(rows.reshape(DEVICES, 2, LANES), ('blk', 'sub'), split_axi...  29.2 us
    pallas_call x1, Pallas kernels, body(): pl.pallas_call(cloud_kernel, out_specs=(whole((COLS, LANES)), hbm), out_s...  7.54 us
    ppermute x1, starting transfers between devices, body(): core_mate = lax.ppermute(to_core_mate, 'blk', pairs(n_blk, 0))  4.75 us
    ppermute x1, starting transfers between devices, body(): neighbour = lax.ppermute(to_neighbour, 'blk', pairs(n_blk, 1))  2.77 us
    ppermute x1, starting transfers between devices, body(): other = lax.ppermute(to_other, 'sub', pairs(n_sub, 1))  2.56 us
    pallas_call x1, Pallas kernels, body(): pl.pallas_call(early_kernel, in_specs=[hbm, whole((GCM_ROWS, LANES)), who...  2.16 us
  transfers between devices with their start and end apart: 4, of which 1 were waited for; matrix products, arithmetic and copies ran while one was open for 0% of the time, Pallas kernels for 5%

profile of v15, /device:TPU:1, one launch (start us, length us, event | category | flops | bytes accessed | tf_op | source)
XLA Modules:
  0.0 52.8 jit_solution(12039456998091684841)
XLA Ops:
  0.6 1.0 %load.1 = (f32[384,128]{1,0:T(8,128)S(1)}, f32[192,128]{1,0:T(8,128)S(1)}, f32[200,128]{1,0:T(8,128)S(1)}, s32[2,128]{1,0:T(2,128)S(1)}, s32[2,128]{1,0:T(2,128)S(1)}, /*index=5*/f32[6,32]{1,0:T(8,128)S(1)}) custom-call(f32[384,128]{1,0:T(8,128)} %bitcast.12, s32[2,128]{1,0:T(2,128)} %owner_hbm.1, s32[2,128]{1,0:T(2,128)} %branch_hbm.1, f32[6,32]{1,0:T(8,128)} %diffusion_hbm.1), custom_call_target="tpu_custom_call" | custom-call | tf_op jit(solution)/shard_map/load/pallas_call | solution.py:412
  1.6 2.8 %collective-permute-start.3 = (f32[200,128]{1,0:T(8,128)S(1)}, f32[200,128]{1,0:T(8,128)S(1)}, u32[]{:S(2)}, u32[]{:S(2)}) collective-permute-start(f32[200,128]{1,0:T(8,128)S(1)} %get-tuple-element.37), channel_id=1, source_target_pairs={{4,8},{12,16},{20,24},{28,32},{36,40},{44,48},{52,56},{60,64},{68,... | collective-permute-start | bytes 307208 | tf_op jit(solution)/shard_map/ppermute | solution.py:427
  4.4 4.7 %collective-permute-start = (f32[192,128]{1,0:T(8,128)S(1)}, f32[192,128]{1,0:T(8,128)S(1)}, u32[]{:S(2)}, u32[]{:S(2)}) collective-permute-start(f32[192,128]{1,0:T(8,128)S(1)} %get-tuple-element.31), channel_id=1, source_target_pairs={{0,4},{8,12},{16,20},{24,28},{32,36},{40,44},{48,52},{56,60},{64,6... | collective-permute-start | bytes 294920 | tf_op jit(solution)/shard_map/ppermute | solution.py:428
  9.1 0.2 edges.1
  9.4 2.6 %collective-permute-start.1 = (f32[8,128]{1,0:T(8,128)S(1)}, f32[8,128]{1,0:T(8,128)S(1)}, u32[]{:S(2)}, u32[]{:S(2)}) collective-permute-start(f32[8,128]{1,0:T(8,128)S(1)} %get-tuple-element.32), channel_id=1, source_target_pairs={{1,2},{3,0},{2,1},{0,3},{5,6},{7,4},{6,5},{4,7},{9,10},{11,8},{10,... | collective-permute-start | bytes 12296 | tf_op jit(solution)/shard_map/ppermute | solution.py:442
  11.9 0.0 collective-permute-start.2
  11.9 2.2 %early.1 = (f32[2,2,2048,128]{3,2,1,0:T(8,128)S(1)}, f32[2,2,32,128]{3,2,1,0:T(8,128)S(1)}, f32[2,192,128]{2,1,0:T(8,128)S(1)}) custom-call(bf16[2,32,64,256]{3,2,1,0:T(8,128)(2,1)} %crm_hbm.1, f32[384,128]{1,0:T(8,128)S(1)} %get-tuple-element.25.gcm, f32[192,128]{1,0:T(8,128)S(1)} %get-tuple-element.29.number), custom_call_target="tpu_custom_call" | custom-call | flops 4194304 | bytes 6291456 | tf_op jit(solution)/shard_map/early/pallas_call | solution.py:444
  14.1 0.0 collective-permute-done.1.other
  14.1 0.3 collective-permute-done.2.chip_mate
  14.4 0.0 collective-permute-done.core_mate
  14.4 0.5 inner.1
  14.9 0.0 collective-permute-done.3.neighbour
  14.9 0.2 outer.1
  15.2 15.2 %all_to_all.10 = f32[128,2,128]{2,1,0:T(2,128)S(1)} all-to-all(f32[128,2,128]{2,1,0:T(2,128)S(1)} %bitcast.9), channel_id=1, replica_groups=mesh['blk'=32,'sub'=4] {'blk','sub'}, dimensions={0} | all-to-all | bytes 262144 | tf_op jit(solution)/shard_map/all_to_all | solution.py:397
  30.3 7.5 %cloud.1 = (f32[256,128]{1,0:T(8,128)S(1)}, f32[384,128]{1,0:T(8,128)}) custom-call(f32[256,128]{1,0:T(8,128)S(1)} %bitcast.7, f32[2,2,2048,128]{3,2,1,0:T(8,128)S(1)} %get-tuple-element.41.start, f32[2,2,32,128]{3,2,1,0:T(8,128)S(1)} %get-tuple-element.42.means, f32[256,128]{1,0:T(8,128)S(1)} %get-tuple-element.43.advanced), custom_call_target="tpu_custom_call" | custom-call | tf_op jit(solution)/shard_map/cloud/pallas_call | solution.py:479
  37.9 14.0 %all_to_all.11 = f32[128,2,128]{2,1,0:T(2,128)S(1)} all-to-all(f32[128,2,128]{2,1,0:T(2,128)S(1)} %bitcast.10), channel_id=1, replica_groups=mesh['blk'=32,'sub'=4] {'blk','sub'}, dimensions={0} | all-to-all | bytes 262144 | tf_op jit(solution)/shard_map/all_to_all | solution.py:397
  51.9 0.9 %home.1 = (f32[384,128]{1,0:T(8,128)}, f32[128,128]{1,0:T(8,128)}) custom-call(f32[256,128]{1,0:T(8,128)S(1)} %bitcast.8, bf16[2,128,256]{2,1,0:T(8,128)(2,1)S(1)} %get-tuple-element.34.routes, f32[384,128]{1,0:T(8,128)} %get-tuple-element.45.begun), custom_call_target="tpu_custom_call", output_to_operand_aliasing={{0}: (2, {})} | custom-call | tf_op jit(solution)/shard_map/home/pallas_call | solution.py:496
Async XLA Ops:
  1.6 13.3 %collective-permute-start.3 = (f32[200,128]{1,0:T(8,128)S(1)}, f32[200,128]{1,0:T(8,128)S(1)}, u32[]{:S(2)}, u32[]{:S(2)}) collective-permute-start(f32[200,128]{1,0:T(8,128)S(1)} %get-tuple-element.37), channel_id=1, source_target_pairs={{4,8},{12,16},{20,24},{28,32},{36,40},{44,48},{52,56},{60,64},{68,... | collective-permute-start | bytes 307208 | tf_op jit(solution)/shard_map/ppermute | solution.py:427
  4.4 10.0 %collective-permute-start = (f32[192,128]{1,0:T(8,128)S(1)}, f32[192,128]{1,0:T(8,128)S(1)}, u32[]{:S(2)}, u32[]{:S(2)}) collective-permute-start(f32[192,128]{1,0:T(8,128)S(1)} %get-tuple-element.31), channel_id=1, source_target_pairs={{0,4},{8,12},{16,20},{24,28},{32,36},{40,44},{48,52},{56,60},{64,6... | collective-permute-start | bytes 294920 | tf_op jit(solution)/shard_map/ppermute | solution.py:428
  9.4 4.7 %collective-permute-start.1 = (f32[8,128]{1,0:T(8,128)S(1)}, f32[8,128]{1,0:T(8,128)S(1)}, u32[]{:S(2)}, u32[]{:S(2)}) collective-permute-start(f32[8,128]{1,0:T(8,128)S(1)} %get-tuple-element.32), channel_id=1, source_target_pairs={{1,2},{3,0},{2,1},{0,3},{5,6},{7,4},{6,5},{4,7},{9,10},{11,8},{10,... | collective-permute-start | bytes 12296 | tf_op jit(solution)/shard_map/ppermute | solution.py:442
  11.9 2.5 %collective-permute-start.2 = (f32[8,128]{1,0:T(8,128)S(1)}, f32[8,128]{1,0:T(8,128)S(1)}, u32[]{:S(2)}, u32[]{:S(2)}) collective-permute-start(f32[8,128]{1,0:T(8,128)S(1)} %get-tuple-element.33), channel_id=1, source_target_pairs={{0,1},{2,3},{1,0},{3,2},{4,5},{6,7},{5,4},{7,6},{8,9},{10,11},{9,8... | collective-permute-start | bytes 12296 | tf_op jit(solution)/shard_map/ppermute | solution.py:441
